TPU v7x, 256 devices: a whole 4x4x8 slice. The times are simulated.
256 devices in a mesh: seq: 32 (over z, y_lo, core), comp: 8 (over x, y_hi).
Axes of the slice: x: 4, y: 4 (y_hi: 2, y_lo: 2; y = y_hi * 2 + y_lo), z: 8, core: 2. Of those that a mesh axis runs over, the one named last changes fastest.
Arguments:
- prompt_inputs: bfloat16 [16384, 128, 64], P('seq', 'comp'), may hold values from -1.25 to 1.25
- prompt_keys: bfloat16 [16384, 8, 128], P('seq', 'comp'), may hold values from -1.75 to 1.75
- prompt_queries: bfloat16 [16384, 8, 128], P('seq', 'comp'), may hold values from -1.75 to 1.75
- prompt_logdecay: float32 [16384, 128], P('seq', 'comp'), may hold values from -1 to 0, as said below
- prompt_cotangent: bfloat16 [16384, 128, 64], P('seq', 'comp'), may hold values from -0.125 to 0.125
- answer_inputs: bfloat16 [8, 1024, 128, 64], P('comp', None, 'seq'), may hold values from -1.25 to 1.25
- answer_keys: bfloat16 [8, 1024, 8, 128], P('comp'), may hold values from -1.75 to 1.75
- answer_queries: bfloat16 [8, 1024, 8, 128], P('comp'), may hold values from -1.75 to 1.75
- answer_logdecay: float32 [8, 1024, 128], P('comp', None, 'seq'), may hold values from -1 to 0, as said below
- answer_cotangent: bfloat16 [8, 1024, 128, 64], P('comp', None, 'seq'), may hold values from -0.125 to 0.125
- answer_lengths: int32 [8], P('comp'), may hold values from 256 to 1024, as said below
Outputs:
- prompt_inputgrad: bfloat16 [16384, 128, 64], P('seq', 'comp')
- prompt_keygrad: bfloat16 [16384, 8, 128], P('seq', 'comp')
- prompt_querygrad: bfloat16 [16384, 8, 128], P('seq', 'comp')
- answer_inputgrad: bfloat16 [8, 1024, 128, 64], P('comp', None, 'seq')
- answer_keygrad: bfloat16 [8, 1024, 8, 128], P('comp', 'seq')
- answer_querygrad: bfloat16 [8, 1024, 8, 128], P('comp', 'seq')
Inputs may be any that keep to these rules, and one draw needn't show every extreme that they name: `answer_lengths`: live tokens of each answer, counted from its start. `prompt_logdecay`: negative log decay factors. `answer_logdecay`: negative log decay factors.
All inputs are finite; a program needn't handle non-finite values.
Results may differ from a plain program's by a relative error of at most 0.0014.
Values sent between devices are 32-bit elements; how exact they have to be, the bound alone decides.
No kernel may reach another device: no remote copies, remote signals or barrier semaphores. Data moves between devices by JAX's collectives and lax.ppermute only.
A program may use at most 128 MiB of HBM per device.

v0:
```python
import jax
import jax.numpy as jnp
from jax import lax
from jax.sharding import PartitionSpec as P

HEAD_SUBSET = 128
GROUPS = 8
BLOCK = 256


PRECISE = lax.Precision.HIGHEST


def prefix(value, axis, join, neutral, backward):
    count, mine = (lax.axis_size(axis), lax.axis_index(axis))
    pieces = jax.tree.map(lambda part: lax.all_gather(part, axis), value)
    if backward:
        pieces = jax.tree.map(lambda part: part[::-1], pieces)
        mine = count - 1 - mine
    so_far = jax.tree.map(
        lambda part, zero: jnp.full_like(part, 0) + jnp.asarray(zero, part.dtype), value, neutral
    )

    def hop(position, so_far):
        longer = join(so_far, jax.tree.map(lambda part: part[position], pieces))
        return jax.tree.map(lambda new, old: jnp.where(position < mine, new, old), longer, so_far)

    return lax.fori_loop(0, count - 1, hop, so_far)


def from_root(shard, axis, root):
    mine = lax.axis_index(axis) == root
    return lax.psum(jnp.where(mine, shard, jnp.zeros_like(shard)), axis)


def lower_mask(length):
    row_ids = lax.broadcasted_iota(jnp.int32, (length, length), 0)
    col_ids = lax.broadcasted_iota(jnp.int32, (length, length), 1)
    return row_ids >= col_ids


def running_logs(logdecay):
    lower_ones = lower_mask(logdecay.shape[1]).astype(jnp.float32)
    return jnp.einsum("ts,msh->mth", lower_ones, logdecay, precision=PRECISE)


def summaries(inputs, key_rows, queries, cotangent, cumlog):
    per_group = inputs.shape[2] // key_rows.shape[2]
    totals = cumlog[:, -1]
    keys_head = jnp.repeat(key_rows, per_group, axis=2)
    queries_head = jnp.repeat(queries, per_group, axis=2)
    tail_decay = jnp.exp(totals[:, None, :] - cumlog)
    carried = jnp.einsum(
        "mshn,mshp->mhnp", tail_decay[..., None] * keys_head, inputs, precision=PRECISE
    )
    pulled = jnp.einsum(
        "mthn,mthp->mhnp", jnp.exp(cumlog)[..., None] * queries_head, cotangent, precision=PRECISE
    )
    return (totals, carried, pulled)


def chain_forward(totals, carried, start_state):
    current = start_state
    starts = []
    for number in range(totals.shape[1]):
        starts.append(current)
        current = jnp.exp(totals[:, number])[:, :, None, None] * current + carried[:, number]
    return (jnp.stack(starts, axis=1), current)


def chain_backward(totals, pulled, finish):
    current = finish
    block_ends = []
    for number in range(totals.shape[1] - 1, -1, -1):
        block_ends.insert(0, current)
        current = jnp.exp(totals[:, number])[:, :, None, None] * current + pulled[:, number]
    return (jnp.stack(block_ends, axis=1), current)


def block_grads(inputs, key_rows, queries, cotangent, cumlog, starts, block_ends):
    item_count, length, head_count, head_width = inputs.shape
    groups_here, state_size = (key_rows.shape[2], key_rows.shape[3])
    per_group = head_count // groups_here
    causal = lower_mask(length)[None, None]
    trail_logs = jnp.swapaxes(cumlog, 1, 2)
    log_gap = trail_logs[:, :, :, None] - trail_logs[:, :, None, :]
    weights = jnp.where(causal, jnp.exp(jnp.where(causal, log_gap, 0.0)), 0.0)
    scores = jnp.einsum("mtgn,msgn->mgts", queries, key_rows, precision=PRECISE)
    masked_scores = weights * jnp.repeat(scores, per_group, axis=1)
    masked_products = weights * jnp.einsum("mthp,mshp->mhts", cotangent, inputs, precision=PRECISE)
    input_grad = jnp.einsum("mhts,mthp->mshp", masked_scores, cotangent, precision=PRECISE)
    summed = masked_products.reshape(item_count, groups_here, per_group, length, length).sum(axis=2)
    key_grad = jnp.einsum("mgts,mtgn->msgn", summed, queries, precision=PRECISE)
    query_grad = jnp.einsum("mgts,msgn->mtgn", summed, key_rows, precision=PRECISE)
    totals = cumlog[:, -1]
    tail_decay = jnp.exp(totals[:, None, :] - cumlog)
    keys_head = jnp.repeat(key_rows, per_group, axis=2)
    input_grad = input_grad + tail_decay[..., None] * jnp.einsum(
        "mshn,mhnp->mshp", keys_head, block_ends, precision=PRECISE
    )
    key_part = tail_decay[..., None] * jnp.einsum(
        "mshp,mhnp->mshn", inputs, block_ends, precision=PRECISE
    )
    query_part = jnp.exp(cumlog)[..., None] * jnp.einsum(
        "mthp,mhnp->mthn", cotangent, starts, precision=PRECISE
    )
    key_grad = key_grad + key_part.reshape(
        item_count, length, groups_here, per_group, state_size
    ).sum(axis=3)
    query_grad = query_grad + query_part.reshape(
        item_count, length, groups_here, per_group, state_size
    ).sum(axis=3)
    return (input_grad, key_grad, query_grad)


def compose(earlier, later):
    return (earlier[0] + later[0], jnp.exp(later[0])[:, None, None] * earlier[1] + later[1])


def body(
    prompt_inputs,
    prompt_keys,
    prompt_queries,
    prompt_logdecay,
    prompt_cotangent,
    answer_inputs,
    answer_keys,
    answer_queries,
    answer_logdecay,
    answer_cotangent,
    answer_lengths,
):
    token_count, heads_here, head_width = prompt_inputs.shape
    groups_here, state_size = (prompt_keys.shape[1], prompt_keys.shape[2])
    blocks = token_count // BLOCK
    prompt_vals = prompt_inputs.reshape(blocks, BLOCK, heads_here, head_width).astype(jnp.float32)
    prompt_kvals = prompt_keys.reshape(blocks, BLOCK, groups_here, state_size).astype(jnp.float32)
    prompt_qvals = prompt_queries.reshape(blocks, BLOCK, groups_here, state_size).astype(
        jnp.float32
    )
    prompt_cvals = prompt_cotangent.reshape(blocks, BLOCK, heads_here, head_width).astype(
        jnp.float32
    )
    prompt_logs = running_logs(prompt_logdecay.reshape(blocks, BLOCK, heads_here))
    totals, carried, pulled = summaries(
        prompt_vals, prompt_kvals, prompt_qvals, prompt_cvals, prompt_logs
    )
    zero_state = jnp.zeros((1, heads_here, state_size, head_width), jnp.float32)
    ignored, device_carried = chain_forward(totals[None], carried[None], zero_state)
    ignored, device_pulled = chain_backward(totals[None], pulled[None], zero_state)
    device_carried = device_carried[0]
    device_pulled = device_pulled[0]
    device_total = jnp.sum(totals, axis=0)
    neutral = (jnp.zeros_like(device_total), jnp.zeros_like(device_carried))
    before_total, prompt_start = prefix(
        (device_total, device_carried), "seq", compose, neutral, False
    )
    seq_count = lax.axis_size("seq")
    inclusive = jnp.exp(device_total)[:, None, None] * prompt_start + device_carried
    final_state = from_root(inclusive, "seq", seq_count - 1)
    answers, length, answer_heads, answer_width = answer_inputs.shape
    first_head = lax.axis_index("seq") * answer_heads
    owner_index = first_head // heads_here
    own_piece = lax.dynamic_slice_in_dim(final_state, first_head % heads_here, answer_heads, 0)
    answer_start = from_root(own_piece, "comp", owner_index)
    answer_blocks = length // BLOCK
    flat_count = answers * answer_blocks
    group_index = first_head // (HEAD_SUBSET // GROUPS)
    own_keys = lax.dynamic_slice_in_dim(answer_keys, group_index, 1, 2)
    own_queries = lax.dynamic_slice_in_dim(answer_queries, group_index, 1, 2)
    answer_vals = answer_inputs.reshape(flat_count, BLOCK, answer_heads, answer_width).astype(
        jnp.float32
    )
    answer_kvals = own_keys.reshape(flat_count, BLOCK, 1, state_size).astype(jnp.float32)
    answer_qvals = own_queries.reshape(flat_count, BLOCK, 1, state_size).astype(jnp.float32)
    live_mask = (
        lax.broadcasted_iota(jnp.int32, (answers, length), 1) < answer_lengths[:, None]
    ).astype(jnp.float32)
    answer_cvals = (answer_cotangent.astype(jnp.float32) * live_mask[:, :, None, None]).reshape(
        flat_count, BLOCK, answer_heads, answer_width
    )
    answer_logs = running_logs(answer_logdecay.reshape(flat_count, BLOCK, answer_heads))
    answer_totals, answer_carried, answer_pulled = summaries(
        answer_vals, answer_kvals, answer_qvals, answer_cvals, answer_logs
    )
    batch_totals = answer_totals.reshape(answers, answer_blocks, answer_heads)
    batch_carried = answer_carried.reshape(
        answers, answer_blocks, answer_heads, state_size, answer_width
    )
    batch_pulled = answer_pulled.reshape(
        answers, answer_blocks, answer_heads, state_size, answer_width
    )
    answer_starts, ignored = chain_forward(batch_totals, batch_carried, answer_start[None])
    answer_ends, start_grad = chain_backward(
        batch_totals, batch_pulled, jnp.zeros_like(answer_starts[:, 0])
    )
    state_sum = lax.psum(jnp.sum(start_grad, axis=0), "comp")
    after_total, after_grad = prefix((device_total, device_pulled), "seq", compose, neutral, True)
    answer_igrad, answer_kgrad, answer_qgrad = block_grads(
        answer_vals,
        answer_kvals,
        answer_qvals,
        answer_cvals,
        answer_logs,
        answer_starts.reshape(flat_count, answer_heads, state_size, answer_width),
        answer_ends.reshape(flat_count, answer_heads, state_size, answer_width),
    )
    every_head = lax.all_gather(state_sum, "seq", axis=0, tiled=True)
    prompt_final_grad = lax.dynamic_slice_in_dim(
        every_head, lax.axis_index("comp") * heads_here, heads_here, 0
    )
    prompt_end = after_grad + jnp.exp(after_total)[:, None, None] * prompt_final_grad
    prompt_starts, ignored = chain_forward(totals[None], carried[None], prompt_start[None])
    prompt_ends, ignored = chain_backward(totals[None], pulled[None], prompt_end[None])
    prompt_igrad, prompt_kgrad, prompt_qgrad = block_grads(
        prompt_vals,
        prompt_kvals,
        prompt_qvals,
        prompt_cvals,
        prompt_logs,
        prompt_starts[0],
        prompt_ends[0],
    )
    own_kgrad = answer_kgrad.reshape(answers, length, state_size)
    own_qgrad = answer_qgrad.reshape(answers, length, state_size)
    slots = (lax.broadcasted_iota(jnp.int32, (1, 1, GROUPS, 1), 2) == group_index).astype(
        jnp.float32
    )
    full_kgrad = own_kgrad[:, :, None, :] * slots
    full_qgrad = own_qgrad[:, :, None, :] * slots
    key_out, query_out = (
        lax.psum_scatter(full_kgrad, "seq", scatter_dimension=1, tiled=True),
        lax.psum_scatter(full_qgrad, "seq", scatter_dimension=1, tiled=True),
    )
    return (
        prompt_igrad.reshape(token_count, heads_here, head_width).astype(jnp.bfloat16),
        prompt_kgrad.reshape(token_count, groups_here, state_size).astype(jnp.bfloat16),
        prompt_qgrad.reshape(token_count, groups_here, state_size).astype(jnp.bfloat16),
        answer_igrad.reshape(answers, length, answer_heads, answer_width).astype(jnp.bfloat16),
        key_out.astype(jnp.bfloat16),
        query_out.astype(jnp.bfloat16),
    )


def solution(mesh):
    in_specs = (
        P("seq", "comp", None),
        P("seq", "comp", None),
        P("seq", "comp", None),
        P("seq", "comp"),
        P("seq", "comp", None),
        P("comp", None, "seq", None),
        P("comp", None, None, None),
        P("comp", None, None, None),
        P("comp", None, "seq"),
        P("comp", None, "seq", None),
        P("comp"),
    )
    out_specs = (
        P("seq", "comp", None),
        P("seq", "comp", None),
        P("seq", "comp", None),
        P("comp", None, "seq", None),
        P("comp", "seq", None, None),
        P("comp", "seq", None, None),
    )
    return jax.shard_map(body, mesh=mesh, in_specs=in_specs, out_specs=out_specs, check_vma=False)
```

profile of v0, /device:TPU:16, one launch (start us, length us, event | category | flops | bytes accessed | tf_op | source)
XLA Modules:
  0.0 942.2 jit_solution(2773144251403820357)
XLA Ops:
  11.5 3.9 fusion.47
  19.4 60.4 %all-reduce = f32[512]{0:T(512)S(1)} all-reduce(f32[512]{0:T(512)S(1)} %dynamic-update-slice), channel_id=2, replica_groups=mesh['seq'=32,'comp'=8] {'seq'}, use_global_device_ids=true, to_apply=%add | all-reduce | flops 512 | bytes 4096
  82.7 1.2 convert_multiply_fusion
  83.9 1.5 reshape.448
  85.9 34.8 %all-gather.9.cloned.1.call-done = f32[32,16,128,64]{2,3,1,0:T(8,128)} async-done(((f32[1,16,128,64]{2,3,1,0:T(8,128)}), f32[32,16,128,64]{2,3,1,0:T(8,128)}) %all-gather.9.cloned.1.call-update) | async-done | bytes 16777232 | tf_op jit(solution)/shard_map/all_gather | solution.py:16
  120.7 74.2 %while.31 = (s32[]{:T(128)}, f32[16,128,64]{2,1,0:T(8,128)S(1)}, s32[]{:T(128)}, f32[32,16]{1,0:T(8,128)}, f32[32,16,128,64]{2,3,1,0:T(8,128)}, /*index=5*/s32[]{:T(128)}, s32[]{:T(128)}) while((s32[]{:T(128)}, f32[16,128,64]{2,1,0:T(8,128)S(1)}, s32[]{:T(128)}, f32[32,16]{1,0:T(8,128)}, f32[32,16,128,64]{2,3,1,0:T(8,128)}, ...), condition=%wide.region_7.8_spmd.clone, body=%wide.region_6.7_spmd.clone.sunk | while | flops 524292 | bytes 3670321 | solution.py:28
  127.9 1.1 constant_dynamic-slice_fusion.8
  195.4 2.6 fusion.99
  198.1 3.6 fusion.53
  202.6 219.8 %all-reduce.5.cloned.1.call-done = f32[16,128,64]{1,2,0:T(8,128)} async-done(((f32[16,128,64]{1,2,0:T(8,128)}), f32[16,128,64]{1,2,0:T(8,128)}) %all-reduce.5.cloned.1.call-update) | async-done | bytes 524304 | tf_op jit(solution)/shard_map/psum | solution.py:33
  422.4 1.6 dynamic-slice_select_fusion
  424.1 3.9 fusion.44
  430.0 82.5 %all-reduce.7.cloned.1.call-done = (f32[4,128,64]{1,2,0:T(8,128)}, f32[4,128,64]{1,2,0:T(8,128)}) async-done(((f32[4,128,64]{1,2,0:T(8,128)}, f32[4,128,64]{1,2,0:T(8,128)}), (f32[4,128,64]{1,2,0:T(8,128)}, f32[4,128,64]{1,2,0:T(8,128)})) %all-reduce.7.cloned.1.call-update) | async-done | bytes 262160 | tf_op jit(solution)/shard_map/psum | solution.py:197
  512.5 10.6 %reduce-scatter.3.cloned.1.call-start = ((), (), s32[]{:S(2)}) async-start(), calls=%async_computation.5 | async-start | bytes 4325376 | tf_op jit(solution)/shard_map/reduce_scatter | solution.py:232
  523.2 2.1 constant_dynamic-slice_fusion.3
  527.7 1.3 fusion.18
  529.0 4.3 multiply_reduce_fusion.1
  533.3 1.4 fusion.59
  534.7 1.2 copy.125
  536.5 2.6 fusion.56
  540.1 3.0 fusion.17
  544.0 4.6 broadcast_multiply_fusion
  548.7 1.4 rev.6
  550.5 4.7 fusion.41
  555.3 1.1 fusion.52
  556.8 1.2 convert_element_type.116
  559.0 5.4 multiply_reduce_fusion
  564.4 51.2 %all-gather.5.cloned.1.call-done = f32[32,16,128,64]{2,3,1,0:T(8,128)} async-done(((f32[1,16,128,64]{2,3,1,0:T(8,128)}), f32[32,16,128,64]{2,3,1,0:T(8,128)}) %all-gather.5.cloned.1.call-update) | async-done | bytes 16777232 | tf_op jit(solution)/shard_map/all_gather | solution.py:16
  615.7 11.8 %rev.7 = f32[32,16,128,64]{2,3,1,0:T(8,128)} reverse(f32[32,16,128,64]{2,3,1,0:T(8,128)} %all-gather.5.cloned.1.call-done), dimensions={0} | reverse | bytes 33554432 | tf_op jit(solution)/shard_map/rev | solution.py:18
  628.1 74.4 %while.30 = (s32[]{:T(128)}, f32[16]{0:T(128)S(1)}, f32[16,128,64]{2,1,0:T(8,128)S(1)}, s32[]{:T(128)}, f32[32,16]{1,0:T(8,128)}, /*index=5*/f32[32,16,128,64]{2,3,1,0:T(8,128)}, s32[]{:T(128)}, s32[]{:T(128)}) while((s32[]{:T(128)}, f32[16]{0:T(128)S(1)}, f32[16,128,64]{2,1,0:T(8,128)S(1)}, s32[]{:T(128)}, f32[32,16]{1,0:T(8,128)}, ...), condition=%wide.region_2.3_spmd.clone, body=%wide.region_1.2_spmd.clone.sunk | while | flops 524340 | bytes 3670459 | solution.py:28
  628.8 1.2 constant_dynamic-slice_fusion.7
  636.1 1.1 constant_dynamic-slice_fusion.7
  652.9 1.1 constant_dynamic-slice_fusion.7
  655.3 1.1 constant_dynamic-slice_fusion.7
  660.1 1.1 constant_dynamic-slice_fusion.7
  664.9 1.1 constant_dynamic-slice_fusion.7
  669.7 1.1 constant_dynamic-slice_fusion.7
  702.6 1.1 copy.100
  703.7 3.6 fusion.4
  708.6 1.3 fusion.102
  709.9 1.8 fusion.29
  711.7 7.1 fusion.38
  719.9 2.1 fusion.5
  722.2 1.3 fusion.64
  723.5 86.3 %reduce-scatter.3.cloned.1.call-done = f32[1,32,8,128]{3,2,1,0:T(8,128)} async-done(((f32[1,1024,8,128]{3,2,1,0:T(8,128)}), f32[1,32,8,128]{3,2,1,0:T(8,128)}) %reduce-scatter.3.cloned.1.call-update) | async-done | bytes 131088 | tf_op jit(solution)/shard_map/reduce_scatter | solution.py:232
  809.8 1.5 convert_element_type.118
  811.4 122.1 %reduce-scatter.5.cloned.1.call-done = f32[1,32,8,128]{3,2,1,0:T(8,128)} async-done(((f32[1,1024,8,128]{3,2,1,0:T(8,128)}), f32[1,32,8,128]{3,2,1,0:T(8,128)}) %reduce-scatter.5.cloned.1.call-update) | async-done | bytes 131088 | tf_op jit(solution)/shard_map/reduce_scatter | solution.py:233
  933.5 1.5 convert_element_type.119
  (408 shorter events, 160.7 us)
Async XLA Ops:
  7.2 73.3 %copy-start = (bf16[1,1024,8,128]{3,2,1,0:T(8,128)(2,1)S(1)}, bf16[1,1024,8,128]{3,2,1,0:T(8,128)(2,1)}, u32[]{:S(2)}) copy-start(bf16[1,1024,8,128]{3,2,1,0:T(8,128)(2,1)} %param.22) | copy-start | bytes 6291460
  7.2 10.7 %copy-start.53 = (u32[256]{0:T(256)S(1)}, u32[256]{0:T(256)}, u32[]{:S(2)}) copy-start(u32[256]{0:T(256)} %constant.107) | copy-start | bytes 3076
  7.2 113.5 %all-gather.9.cloned.1.call-start = ((), (), s32[]{:S(2)}) async-start(), calls=%async_computation.4 | async-start | bytes 17301504 | tf_op jit(solution)/shard_map/all_gather | solution.py:16
  9.3 8.1 copy-start.28
  9.9 7.5 copy-start.37
  10.4 6.9 copy-start.42
  16.3 69.0 %copy-start.52 = (f32[1,1024,4]{1,2,0:T(4,128)S(1)}, f32[1,1024,4]{1,2,0:T(4,128)}, u32[]{:S(2)}) copy-start(f32[1,1024,4]{1,2,0:T(4,128)} %param.23) | copy-start | bytes 49156
  17.3 405.1 %all-reduce.5.cloned.1.call-start = ((), (), s32[]{:S(2)}) async-start(), calls=%async_computation.6 | async-start | bytes 1048576 | tf_op jit(solution)/shard_map/psum | solution.py:33
  85.6 35.1 %copy-start.27 = (f32[256,4,4]{0,2,1:T(4,128)}, f32[256,4,4]{0,2,1:T(4,128)S(1)}, u32[]{:S(2)}) copy-start(f32[256,4,4]{0,2,1:T(4,128)S(1)} %fusion.109) | copy-start | bytes 49156
  85.8 34.9 %copy-start.32 = (f32[4,4]{1,0:T(4,128)}, f32[4,4]{1,0:T(4,128)S(1)}, u32[]{:S(2)}) copy-start(f32[4,4]{1,0:T(4,128)S(1)} %slice_reduce_fusion.2) | copy-start | bytes 196
  85.9 112.2 %copy-start.24 = (f32[4,256,4]{1,2,0:T(4,128)}, f32[4,256,4]{1,2,0:T(4,128)S(1)}, u32[]{:S(2)}) copy-start(f32[4,256,4]{1,2,0:T(4,128)S(1)} %get-tuple-element.326) | copy-start | bytes 49156
  120.7 74.6 %copy-start.38 = (f32[16]{0:T(128)S(1)}, f32[16]{0:T(128)}, u32[]{:S(2)}) copy-start(f32[16]{0:T(128)} %copy-done.37) | copy-start | bytes 196
  120.7 74.6 %copy-start.40 = (f32[16]{0:T(128)S(1)}, f32[16]{0:T(128)}, u32[]{:S(2)}) copy-start(f32[16]{0:T(128)} %get-tuple-element.332) | copy-start | bytes 196
  120.7 74.6 %copy-start.43 = (f32[16]{0:T(128)S(1)}, f32[16]{0:T(128)}, u32[]{:S(2)}) copy-start(f32[16]{0:T(128)} %copy-done.42) | copy-start | bytes 196
  120.7 74.6 %copy-start.47 = (f32[16]{0:T(128)S(1)}, f32[16]{0:T(128)}, u32[]{:S(2)}) copy-start(f32[16]{0:T(128)} %exp.152) | copy-start | bytes 196
  195.0 6.7 copy-start.13
  195.3 6.5 copy-start.33
  195.3 228.7 %copy-start.30 = (f32[2,256,16]{1,2,0:T(8,128)S(1)}, f32[2,256,16]{1,2,0:T(8,128)}, u32[]{:S(2)}) copy-start(f32[2,256,16]{1,2,0:T(8,128)} %get-tuple-element.324) | copy-start | bytes 98308
  198.0 231.0 %copy-start.41 = (f32[16]{0:T(128)S(1)}, f32[16]{0:T(128)}, u32[]{:S(2)}) copy-start(f32[16]{0:T(128)} %get-tuple-element.332) | copy-start | bytes 196
  198.0 231.0 %copy-start.46 = (f32[16]{0:T(128)S(1)}, f32[16]{0:T(128)}, u32[]{:S(2)}) copy-start(f32[16]{0:T(128)} %get-tuple-element.334) | copy-start | bytes 196
  198.0 314.5 %all-reduce.7.cloned.1.call-start = ((), (), s32[]{:S(2)}) async-start(), calls=%async_computation.8 | async-start | bytes 524288 | tf_op jit(solution)/shard_map/psum | solution.py:197
  201.8 323.5 %copy-start.35 = (f32[4]{0:T(128)}, f32[4]{0:T(128)S(1)}, u32[]{:S(2)}) copy-start(f32[4]{0:T(128)S(1)} %get-tuple-element.329) | copy-start | bytes 52
  201.8 323.5 %copy-start.36 = (f32[4]{0:T(128)}, f32[4]{0:T(128)S(1)}, u32[]{:S(2)}) copy-start(f32[4]{0:T(128)S(1)} %get-tuple-element.330) | copy-start | bytes 52
  201.8 323.5 %copy-start.44 = (f32[4]{0:T(128)}, f32[4]{0:T(128)S(1)}, u32[]{:S(2)}) copy-start(f32[4]{0:T(128)S(1)} %get-tuple-element.327) | copy-start | bytes 52
  201.9 323.5 %copy-start.45 = (f32[4]{0:T(128)}, f32[4]{0:T(128)S(1)}, u32[]{:S(2)}) copy-start(f32[4]{0:T(128)S(1)} %get-tuple-element.328) | copy-start | bytes 52
  424.0 102.4 %copy-start.14 = (bf16[1,1024,4,64]{1,3,2,0:T(8,128)(2,1)S(1)}, bf16[1,1024,4,64]{1,3,2,0:T(8,128)(2,1)}, u32[]{:S(2)}) copy-start(bf16[1,1024,4,64]{1,3,2,0:T(8,128)(2,1)} %param.20) | copy-start | bytes 1572868
  424.0 191.7 %all-gather.5.cloned.1.call-start = ((), (), s32[]{:S(2)}) async-start(), calls=%async_computation.2 | async-start | bytes 17301504 | tf_op jit(solution)/shard_map/all_gather | solution.py:16
  430.0 278.6 %all-gather.7.cloned.1.call-start = ((), (), s32[]{:S(2)}) async-start(), calls=%async_computation.3 | async-start | bytes 4325376 | tf_op jit(solution)/shard_map/all_gather | solution.py:208
  512.5 297.3 %reduce-scatter.3.cloned.1.call-start = ((), (), s32[]{:S(2)}) async-start(), calls=%async_computation.5 | async-start | bytes 4325376 | tf_op jit(solution)/shard_map/reduce_scatter | solution.py:232
  526.8 6.5 copy-start.25
  548.7 384.8 %reduce-scatter.5.cloned.1.call-start = ((), (), s32[]{:S(2)}) async-start(), calls=%async_computation.7 | async-start | bytes 4325376 | tf_op jit(solution)/shard_map/reduce_scatter | solution.py:233
  550.4 4.8 copy-start.11
  550.5 4.7 copy-start.17
  550.5 4.7 copy-start.19
  550.5 4.7 copy-start.21
  550.5 4.7 copy-start.49
  555.3 3.7 copy-start.23
  555.3 3.7 copy-start.26
  628.1 75.6 %copy-start.31 = (f32[2,256,16]{1,2,0:T(8,128)S(1)}, f32[2,256,16]{1,2,0:T(8,128)}, u32[]{:S(2)}) copy-start(f32[2,256,16]{1,2,0:T(8,128)} %get-tuple-element.324) | copy-start | bytes 98308
  702.6 4.9 copy-start.8
  702.6 6.0 copy-start.6
  702.6 6.0 copy-start.39
  703.7 4.8 copy-start.10
  708.6 3.1 copy-start.50
  711.7 8.2 copy-start.29
  711.7 8.2 copy-start.51
  711.7 223.3 %copy-start.1 = (bf16[1,1024,8,128]{3,2,1,0:T(8,128)(2,1)S(1)}, bf16[1,1024,8,128]{3,2,1,0:T(8,128)(2,1)}, u32[]{:S(2)}) copy-start(bf16[1,1024,8,128]{3,2,1,0:T(8,128)(2,1)} %param.22) | copy-start | bytes 6291460
  718.8 3.3 copy-start.9
  (13 other events, 23.5 us)
Sparse Core Ops, SparseCore 0:
  17.4 103.2 all-gather.8
  198.1 224.2 all-reduce.4
  425.8 86.6 all-reduce.6
  514.2 101.4 all-gather.4
  617.4 66.9 all-gather.6
  686.7 123.0 reduce-scatter.2
  812.4 121.0 reduce-scatter.4
where the time goes:
time: 956 us; the launch traced here: 942 us
  waiting for transfers between devices  597 us (62%)
  local copies, waits for them, and re-layouts  143 us (15%)
  blocking collectives  60.4 us (6%)
  other arithmetic  57.4 us (6%)
  matrix products  54.7 us (6%)
  between operations  16.7 us (2%)
  starting transfers between devices  10.9 us (1%)
    psum x1, waiting for transfers between devices, from_root(): return lax.psum(jnp.where(mine, shard, jnp.zeros_like(shard)), axis)  220 us
    reduce_scatter x1, waiting for transfers between devices, body(): lax.psum_scatter(full_qgrad, 'seq', scatter_dimension=1, tiled=True)  122 us
    dynamic_slice x124, local copies, waits for them, and re-layouts, hop(): longer = join(so_far, jax.tree.map(lambda part: part[position], pieces))  88.2 us
    reduce_scatter x1, waiting for transfers between devices, body(): lax.psum_scatter(full_kgrad, 'seq', scatter_dimension=1, tiled=True)  86.3 us
    all_gather x2, waiting for transfers between devices, prefix(): pieces = jax.tree.map(lambda part: lax.all_gather(part, axis), value)  86 us
    psum x1, waiting for transfers between devices, body(): state_sum = lax.psum(jnp.sum(start_grad, axis=0), 'comp')  82.5 us
    unnamed x1, blocking collectives  60.4 us
    exp x31, other arithmetic, compose(): jnp.exp(later[0])[:, None, None] * earlier[1] + later[1]  21.5 us
  transfers between devices with their start and end apart: 7, of which 6 were waited for; matrix products, arithmetic and copies ran while one was open for 17% of the time, Pallas kernels for 0%

commit v1 on v0

v1 whole, which is shorter than its diff:
```python
import functools

import jax
import jax.numpy as jnp
from jax import lax
from jax.experimental import pallas as pl
from jax.experimental.pallas import tpu as pltpu
from jax.sharding import PartitionSpec as P

F32 = jnp.float32
BF16 = jnp.bfloat16
T = 128
MID = 63
N = 128
HEAD = 64
VMEM_BYTES = 48 * 1024 * 1024


def dot(left, right):
    return lax.dot_general(left, right, (((1,), (0,)), ((), ())), preferred_element_type=F32)


def dot_nt(left, right):
    return lax.dot_general(left, right, (((1,), (1,)), ((), ())), preferred_element_type=F32)


def split(value):
    high = value.astype(BF16)
    return high, (value - high.astype(F32)).astype(BF16)


def running(logs):
    first, rest = split(logs)
    second, third = split(logs - first.astype(F32))
    upper = lax.broadcasted_iota(jnp.int32, (T, T), 0) <= lax.broadcasted_iota(jnp.int32, (T, T), 1)
    ones = jnp.where(upper, 1.0, 0.0).astype(BF16)
    return dot(first, ones) + (dot(second, ones) + dot(third, ones))


def rows(per_head):
    heads, lanes = per_head.shape
    spread = jnp.broadcast_to(per_head[:, None, :], (heads, HEAD, lanes))
    return spread.reshape(heads * HEAD, lanes)


def column(logs, token):
    return jnp.broadcast_to(logs[:, token : token + 1], logs.shape)


def chunk_logs(logs_ref, number):
    sums = running(logs_ref[:, pl.ds(pl.multiple_of(number * T, T), T)])
    return sums, column(sums, MID), column(sums, T - 1)


def lanes_of(ref, number):
    return ref[:, pl.ds(pl.multiple_of(number * T, T), T)].astype(F32)


def tokens_of(ref, number):
    return ref[pl.ds(pl.multiple_of(number * T, T), T), :]


def live_mask(number, length, width):
    token = lax.broadcasted_iota(jnp.int32, (width, T), 1) + number * T
    return token < length


def twice(value):
    return jnp.concatenate([value, value], axis=0)


def side(left, right):
    return jnp.concatenate([left, right], axis=1)


def ends_kernel(length_ref, cot_ref, logs_ref, query_ref, ends_ref, start_ref):
    chunks, width = ends_ref.shape[0], ends_ref.shape[1]
    start_ref[...] = jnp.zeros_like(start_ref)

    def step(index, carry):
        number = chunks - 1 - index
        sums, mid, last = chunk_logs(logs_ref, number)
        scaled = lanes_of(cot_ref, number) * rows(jnp.exp(sums - mid))
        scaled = jnp.where(live_mask(number, length_ref[0], width), scaled, 0.0)
        high, low = split(scaled)
        pulled = dot(side(high, low), twice(tokens_of(query_ref, number)))
        current = start_ref[...]
        ends_ref[number] = current
        start_ref[...] = rows(jnp.exp(last)) * current + rows(jnp.exp(mid)) * pulled
        return carry

    lax.fori_loop(0, chunks, step, 0)


def summary_kernel(
    input_ref, cot_ref, logs_ref, key_ref, query_ref, carried_ref, pulled_ref, all_c, all_p, total_ref
):
    chunks = carried_ref.shape[0]
    all_c[...] = jnp.zeros_like(all_c)
    all_p[...] = jnp.zeros_like(all_p)
    total_ref[...] = jnp.zeros_like(total_ref)

    def step(number, carry):
        sums, mid, last = chunk_logs(logs_ref, number)
        high, low = split(lanes_of(input_ref, number) * rows(jnp.exp(mid - sums)))
        carried = dot(side(high, low), twice(tokens_of(key_ref, number)))
        carried = rows(jnp.exp(last - mid)) * carried
        carried_ref[number] = carried
        all_c[...] = rows(jnp.exp(last)) * all_c[...] + carried
        high, low = split(lanes_of(cot_ref, number) * rows(jnp.exp(sums - mid)))
        pulled = dot(side(high, low), twice(tokens_of(query_ref, number)))
        pulled = rows(jnp.exp(mid)) * pulled
        pulled_ref[number] = pulled
        all_p[...] = all_p[...] + rows(jnp.exp(total_ref[...])) * pulled
        total_ref[...] = total_ref[...] + last
        return carry

    lax.fori_loop(0, chunks, step, 0)


def scan_kernel(blocks_ref, final_grad_ref, out_ref, final_ref):
    count = blocks_ref.shape[0]
    current = jnp.zeros(final_ref.shape, F32)
    size = current.shape[0]
    for place in range(count):
        out_ref[place, :size] = current
        decay = jnp.exp(blocks_ref[place, 2 * size : 2 * size + 1])
        current = decay * current + blocks_ref[place, :size]
    final_ref[...] = current
    current = final_grad_ref[...]
    for place in range(count - 1, -1, -1):
        out_ref[place, size : 2 * size] = current
        decay = jnp.exp(blocks_ref[place, 2 * size : 2 * size + 1])
        current = decay * current + blocks_ref[place, size : 2 * size]


def chunk_grads(number, inputs, cot, logs3, keys, queries, start, end):
    sums, mid, last = logs3
    grow = rows(jnp.exp(mid - sums))
    fall = rows(jnp.exp(sums - mid))
    in_high, in_low = split(inputs * grow)
    cot_high, cot_low = split(cot * fall)
    end_high, end_low = split(rows(jnp.exp(last - mid)) * end)
    start_high, start_low = split(rows(jnp.exp(mid)) * start)
    first = lax.broadcasted_iota(jnp.int32, (T, T), 0)
    second = lax.broadcasted_iota(jnp.int32, (T, T), 1)
    score_high, score_low = split(jnp.where(first >= second, dot_nt(queries, keys), 0.0))
    input_grad = dot(side(cot_high, cot_low), twice(score_high)) + dot(cot_high, score_low)
    input_grad = input_grad + dot_nt(side(end_high, end_low), side(keys, keys))
    input_grad = grow * input_grad
    in_high_t, in_low_t = in_high.T, in_low.T
    right_high, right_low = side(cot_high, end_high), side(cot_low, end_low)
    both = dot(in_high_t, right_high) + (dot(in_high_t, right_low) + dot(in_low_t, right_high))
    products = jnp.where(second >= first, both[:, :T], 0.0)
    high, low = split(products)
    key_grad = both[:, T:] + dot(side(high, low), twice(queries))
    high, low = split(products.T)
    query_grad = dot(side(high, low), twice(keys))
    cot_high_t, cot_low_t = cot_high.T, cot_low.T
    query_grad = query_grad + dot(cot_high_t, start_high)
    query_grad = query_grad + (dot(cot_high_t, start_low) + dot(cot_low_t, start_high))
    return input_grad, key_grad, query_grad, (in_high, in_low)


def answer_kernel(
    length_ref, input_ref, cot_ref, logs_ref, key_ref, query_ref, ends_ref,
    input_grad_ref, key_grad_ref, query_grad_ref, state_ref,
):
    chunks, width = ends_ref.shape[0], ends_ref.shape[1]
    state_ref[...] = jnp.zeros_like(state_ref)

    def step(number, carry):
        logs3 = chunk_logs(logs_ref, number)
        sums, mid, last = logs3
        cot = jnp.where(live_mask(number, length_ref[0], width), lanes_of(cot_ref, number), 0.0)
        keys, queries = tokens_of(key_ref, number), tokens_of(query_ref, number)
        start = state_ref[...]
        input_grad, key_grad, query_grad, (high, low) = chunk_grads(
            number, lanes_of(input_ref, number), cot, logs3, keys, queries, start, ends_ref[number]
        )
        place = pl.ds(pl.multiple_of(number * T, T), T)
        input_grad_ref[:, place] = input_grad.astype(BF16)
        key_grad_ref[place, :] = key_grad
        query_grad_ref[place, :] = query_grad
        carried = dot(side(high, low), twice(keys))
        state_ref[...] = rows(jnp.exp(last)) * start + rows(jnp.exp(last - mid)) * carried
        return carry

    lax.fori_loop(0, chunks, step, 0)


def prompt_kernel(
    input_ref, cot_ref, logs_ref, key_ref, query_ref, carried_ref, pulled_ref, start_ref, end_ref,
    input_grad_ref, key_grad_ref, query_grad_ref, state_ref, ends_ref,
):
    chunks = carried_ref.shape[0]
    state_ref[...] = end_ref[...]

    def back(index, carry):
        number = chunks - 1 - index
        _, _, last = chunk_logs(logs_ref, number)
        current = state_ref[...]
        ends_ref[number] = current
        state_ref[...] = rows(jnp.exp(last)) * current + pulled_ref[number]
        return carry

    lax.fori_loop(0, chunks, back, 0)
    state_ref[...] = start_ref[...]

    def step(number, carry):
        logs3 = chunk_logs(logs_ref, number)
        keys, queries = tokens_of(key_ref, number), tokens_of(query_ref, number)
        start = state_ref[...]
        input_grad, key_grad, query_grad, _ = chunk_grads(
            number, lanes_of(input_ref, number), lanes_of(cot_ref, number), logs3, keys, queries,
            start, ends_ref[number],
        )
        place = pl.ds(pl.multiple_of(number * T, T), T)
        input_grad_ref[:, place] = input_grad.astype(BF16)
        key_grad_ref[place, :] = key_grad.astype(BF16)
        query_grad_ref[place, :] = query_grad.astype(BF16)
        state_ref[...] = rows(jnp.exp(logs3[2])) * start + carried_ref[number]
        return carry

    lax.fori_loop(0, chunks, step, 0)


def start_part_kernel(length_ref, cot_ref, logs_ref, state_ref, local_ref, out_ref, total_ref):
    chunks, width = out_ref.shape[0] // T, state_ref.shape[0]
    state_high, state_low = split(state_ref[...])
    total_ref[...] = jnp.zeros_like(total_ref)

    def step(number, carry):
        sums, _, last = chunk_logs(logs_ref, number)
        scaled = lanes_of(cot_ref, number) * rows(jnp.exp(total_ref[...] + sums))
        scaled = jnp.where(live_mask(number, length_ref[0], width), scaled, 0.0)
        high, low = split(scaled)
        high, low = high.T, low.T
        part = dot(high, state_high) + (dot(high, state_low) + dot(low, state_high))
        place = pl.ds(pl.multiple_of(number * T, T), T)
        out_ref[place, :] = local_ref[place, :] + part
        total_ref[...] = total_ref[...] + last
        return carry

    lax.fori_loop(0, chunks, step, 0)


def shape(*dims, dtype=F32):
    return jax.ShapeDtypeStruct(dims, dtype)


def call(kernel, outs, scratch=(), scalar=False, count=0, flops=0, name=None):
    vmem = pl.BlockSpec(memory_space=pltpu.VMEM)
    first = [pl.BlockSpec(memory_space=pltpu.SMEM)] if scalar else []
    return pl.pallas_call(
        kernel,
        out_shape=outs,
        in_specs=first + [vmem] * count,
        out_specs=[vmem] * len(outs),
        scratch_shapes=scratch,
        compiler_params=pltpu.CompilerParams(vmem_limit_bytes=VMEM_BYTES),
        cost_estimate=pl.CostEstimate(flops=flops, bytes_accessed=4000000, transcendentals=0),
        name=name,
    )


def body(
    prompt_inputs, prompt_keys, prompt_queries, prompt_logdecay, prompt_cotangent,
    answer_inputs, answer_keys, answer_queries, answer_logdecay, answer_cotangent, answer_lengths,
):
    tokens, heads, _ = prompt_inputs.shape
    _, length, answer_heads, _ = answer_inputs.shape
    width, answer_width = heads * HEAD, answer_heads * HEAD
    chunks, answer_chunks = tokens // T, length // T
    seq, comp = lax.axis_size("seq"), lax.axis_size("comp")
    quads = heads // answer_heads
    planes = seq // quads
    part = answer_width // planes
    swap = [
        ((z * quads + q) * comp + c, (c * quads + q) * comp + z)
        for z in range(planes) for q in range(quads) for c in range(comp)
    ]
    group = lax.axis_index("seq") // quads

    x = jnp.transpose(prompt_inputs, (1, 2, 0)).reshape(width, tokens)
    cot = jnp.transpose(prompt_cotangent, (1, 2, 0)).reshape(width, tokens)
    logs = prompt_logdecay.T
    keys, queries = prompt_keys.reshape(tokens, N), prompt_queries.reshape(tokens, N)
    ax = jnp.transpose(answer_inputs[0], (1, 2, 0)).reshape(answer_width, length)
    acot = jnp.transpose(answer_cotangent[0], (1, 2, 0)).reshape(answer_width, length)
    alogs = answer_logdecay[0].T
    akeys = lax.dynamic_slice_in_dim(answer_keys[0], group, 1, 1).reshape(length, N)
    aqueries = lax.dynamic_slice_in_dim(answer_queries[0], group, 1, 1).reshape(length, N)

    ends, start_grad = call(
        ends_kernel, [shape(answer_chunks, answer_width, N), shape(answer_width, N)],
        scalar=True, count=3, flops=10**9, name="answer_ends",
    )(answer_lengths, acot, alogs, aqueries)
    parts = lax.all_to_all(start_grad.reshape(comp, part, N), "comp", 0, 0, tiled=True)
    final_grad = lax.ppermute(jnp.sum(parts, axis=0), ("seq", "comp"), swap)

    carried, pulled, all_carried, all_pulled, totals = call(
        summary_kernel,
        [shape(chunks, width, N), shape(chunks, width, N), shape(width, N), shape(width, N), shape(heads, N)],
        count=5, flops=10**9, name="prompt_summary",
    )(x, cot, logs, keys, queries)

    ax_grad, ak_grad, aq_local = call(
        answer_kernel,
        [shape(answer_width, length, dtype=BF16), shape(length, N), shape(length, N)],
        scratch=[pltpu.VMEM((answer_width, N), F32)],
        scalar=True, count=6, flops=2 * 10**9, name="answer_grads",
    )(answer_lengths, ax, acot, alogs, akeys, aqueries, ends)

    def by_owner(value):
        value = value.reshape(quads, planes, part, N)
        return jnp.swapaxes(value, 0, 1).reshape(seq, part, N)

    def by_row(value):
        value = value.reshape(planes, quads, part, N)
        return jnp.swapaxes(value, 0, 1).reshape(width, N)

    slice_total = jnp.repeat(totals, HEAD // part, axis=0)[:, None, :]
    slice_total = jnp.broadcast_to(slice_total, (seq, 8, N)).reshape(quads, planes, 8, N)
    slice_total = jnp.swapaxes(slice_total, 0, 1).reshape(seq, 8, N)
    token_part = length // seq
    sent = jnp.concatenate(
        [by_owner(all_carried), by_owner(all_pulled), slice_total, ak_grad.reshape(seq, token_part, N)], axis=1
    )
    got = lax.all_to_all(sent, "seq", 0, 0, tiled=True)
    back, final = call(
        scan_kernel, [shape(seq, 2 * part, N), shape(part, N)], count=2, flops=10**7, name="scan"
    )(got, final_grad)
    key_parts = got[:, 2 * part + 8 :]

    final = lax.ppermute(final, ("seq", "comp"), swap)
    final = lax.all_to_all(jnp.broadcast_to(final[None], (comp, part, N)), "comp", 0, 0, tiled=True)
    (aq_grad,) = call(
        start_part_kernel, [shape(length, N)], scratch=[pltpu.VMEM((answer_heads, N), F32)],
        scalar=True, count=4, flops=10**9, name="answer_start_part",
    )(answer_lengths, acot, alogs, final.reshape(answer_width, N), aq_local)
    sent = jnp.concatenate([back, aq_grad.reshape(seq, token_part, N)], axis=1)
    got = lax.all_to_all(sent, "seq", 0, 0, tiled=True)
    start, end = by_row(got[:, :part]), by_row(got[:, part : 2 * part])
    query_parts = got[:, 2 * part :]

    x_grad, k_grad, q_grad = call(
        prompt_kernel,
        [shape(width, tokens, dtype=BF16), shape(tokens, N, dtype=BF16), shape(tokens, N, dtype=BF16)],
        scratch=[pltpu.VMEM((width, N), F32), pltpu.VMEM((chunks, width, N), F32)],
        count=9, flops=3 * 10**9, name="prompt_grads",
    )(x, cot, logs, keys, queries, carried, pulled, start, end)

    def gather_groups(parts):
        summed = jnp.sum(parts.reshape(planes, quads, token_part, N), axis=1)
        return jnp.swapaxes(summed, 0, 1)[None].astype(BF16)

    return (
        jnp.transpose(x_grad.reshape(heads, HEAD, tokens), (2, 0, 1)),
        k_grad.reshape(tokens, 1, N),
        q_grad.reshape(tokens, 1, N),
        jnp.transpose(ax_grad.reshape(answer_heads, HEAD, length), (2, 0, 1))[None],
        gather_groups(key_parts),
        gather_groups(query_parts),
    )


def solution(mesh):
    in_specs = (
        P("seq", "comp", None),
        P("seq", "comp", None),
        P("seq", "comp", None),
        P("seq", "comp"),
        P("seq", "comp", None),
        P("comp", None, "seq", None),
        P("comp", None, None, None),
        P("comp", None, None, None),
        P("comp", None, "seq"),
        P("comp", None, "seq", None),
        P("comp"),
    )
    out_specs = (
        P("seq", "comp", None),
        P("seq", "comp", None),
        P("seq", "comp", None),
        P("comp", None, "seq", None),
        P("comp", "seq", None, None),
        P("comp", "seq", None, None),
    )
    return jax.shard_map(body, mesh=mesh, in_specs=in_specs, out_specs=out_specs, check_vma=False)
```

time: 956 us -> 182 us (0.19); the launches traced: 942 us -> 179 us
  waiting for transfers between devices: 597 us -> 83.4 us
  local copies, waits for them, and re-layouts: 143 us -> 13.2 us
  matrix products: 54.7 us -> 0 us
  other arithmetic: 57.4 us -> 5.32 us
  blocking collectives: 60.4 us -> 19.7 us
  Pallas kernels: 0 us -> 29.1 us
  starting transfers between devices: 10.9 us -> 26.7 us
  between operations: 16.7 us -> 1.61 us
    psum x2 -> x0, waiting for transfers between devices: 302 us -> none  [the longest x1 220 us: from_root(): return lax.psum(jnp.where(mine, shard, jnp.zeros_like(shard)), axis)]
    reduce_scatter x2 -> x0, waiting for transfers between devices: 208 us -> none  [the longest x1 122 us: body(): lax.psum_scatter(full_qgrad, 'seq', scatter_dimension=1, tiled=True)]
    dynamic_slice x126 -> x1, local copies, waits for them, and re-layouts: 90.9 us -> 4.1 us  [body(): lax.dynamic_slice_in_dim(answer_queries[0], group, 1, 1).reshape(length, N)]
    all_gather x3 -> x0, waiting for transfers between devices: 86 us -> none  [the longest x2 86 us: prefix(): pieces = jax.tree.map(lambda part: lax.all_gather(part, axis), value)]
    unnamed x1 -> x0, blocking collectives: 60.4 us -> none
    dot_general x21 -> x0, matrix products: 54.4 us -> none  [the longest x2 11.8 us: block_grads(): jnp.einsum('mhts,mthp->mshp', masked_scores, cotangent, precision=PRECISE)]
    all_to_all x0 -> x3, waiting for transfers between devices: none -> 42.6 us  [the longest x2 42.6 us: body(): got = lax.all_to_all(sent, 'seq', 0, 0, tiled=True)]
    ppermute x0 -> x2, waiting for transfers between devices: none -> 40.8 us  [the longest x1 35.2 us: body(): final_grad = lax.ppermute(jnp.sum(parts, axis=0), ('seq', 'comp'), swap)]
  transfers between devices with their start and end apart: 7 -> 5, of which waited for: 6 -> 4; matrix products, arithmetic and copies ran while one was open for 17% -> 3% of each run, Pallas kernels for 0% -> 6%
where the time goes in v1:
time: 182 us; the launch traced here: 179 us
  waiting for transfers between devices  83.4 us (46%)
  Pallas kernels  29.1 us (16%)
  starting transfers between devices  26.7 us (15%)
  blocking collectives  19.7 us (11%)
  local copies, waits for them, and re-layouts  13.2 us (7%)
  other arithmetic  5.32 us (3%)
    all_to_all x2, waiting for transfers between devices, body(): got = lax.all_to_all(sent, 'seq', 0, 0, tiled=True)  42.6 us
    ppermute x1, waiting for transfers between devices, body(): final_grad = lax.ppermute(jnp.sum(parts, axis=0), ('seq', 'comp'), swap)  35.2 us
    all_to_all x1, blocking collectives, body(): lax.all_to_all(jnp.broadcast_to(final[None], (comp, part, N)), 'comp', 0,...  19.7 us
    all_to_all x2, starting transfers between devices, body(): got = lax.all_to_all(sent, 'seq', 0, 0, tiled=True)  14.3 us
    pallas_call x1, Pallas kernels, body(): call(prompt_kernel, [shape(width, tokens, dtype=BF16), shape(tokens, N, d...  9.97 us
    unnamed x40, local copies, waits for them, and re-layouts  7.49 us
    all_to_all x1, starting transfers between devices, body(): lax.all_to_all(start_grad.reshape(comp, part, N), 'comp', 0, 0, tiled=True)  7.26 us
    pallas_call x1, Pallas kernels, body(): call(answer_kernel, [shape(answer_width, length, dtype=BF16), shape(lengt...  7.05 us
  transfers between devices with their start and end apart: 5, of which 4 were waited for; matrix products, arithmetic and copies ran while one was open for 3% of the time, Pallas kernels for 6%

profile of v1, /device:TPU:16, one launch (start us, length us, event | category | flops | bytes accessed | tf_op | source)
XLA Modules:
  0.0 179.0 jit_solution(3848045876439971545)
XLA Ops:
  0.6 0.0 copy-start.4
  0.6 0.0 copy-start.9
  1.4 4.1 %constant_dynamic-slice_fusion = (bf16[1,1024,1,128]{3,2,1,0:T(2,128)(2,1)S(1)}, bf16[1,1024,1,128]{3,2,1,0:T(2,128)(2,1)}) fusion(bf16[1,1024,8,128]{3,2,1,0:T(8,128)(2,1)} %param.18, s32[]{:T(128)S(6)} %select_n.10, bf16[1,1024,8,128]{3,2,1,0:T(8,128)(2,1)} %param.17), kind=kLoop, calls=%fused_computation.8 | loop fusion | bytes 1048580 | tf_op jit(solution)/shard_map/dynamic_slice | solution.py:293
  5.5 0.0 copy-done.4
  5.5 0.0 copy-done.9
  5.5 0.0 copy-start
  5.5 0.0 copy-start.1
  5.6 0.0 copy-start.5
  5.6 0.0 copy-start.6
  5.6 0.0 copy-start.7
  5.6 4.2 %answer_ends.1 = (f32[8,256,128]{2,1,0:T(8,128)S(1)}, f32[256,128]{1,0:T(8,128)}) custom-call(s32[1]{0:T(128)S(6)} %copy.43.length_ref, bf16[256,1024]{1,0:T(8,128)(2,1)S(1)} %bitcast.91, f32[4,1024]{1,0:T(4,128)S(1)} %bitcast.100, bf16[1024,128]{1,0:T(8,128)(2,1)S(1)} %bitcast.82), custom_call_target="tpu_custom_call" | custom-call | flops 1000000000 | bytes 4000000 | tf_op jit(solution)/shard_map/answer_ends/pallas_call | solution.py:295
  9.7 1.0 copy-done.15
  10.7 7.3 %all-to-all-start.1 = ((f32[8,32,128]{2,1,0:T(8,128)}), f32[8,32,128]{2,1,0:T(8,128)S(1)}, u32[]{:S(2)}, u32[]{:S(2)}) async-start(f32[8,32,128]{2,1,0:T(8,128)} %bitcast.32), calls=%async_computation.1 | async-start | bytes 262144 | tf_op jit(solution)/shard_map/all_to_all | solution.py:299
  18.0 1.1 copy.42
  19.1 0.0 copy-done
  19.1 0.0 copy-done.1
  19.1 0.0 copy-done.5
  19.1 4.2 %prompt_summary.1 = (f32[4,1024,128]{2,1,0:T(8,128)S(1)}, f32[4,1024,128]{2,1,0:T(8,128)}, f32[1024,128]{1,0:T(8,128)S(1)}, f32[1024,128]{1,0:T(8,128)S(1)}, f32[16,128]{1,0:T(8,128)S(1)}) custom-call(bf16[1024,512]{1,0:T(8,128)(2,1)S(1)} %bitcast.86, bf16[1024,512]{1,0:T(8,128)(2,1)S(1)} %bitcast.88, f32[16,512]{1,0:T(8,128)S(1)} %bitcast.98, ...), custom_call_target="tpu_custom_call" | custom-call | flops 1000000000 | bytes 4000000 | tf_op jit(solution)/shard_map/prompt_summary/pallas_call | solution.py:302
  23.3 1.3 copy-done.11
  24.7 0.9 copy-done.3
  25.6 0.3 copy-done.16
  26.0 7.1 %answer_grads.1 = (bf16[256,1024]{1,0:T(8,128)(2,1)}, f32[1024,128]{1,0:T(8,128)S(1)}, f32[1024,128]{1,0:T(8,128)S(1)}) custom-call(s32[1]{0:T(128)S(6)} %copy.43.length_ref, bf16[256,1024]{1,0:T(8,128)(2,1)S(1)} %bitcast.90, bf16[256,1024]{1,0:T(8,128)(2,1)S(1)} %bitcast.92, f32[4,1024]{1,0:T(4,128)S(1)} %bitcast.101, bf16[1024,128]{1,0:T(8,128)(2,1)S(1)} %bitcast.84, ...), custom_call_target="tpu_custom_call" | custom-call | flops 2000000000 | bytes 4000000 | tf_op jit(solution)/shard_map/answer_grads/pallas_call | solution.py:308
  33.0 0.8 copy-done.13
  33.9 1.3 pad_maximum_fusion
  35.2 0.0 all-to-all-done.1
  35.2 0.7 copy-done.17
  35.8 9.6 %all-to-all-start = ((f32[32,104,128]{2,1,0:T(8,128)}), f32[32,104,128]{2,1,0:T(8,128)S(1)}, u32[]{:S(2)}, u32[]{:S(2)}) async-start(f32[32,104,128]{2,1,0:T(8,128)} %pad_maximum_fusion), calls=%async_computation | async-start | bytes 3407872 | tf_op jit(solution)/shard_map/all_to_all | solution.py:330
  45.4 1.5 reduce_sum.27
  46.9 2.5 %collective-permute-start = (f32[32,128]{1,0:T(8,128)}, f32[32,128]{1,0:T(8,128)S(1)}, u32[]{:S(2)}, u32[]{:S(2)}) collective-permute-start(f32[32,128]{1,0:T(8,128)} %reduce_sum.27), channel_id=1, source_target_pairs={{0,0},{1,32},{2,64},{3,96},{4,128},{5,160},{6,192},{7,224},{8,8},{... | collective-permute-start | bytes 49160 | tf_op jit(solution)/shard_map/ppermute | solution.py:300
  49.5 35.2 %collective-permute-done.final_grad_ref = f32[32,128]{1,0:T(8,128)S(1)} collective-permute-done((f32[32,128]{1,0:T(8,128)}, f32[32,128]{1,0:T(8,128)S(1)}, u32[]{:S(2)}, u32[]{:S(2)}) %collective-permute-start) | collective-permute-done | bytes 16416 | tf_op jit(solution)/shard_map/ppermute | solution.py:300
  84.7 2.9 %all-to-all-done.blocks_ref = f32[32,104,128]{2,1,0:T(8,128)S(1)} async-done(((f32[32,104,128]{2,1,0:T(8,128)}), f32[32,104,128]{2,1,0:T(8,128)S(1)}, u32[]{:S(2)}, u32[]{:S(2)}) %all-to-all-start) | async-done | bytes 1703968 | tf_op jit(solution)/shard_map/all_to_all | solution.py:330
  87.6 0.1 scan.1
  87.7 2.6 %collective-permute-start.1 = (f32[32,128]{1,0:T(8,128)S(1)}, f32[32,128]{1,0:T(8,128)S(1)}, u32[]{:S(2)}, u32[]{:S(2)}) collective-permute-start(f32[32,128]{1,0:T(8,128)S(1)} %get-tuple-element.30), channel_id=1, source_target_pairs={{0,0},{1,32},{2,64},{3,96},{4,128},{5,160},{6,192},{7,224},{8,8},{... | collective-permute-start | bytes 49160 | tf_op jit(solution)/shard_map/ppermute | solution.py:336
  90.3 5.6 %collective-permute-done.1 = f32[32,128]{1,0:T(8,128)S(1)} collective-permute-done((f32[32,128]{1,0:T(8,128)S(1)}, f32[32,128]{1,0:T(8,128)S(1)}, u32[]{:S(2)}, u32[]{:S(2)}) %collective-permute-start.1) | collective-permute-done | bytes 16416 | tf_op jit(solution)/shard_map/ppermute | solution.py:336
  95.9 19.7 %all_to_all.20 = f32[8,32,128]{2,1,0:T(8,128)S(1)} all-to-all(f32[8,32,128]{2,1,0:T(8,128)S(1)} %broadcast_in_dim.24), channel_id=1, replica_groups=mesh['seq'=32,'comp'=8] {'comp'}, dimensions={0} | all-to-all | bytes 262144 | tf_op jit(solution)/shard_map/all_to_all | solution.py:337
  115.6 0.0 copy-done.14
  115.6 3.6 %answer_start_part.1 = f32[1024,128]{1,0:T(8,128)S(1)} custom-call(s32[1]{0:T(128)S(6)} %copy.43.length_ref, bf16[256,1024]{1,0:T(8,128)(2,1)S(1)} %bitcast.93, f32[4,1024]{1,0:T(4,128)S(1)} %bitcast.102, f32[256,128]{1,0:T(8,128)S(1)} %bitcast.85, f32[1024,128]{1,0:T(8,128)S(1)} %copy-done.14), custom_call_target="tpu_custom_call" | custom-call | flops 1000000000 | bytes 4000000 | tf_op jit(solution)/shard_map/answer_start_part/pallas_call | solution.py:338
  119.2 1.3 pad_maximum_fusion.1
  120.5 4.7 %all-to-all-start.3 = ((f32[32,96,128]{2,1,0:T(8,128)}), f32[32,96,128]{2,1,0:T(8,128)}, u32[]{:S(2)}, u32[]{:S(2)}) async-start(f32[32,96,128]{2,1,0:T(8,128)} %pad_maximum_fusion.1), calls=%async_computation.3 | async-start | bytes 3145728 | tf_op jit(solution)/shard_map/all_to_all | solution.py:343
  125.3 0.7 copy.35
  125.9 39.8 %all-to-all-done.3 = f32[32,96,128]{2,1,0:T(8,128)} async-done(((f32[32,96,128]{2,1,0:T(8,128)}), f32[32,96,128]{2,1,0:T(8,128)}, u32[]{:S(2)}, u32[]{:S(2)}) %all-to-all-start.3) | async-done | bytes 1572896 | tf_op jit(solution)/shard_map/all_to_all | solution.py:343
  165.7 1.4 fusion
  167.1 0.0 copy-start.2
  167.1 0.0 copy-start.8
  167.2 1.2 bitcast_reduce_fusion
  168.4 0.7 copy.36
  169.1 0.0 copy-done.8
  169.1 10.0 %prompt_grads.1 = (bf16[1024,512]{1,0:T(8,128)(2,1)}, bf16[512,128]{1,0:T(8,128)(2,1)}, bf16[512,128]{1,0:T(8,128)(2,1)}) custom-call(bf16[1024,512]{1,0:T(8,128)(2,1)S(1)} %bitcast.87, bf16[1024,512]{1,0:T(8,128)(2,1)S(1)} %bitcast.89, f32[16,512]{1,0:T(8,128)S(1)} %bitcast.99, bf16[512,128]{1,0:T(8,128)(2,1)S(1)} %bitcast.95, ...), custom_call_target="tpu_custom_call" | custom-call | flops 3000000000 | bytes 4000000 | tf_op jit(solution)/shard_map/prompt_grads/pallas_call | solution.py:347
  (24 shorter events, 0.3 us)
Async XLA Ops:
  0.6 4.9 %copy-start.4 = (bf16[1,1024,4,64]{1,3,2,0:T(8,128)(2,1)S(1)}, bf16[1,1024,4,64]{1,3,2,0:T(8,128)(2,1)}, u32[]{:S(2)}) copy-start(bf16[1,1024,4,64]{1,3,2,0:T(8,128)(2,1)} %param.20) | copy-start | bytes 1572868
  0.6 4.9 %copy-start.9 = (f32[1,1024,4]{1,2,0:T(4,128)S(1)}, f32[1,1024,4]{1,2,0:T(4,128)}, u32[]{:S(2)}) copy-start(f32[1,1024,4]{1,2,0:T(4,128)} %param.19) | copy-start | bytes 49156
  5.5 13.5 %copy-start = (bf16[512,16,64]{0,2,1:T(8,128)(2,1)S(1)}, bf16[512,16,64]{0,2,1:T(8,128)(2,1)}, u32[]{:S(2)}) copy-start(bf16[512,16,64]{0,2,1:T(8,128)(2,1)} %param.11) | copy-start | bytes 3145732
  5.5 13.5 %copy-start.1 = (bf16[512,16,64]{0,2,1:T(8,128)(2,1)S(1)}, bf16[512,16,64]{0,2,1:T(8,128)(2,1)}, u32[]{:S(2)}) copy-start(bf16[512,16,64]{0,2,1:T(8,128)(2,1)} %param.15) | copy-start | bytes 3145732
  5.6 13.5 %copy-start.5 = (bf16[512,1,128]{2,0,1:T(8,128)(2,1)S(1)}, bf16[512,1,128]{2,0,1:T(8,128)(2,1)}, u32[]{:S(2)}) copy-start(bf16[512,1,128]{2,0,1:T(8,128)(2,1)} %param.12) | copy-start | bytes 393220
  5.6 13.5 %copy-start.6 = (bf16[512,1,128]{2,0,1:T(8,128)(2,1)S(1)}, bf16[512,1,128]{2,0,1:T(8,128)(2,1)}, u32[]{:S(2)}) copy-start(bf16[512,1,128]{2,0,1:T(8,128)(2,1)} %param.13) | copy-start | bytes 393220
  5.6 13.5 %copy-start.7 = (f32[512,16]{0,1:T(8,128)S(1)}, f32[512,16]{0,1:T(8,128)}, u32[]{:S(2)}) copy-start(f32[512,16]{0,1:T(8,128)} %param.14) | copy-start | bytes 98308
  9.7 1.0 copy-start.15
  10.7 24.5 %all-to-all-start.1 = ((f32[8,32,128]{2,1,0:T(8,128)}), f32[8,32,128]{2,1,0:T(8,128)S(1)}, u32[]{:S(2)}, u32[]{:S(2)}) async-start(f32[8,32,128]{2,1,0:T(8,128)} %bitcast.32), calls=%async_computation.1 | async-start | bytes 262144 | tf_op jit(solution)/shard_map/all_to_all | solution.py:299
  23.3 1.3 copy-start.11
  24.6 1.0 copy-start.3
  24.6 1.4 copy-start.16
  33.0 0.8 copy-start.13
  35.2 0.7 copy-start.17
  35.8 51.7 %all-to-all-start = ((f32[32,104,128]{2,1,0:T(8,128)}), f32[32,104,128]{2,1,0:T(8,128)S(1)}, u32[]{:S(2)}, u32[]{:S(2)}) async-start(f32[32,104,128]{2,1,0:T(8,128)} %pad_maximum_fusion), calls=%async_computation | async-start | bytes 3407872 | tf_op jit(solution)/shard_map/all_to_all | solution.py:330
  46.9 37.8 %collective-permute-start = (f32[32,128]{1,0:T(8,128)}, f32[32,128]{1,0:T(8,128)S(1)}, u32[]{:S(2)}, u32[]{:S(2)}) collective-permute-start(f32[32,128]{1,0:T(8,128)} %reduce_sum.27), channel_id=1, source_target_pairs={{0,0},{1,32},{2,64},{3,96},{4,128},{5,160},{6,192},{7,224},{8,8},{... | collective-permute-start | bytes 49160 | tf_op jit(solution)/shard_map/ppermute | solution.py:300
  87.6 28.0 %copy-start.10 = (f32[1,1024,4]{1,2,0:T(4,128)S(1)}, f32[1,1024,4]{1,2,0:T(4,128)}, u32[]{:S(2)}) copy-start(f32[1,1024,4]{1,2,0:T(4,128)} %param.19) | copy-start | bytes 49156
  87.6 28.0 %copy-start.14 = (f32[1024,128]{1,0:T(8,128)S(1)}, f32[1024,128]{1,0:T(8,128)}, u32[]{:S(2)}) copy-start(f32[1024,128]{1,0:T(8,128)} %copy-done.13) | copy-start | bytes 1572868
  87.7 8.2 %collective-permute-start.1 = (f32[32,128]{1,0:T(8,128)S(1)}, f32[32,128]{1,0:T(8,128)S(1)}, u32[]{:S(2)}, u32[]{:S(2)}) collective-permute-start(f32[32,128]{1,0:T(8,128)S(1)} %get-tuple-element.30), channel_id=1, source_target_pairs={{0,0},{1,32},{2,64},{3,96},{4,128},{5,160},{6,192},{7,224},{8,8},{... | collective-permute-start | bytes 49160 | tf_op jit(solution)/shard_map/ppermute | solution.py:336
  120.5 45.2 %all-to-all-start.3 = ((f32[32,96,128]{2,1,0:T(8,128)}), f32[32,96,128]{2,1,0:T(8,128)}, u32[]{:S(2)}, u32[]{:S(2)}) async-start(f32[32,96,128]{2,1,0:T(8,128)} %pad_maximum_fusion.1), calls=%async_computation.3 | async-start | bytes 3145728 | tf_op jit(solution)/shard_map/all_to_all | solution.py:343
  165.7 3.4 %copy-start.12 = (f32[4,1024,128]{2,1,0:T(8,128)S(1)}, f32[4,1024,128]{2,1,0:T(8,128)}, u32[]{:S(2)}) copy-start(f32[4,1024,128]{2,1,0:T(8,128)} %copy-done.11) | copy-start | bytes 6291460
  167.1 1.9 %copy-start.2 = (bf16[512,16,64]{0,2,1:T(8,128)(2,1)S(1)}, bf16[512,16,64]{0,2,1:T(8,128)(2,1)}, u32[]{:S(2)}) copy-start(bf16[512,16,64]{0,2,1:T(8,128)(2,1)} %param.15) | copy-start | bytes 3145732
  167.1 1.9 %copy-start.8 = (f32[512,16]{0,1:T(8,128)S(1)}, f32[512,16]{0,1:T(8,128)}, u32[]{:S(2)}) copy-start(f32[512,16]{0,1:T(8,128)} %param.14) | copy-start | bytes 98308

commit v2 on v1

v2 whole, which is shorter than its diff:
```python
import functools

import jax
import jax.numpy as jnp
from jax import lax
from jax.experimental import pallas as pl
from jax.experimental.pallas import tpu as pltpu
from jax.sharding import PartitionSpec as P

F32 = jnp.float32
BF16 = jnp.bfloat16
T = 128
MID = 63
N = 128
GROUPS = 8
HEAD = 64
PART = 32
SMALL, LARGE = 16 * 1024 * 1024, 56 * 1024 * 1024


def dot(left, right):
    return lax.dot_general(left, right, (((1,), (0,)), ((), ())), preferred_element_type=F32)


def dot_nt(left, right):
    return lax.dot_general(left, right, (((1,), (1,)), ((), ())), preferred_element_type=F32)


def split(value):
    high = value.astype(BF16)
    return high, (value - high.astype(F32)).astype(BF16)


def running(logs):
    first, rest = split(logs)
    second, third = split(logs - first.astype(F32))
    upper = lax.broadcasted_iota(jnp.int32, (T, T), 0) <= lax.broadcasted_iota(jnp.int32, (T, T), 1)
    ones = jnp.where(upper, 1.0, 0.0).astype(BF16)
    return dot(first, ones) + (dot(second, ones) + dot(third, ones))


def rows(per_head):
    heads, lanes = per_head.shape
    spread = jnp.broadcast_to(per_head[:, None, :], (heads, HEAD, lanes))
    return spread.reshape(heads * HEAD, lanes)


def column(logs, token):
    return jnp.broadcast_to(logs[:, token : token + 1], logs.shape)


def chunk_logs(logs_ref, number):
    return block_logs(logs_ref[:, number * T : (number + 1) * T])


def block_logs(logs):
    sums = running(logs)
    return sums, column(sums, MID), column(sums, T - 1)


def tokens_of(ref, number):
    return ref[number * T : (number + 1) * T, :]


def lanes_at(ref, number):
    return ref.at[:, number * T : (number + 1) * T]


def tokens_at(ref, number, count=T):
    return ref.at[number * count : (number + 1) * count, :]


def start_copies(pairs, sems, first=0):
    copies = [pltpu.make_async_copy(source, target, sems.at[first + n]) for n, (source, target) in enumerate(pairs)]
    for copy in copies:
        copy.start()
    return copies


def wait_all(copies):
    for copy in copies:
        copy.wait()


def lanes_of(ref, number):
    return ref[:, number * T : (number + 1) * T]


def chunk_pairs(hbm_ref, ref, order):
    return [(hbm_ref.at[n], ref.at[n]) for n in order]


def live_mask(number, length, width):
    token = lax.broadcasted_iota(jnp.int32, (width, T), 1) + number * T
    return token < length


def twice(value):
    return jnp.concatenate([value, value], axis=0)


def side(left, right):
    return jnp.concatenate([left, right], axis=1)


def own_group(ref, group, all_ref):
    all_ref[...] = ref.astype(F32)
    return all_ref[pl.ds(group, T, stride=GROUPS), :].astype(BF16)


def ends_kernel(
    length_ref, group_ref, cot_hbm, logs_hbm, key_hbm, query_hbm, ends_hbm, own_key_hbm, own_query_hbm, start_ref,
    cot_ref, logs_ref, ends_ref, own_key_ref, own_query_ref, raw_k, raw_q, all_k, all_q, sems,
):
    chunks, width = ends_ref.shape[0], ends_ref.shape[1]
    order = list(range(chunks - 1, -1, -1))
    raw_pairs = [(tokens_at(query_hbm, n, T * GROUPS), raw_q.at[n]) for n in order]
    pairs = [(logs_hbm, logs_ref), (cot_hbm, cot_ref)] + raw_pairs
    pairs += [(tokens_at(key_hbm, n, T * GROUPS), raw_k.at[n]) for n in order]
    copies = start_copies(pairs, sems)
    wait_all(copies[:2])
    current = jnp.zeros((width, N), F32)
    sent = []
    for step, n in enumerate(order):
        copies[2 + step].wait()
        queries = own_group(raw_q[n], group_ref[0], all_q.at[step % 2])
        own_query_ref[n * T : (n + 1) * T, :] = queries
        sums, mid, last = chunk_logs(logs_ref, n)
        scaled = lanes_of(cot_ref, n).astype(F32) * rows(jnp.exp(sums - mid))
        scaled = jnp.where(live_mask(n, length_ref[0], width), scaled, 0.0)
        high, low = split(scaled)
        pulled = dot(side(high, low), twice(queries))
        ends_ref[n] = current
        sent += start_copies([(ends_ref.at[n], ends_hbm.at[n])], sems, len(copies) + step)
        current = rows(jnp.exp(last)) * current + rows(jnp.exp(mid)) * pulled
    start_ref[...] = current
    for step, n in enumerate(order):
        copies[2 + chunks + step].wait()
        own_key_ref[n * T : (n + 1) * T, :] = own_group(raw_k[n], group_ref[0], all_k.at[step % 2])
    pairs = [(own_key_ref, own_key_hbm), (own_query_ref, own_query_hbm)]
    wait_all(sent + start_copies(pairs, sems, len(copies) + chunks))


PLANES = 8


def half_rows(place, core):
    return pl.multiple_of((place // PLANES) * 8 * HEAD + core * 4 * HEAD + (place % PLANES) * PART, PART)


def summary_kernel(
    core_ref, input_hbm, cot_hbm, logs_hbm, key_hbm, query_hbm,
    carried_hbm, pulled_hbm, mine_ref, peer_ref, total_ref,
    input_ref, cot_ref, logs_ref, key_ref, query_ref, carried_ref, pulled_ref, all_c, all_p, sems,
):
    chunks = carried_ref.shape[0]
    order = range(chunks)
    pairs = [
        (logs_hbm, logs_ref), (key_hbm, key_ref), (input_hbm, input_ref), (query_hbm, query_ref), (cot_hbm, cot_ref)
    ]
    copies = start_copies(pairs, sems)
    wait_all(copies[:3])
    total = jnp.zeros(total_ref.shape, F32)
    sent = []
    for n in order:
        sums, mid, last = chunk_logs(logs_ref, n)
        high, low = split(lanes_of(input_ref, n).astype(F32) * rows(jnp.exp(mid - sums)))
        carried = dot(side(high, low), twice(tokens_of(key_ref, n)))
        carried = rows(jnp.exp(last - mid)) * carried
        carried_ref[n] = carried
        sent += start_copies([(carried_ref.at[n], carried_hbm.at[n])], sems, len(copies) + 2 * n)
        all_c[...] = carried if n == 0 else rows(jnp.exp(last)) * all_c[...] + carried
        if n == 0:
            wait_all(copies[3:])
        high, low = split(lanes_of(cot_ref, n).astype(F32) * rows(jnp.exp(sums - mid)))
        pulled = dot(side(high, low), twice(tokens_of(query_ref, n)))
        pulled = rows(jnp.exp(mid)) * pulled
        pulled_ref[n] = pulled
        sent += start_copies([(pulled_ref.at[n], pulled_hbm.at[n])], sems, len(copies) + 2 * n + 1)
        all_p[...] = pulled if n == 0 else all_p[...] + rows(jnp.exp(total)) * pulled
        total = total + last
    total_ref[...] = total
    core = core_ref[0]
    places = mine_ref.shape[0]
    for place in range(places):
        for ref, side_core in ((mine_ref, core), (peer_ref, 1 - core)):
            here = pl.ds(half_rows(place, side_core), PART)
            ref[place, :PART] = all_c[here, :]
            ref[place, PART:] = all_p[here, :]
    heads = total_ref.shape[0]
    peer_ref[places, :heads] = total_ref[...]
    peer_ref[places, heads:] = jnp.zeros_like(peer_ref[places, heads:])
    wait_all(sent)


def both_totals(first, head, mine_ref, got_ref):
    mine = mine_ref[pl.ds(head, 1), :]
    theirs = got_ref[got_ref.shape[0] - 1, pl.ds(head, 1), :]
    return jnp.where(first, mine, theirs), jnp.where(first, theirs, mine)


STATES = 2 * PART
GRADS = STATES + 8


def head_of(place, side_y, core):
    return side_y * 8 + core * 4 + place * PART // HEAD


def joined(first, mine, theirs, total0, total1):
    zero, one = jnp.where(first, mine, theirs), jnp.where(first, theirs, mine)
    return jnp.exp(total1) * zero[:PART] + one[:PART], zero[PART:] + jnp.exp(total0) * one[PART:]


def parted(first, mine, theirs, total0, total1, start, end):
    carried0 = jnp.where(first, mine[:PART], theirs[:PART])
    pulled1 = jnp.where(first, theirs[PART:], mine[PART:])
    start1 = jnp.exp(total0) * start + carried0
    end0 = jnp.exp(total1) * end + pulled1
    own = jnp.where(first, start, start1), jnp.where(first, end0, end)
    return own, (jnp.where(first, start1, start), jnp.where(first, end, end0))


def pack_chip_kernel(at_ref, mine_ref, got_ref, total_ref, keep_ref, away_ref, chip_total_ref):
    core, y = at_ref[0], at_ref[1]
    heads = total_ref.shape[0]
    chip_total_ref[...] = total_ref[...] + got_ref[got_ref.shape[0] - 1, :heads]
    for place in range(PLANES):
        for ref, side_y in ((keep_ref, y), (away_ref, 1 - y)):
            total0, total1 = both_totals(core == 0, head_of(place, side_y, core), total_ref, got_ref)
            here = side_y * PLANES + place
            carried, pulled = joined(core == 0, mine_ref[here], got_ref[here], total0, total1)
            ref[place, :PART] = carried
            ref[place, PART:] = pulled
    away_ref[PLANES, :heads] = chip_total_ref[...]
    away_ref[PLANES, heads:] = jnp.zeros_like(away_ref[PLANES, heads:])


def pack_kernel(at_ref, keep_ref, got_ref, total_ref, start_ref, out_ref):
    core, y = at_ref[0], at_ref[1]
    for place in range(PLANES):
        total0, total1 = both_totals(y == 0, head_of(place, y, core), total_ref, got_ref)
        carried, pulled = joined(y == 0, keep_ref[place], got_ref[place], total0, total1)
        out_ref[place, :PART] = carried
        out_ref[place, PART:STATES] = pulled
        out_ref[place, STATES:GRADS] = jnp.broadcast_to(total0 + total1, (8, N))
        out_ref[place, GRADS:] = start_ref[PART * place : PART * (place + 1)]


def scan_kernel(blocks_ref, starts_ref, out_ref):
    current = jnp.zeros((PART, N), F32)
    for place in range(PLANES):
        starts_ref[place] = current
        current = jnp.exp(blocks_ref[place, STATES : STATES + 1]) * current + blocks_ref[place, :PART]
    for group in range(out_ref.shape[0]):
        out_ref[group, :PART] = blocks_ref[group, GRADS:]
        out_ref[group, PART:] = current


def scan_back_kernel(blocks_ref, starts_ref, got_ref, out_ref):
    current = got_ref[0, :PART]
    for answer in range(1, got_ref.shape[0]):
        current = current + got_ref[answer, :PART]
    for place in range(PLANES - 1, -1, -1):
        out_ref[place, :PART] = starts_ref[place]
        out_ref[place, PART:STATES] = current
        out_ref[place, STATES:] = got_ref[place, PART:]
        current = jnp.exp(blocks_ref[place, STATES : STATES + 1]) * current + blocks_ref[place, PART:STATES]


def unpack_kernel(at_ref, keep_ref, got_ref, total_ref, states_ref, own_ref, other_ref):
    core, y = at_ref[0], at_ref[1]
    for place in range(PLANES):
        total0, total1 = both_totals(y == 0, head_of(place, y, core), total_ref, got_ref)
        own, other = parted(
            y == 0, keep_ref[place], got_ref[place], total0, total1,
            states_ref[place, :PART], states_ref[place, PART:STATES],
        )
        for ref, (start, end) in ((own_ref, own), (other_ref, other)):
            ref[place, :PART] = start
            ref[place, PART:] = end


def unpack_chip_kernel(at_ref, mine_ref, got_ref, total_ref, near_ref, away_ref, own_ref, other_ref):
    core, y = at_ref[0], at_ref[1]
    for place in range(PLANES):
        for chip_ref, side_y in ((near_ref, y), (away_ref, 1 - y)):
            total0, total1 = both_totals(core == 0, head_of(place, side_y, core), total_ref, got_ref)
            here = side_y * PLANES + place
            own, other = parted(
                core == 0, mine_ref[here], got_ref[here], total0, total1,
                chip_ref[place, :PART], chip_ref[place, PART:],
            )
            for ref, (start, end) in ((own_ref, own), (other_ref, other)):
                ref[here, :PART] = start
                ref[here, PART:] = end


def gather_kernel(parts_ref, key_ref, query_ref, sums_ref):
    for ref, first in ((key_ref, 0), (query_ref, PART)):
        for group in range(GROUPS):
            chip0, chip1 = parts_ref[2 * group], parts_ref[2 * group + 1]
            sums_ref[pl.ds(group, PART, stride=GROUPS), :] = (chip0 + chip1)[first : first + PART]
        ref[...] = sums_ref[...].astype(BF16)


def chunk_grads(inputs, cot, logs3, keys, queries, start, end):
    sums, mid, last = logs3
    grow = rows(jnp.exp(mid - sums))
    fall = rows(jnp.exp(sums - mid))
    in_high, in_low = split(inputs * grow)
    cot_high, cot_low = split(cot * fall)
    end_high, end_low = split(rows(jnp.exp(last - mid)) * end)
    start_high, start_low = split(rows(jnp.exp(mid)) * start)
    first = lax.broadcasted_iota(jnp.int32, (T, T), 0)
    second = lax.broadcasted_iota(jnp.int32, (T, T), 1)
    score_high, score_low = split(jnp.where(first >= second, dot_nt(queries, keys), 0.0))
    input_grad = dot(side(cot_high, cot_low), twice(score_high)) + dot(cot_high, score_low)
    input_grad = input_grad + dot_nt(side(end_high, end_low), side(keys, keys))
    input_grad = grow * input_grad
    in_high_t, in_low_t = in_high.T, in_low.T
    right_high, right_low = side(cot_high, end_high), side(cot_low, end_low)
    both = dot(in_high_t, right_high) + (dot(in_high_t, right_low) + dot(in_low_t, right_high))
    products = jnp.where(second >= first, both[:, :T], 0.0)
    high, low = split(products)
    key_grad = both[:, T:] + dot(side(high, low), twice(queries))
    high, low = split(products.T)
    query_grad = dot(side(high, low), twice(keys))
    cot_high_t, cot_low_t = cot_high.T, cot_low.T
    query_grad = query_grad + dot(cot_high_t, start_high)
    query_grad = query_grad + (dot(cot_high_t, start_low) + dot(cot_low_t, start_high))
    return input_grad, key_grad, query_grad, (in_high, in_low)


def by_core(number, core, value, mine_ref, peer_ref):
    value = value.reshape(2, 2, PART, N)
    here = pl.ds(2 * number, 2)
    mine_ref[here] = jnp.where(core == 0, value[:, 0], value[:, 1])
    peer_ref[here] = jnp.where(core == 0, value[:, 1], value[:, 0])


def answer_kernel(
    length_ref, core_ref, input_hbm, cot_hbm, logs_hbm, key_hbm, query_hbm, ends_hbm,
    input_grad_hbm, query_grad_hbm, key_mine_ref, key_peer_ref,
    input_ref, cot_ref, logs_ref, key_ref, query_ref, ends_ref, input_grad_ref, query_grad_ref, state_ref, sems,
):
    chunks, width = ends_ref.shape[0], ends_ref.shape[1]
    order = range(chunks)
    pairs = [
        (logs_hbm, logs_ref), (key_hbm, key_ref), (query_hbm, query_ref), (input_hbm, input_ref), (cot_hbm, cot_ref)
    ]
    copies = start_copies(pairs + chunk_pairs(ends_hbm, ends_ref, order), sems)
    wait_all(copies[:5])
    state_ref[...] = jnp.zeros_like(state_ref)
    sent = []
    for n in order:
        logs3 = chunk_logs(logs_ref, n)
        sums, mid, last = logs3
        copies[5 + n].wait()
        cot = jnp.where(live_mask(n, length_ref[0], width), lanes_of(cot_ref, n).astype(F32), 0.0)
        keys, queries = tokens_of(key_ref, n), tokens_of(query_ref, n)
        start = state_ref[...]
        input_grad, key_grad, query_grad, (high, low) = chunk_grads(
            lanes_of(input_ref, n).astype(F32), cot, logs3, keys, queries, start, ends_ref[n]
        )
        input_grad_ref[n] = input_grad.astype(BF16)
        by_core(n, core_ref[0], key_grad, key_mine_ref, key_peer_ref)
        query_grad_ref[n * T : (n + 1) * T, :] = query_grad
        pairs = [
            (input_grad_ref.at[n], lanes_at(input_grad_hbm, n)),
            (tokens_at(query_grad_ref, n), tokens_at(query_grad_hbm, n)),
        ]
        sent += start_copies(pairs, sems, len(copies) + 2 * n)
        carried = dot(side(high, low), twice(keys))
        state_ref[...] = rows(jnp.exp(last)) * start + rows(jnp.exp(last - mid)) * carried
    wait_all(sent)


def prompt_near_kernel(
    input_hbm, cot_hbm, logs_hbm, key_hbm, query_hbm, input_grad_hbm, key_grad_hbm, query_grad_hbm,
    input_ref, cot_ref, logs_ref, key_ref, query_ref, input_grad_ref, key_grad_ref, query_grad_ref, sems,
):
    first = lax.broadcasted_iota(jnp.int32, (T, T), 0)
    second = lax.broadcasted_iota(jnp.int32, (T, T), 1)
    order = range(input_ref.shape[1] // T)
    pairs = [
        (logs_hbm, logs_ref), (key_hbm, key_ref), (query_hbm, query_ref), (input_hbm, input_ref), (cot_hbm, cot_ref)
    ]
    copies = start_copies(pairs, sems)
    wait_all(copies)
    sent = []
    for n in order:
        here = slice(n * T, (n + 1) * T)
        sums, mid, _ = chunk_logs(logs_ref, n)
        keys, queries = tokens_of(key_ref, n), tokens_of(query_ref, n)
        grow = rows(jnp.exp(mid - sums))
        in_high, in_low = split(lanes_of(input_ref, n).astype(F32) * grow)
        cot_high, cot_low = split(lanes_of(cot_ref, n).astype(F32) * rows(jnp.exp(sums - mid)))
        score_high, score_low = split(jnp.where(first >= second, dot_nt(queries, keys), 0.0))
        input_grad = dot(side(cot_high, cot_low), twice(score_high)) + dot(cot_high, score_low)
        input_grad_ref[n] = grow * input_grad
        in_high_t, in_low_t = in_high.T, in_low.T
        both = dot(in_high_t, side(cot_high, cot_low))
        products = both[:, :T] + (both[:, T:] + dot(in_low_t, cot_high))
        products = jnp.where(second >= first, products, 0.0)
        high, low = split(products)
        key_grad_ref[here, :] = dot(side(high, low), twice(queries))
        high, low = split(products.T)
        query_grad_ref[here, :] = dot(side(high, low), twice(keys))
        pairs = [
            (input_grad_ref.at[n], input_grad_hbm.at[n]),
            (tokens_at(key_grad_ref, n), tokens_at(key_grad_hbm, n)),
            (tokens_at(query_grad_ref, n), tokens_at(query_grad_hbm, n)),
        ]
        sent += start_copies(pairs, sems, len(copies) + 3 * n)
    wait_all(sent)


def prompt_far_kernel(
    core_ref, input_hbm, cot_hbm, logs_hbm, key_hbm, carried_hbm, pulled_hbm,
    near_input_hbm, near_key_hbm, near_query_hbm, own_hbm, got_hbm,
    input_grad_hbm, key_grad_hbm, query_grad_hbm,
    input_ref, cot_ref, logs_ref, key_ref, carried_ref, pulled_ref, near_input_ref, near_key_ref, near_query_ref,
    own_ref, got_ref, input_grad_ref, key_grad_ref, query_grad_ref, end_ref, start_ref, sems,
):
    chunks = carried_ref.shape[0]
    core = core_ref[0]
    order = range(chunks)
    pairs = [
        (own_hbm, own_ref), (got_hbm, got_ref), (logs_hbm, logs_ref), (key_hbm, key_ref), (input_hbm, input_ref),
        (cot_hbm, cot_ref), (near_key_hbm, near_key_ref), (near_query_hbm, near_query_ref),
    ]
    first = len(pairs)
    for three in zip(
        chunk_pairs(near_input_hbm, near_input_ref, order[::-1]), chunk_pairs(pulled_hbm, pulled_ref, order[::-1]),
        chunk_pairs(carried_hbm, carried_ref, order),
    ):
        pairs += three
    copies = start_copies(pairs, sems)
    wait_all(copies[:2])
    for place in range(own_ref.shape[0]):
        for ref, side_core in ((own_ref, core), (got_ref, 1 - core)):
            here = pl.ds(half_rows(place, side_core), PART)
            start_ref[here, :] = ref[place, :PART]
            end_ref[here, :] = ref[place, PART:]
    wait_all(copies[2:first])
    sent = []
    for step in range(chunks):
        wait_all(copies[first + 3 * step : first + 3 * step + 3])
        n = chunks - 1 - step
        here = slice(n * T, (n + 1) * T)
        sums, mid, last = chunk_logs(logs_ref, n)
        end = end_ref[...]
        end_ref[...] = rows(jnp.exp(last)) * end + pulled_ref[n]
        keys = tokens_of(key_ref, n)
        grow = rows(jnp.exp(mid - sums))
        in_high, in_low = split(lanes_of(input_ref, n).astype(F32) * grow)
        end_high, end_low = split(rows(jnp.exp(last - mid)) * end)
        input_grad = dot_nt(side(end_high, end_low), side(keys, keys))
        input_grad_ref[n] = (near_input_ref[n] + grow * input_grad).astype(BF16)
        pairs = [(input_grad_ref.at[n], lanes_at(input_grad_hbm, n))]
        sent += start_copies(pairs, sems, len(copies) + 3 * step)
        in_high_t, in_low_t = in_high.T, in_low.T
        both = dot(in_high_t, side(end_high, end_low))
        key_grad = both[:, :N] + (both[:, N:] + dot(in_low_t, end_high))
        key_grad_ref[here, :] = (near_key_ref[here, :] + key_grad).astype(BF16)
        pairs = [(tokens_at(key_grad_ref, n), tokens_at(key_grad_hbm, n))]
        sent += start_copies(pairs, sems, len(copies) + 3 * step + 1)

        n = step
        here = slice(n * T, (n + 1) * T)
        sums, mid, last = chunk_logs(logs_ref, n)
        start = start_ref[...]
        start_ref[...] = rows(jnp.exp(last)) * start + carried_ref[n]
        cot_high, cot_low = split(lanes_of(cot_ref, n).astype(F32) * rows(jnp.exp(sums - mid)))
        start_high, start_low = split(rows(jnp.exp(mid)) * start)
        cot_high_t, cot_low_t = cot_high.T, cot_low.T
        both = dot(cot_high_t, side(start_high, start_low))
        query_grad = both[:, :N] + (both[:, N:] + dot(cot_low_t, start_high))
        query_grad_ref[here, :] = (near_query_ref[here, :] + query_grad).astype(BF16)
        pairs = [(tokens_at(query_grad_ref, n), tokens_at(query_grad_hbm, n))]
        sent += start_copies(pairs, sems, len(copies) + 3 * step + 2)
    wait_all(sent)


def start_part_kernel(length_ref, core_ref, cot_ref, logs_ref, local_ref, state_ref, mine_ref, peer_ref):
    width = cot_ref.shape[0]
    state = jnp.concatenate([state_ref[place, STATES:] for place in range(state_ref.shape[0])], axis=0)
    state_high, state_low = split(state)
    total = jnp.zeros((logs_ref.shape[0], T), F32)
    for n in range(cot_ref.shape[1] // T):
        sums, _, last = chunk_logs(logs_ref, n)
        scaled = lanes_of(cot_ref, n).astype(F32) * rows(jnp.exp(total + sums))
        scaled = jnp.where(live_mask(n, length_ref[0], width), scaled, 0.0)
        high, low = split(scaled)
        high, low = high.T, low.T
        both = dot(high, side(state_high, state_low))
        part = both[:, :N] + (both[:, N:] + dot(low, state_high))
        by_core(n, core_ref[0], tokens_of(local_ref, n) + part, mine_ref, peer_ref)
        total = total + last


def tail_kernel(key_ref, query_mine_ref, query_got_ref, out_ref):
    out_ref[:, :PART] = key_ref[...]
    out_ref[:, PART:] = query_mine_ref[...] + query_got_ref[...]


def shape(*dims, dtype=F32):
    return jax.ShapeDtypeStruct(dims, dtype)


IN_HBM = pl.BlockSpec(memory_space=pltpu.HBM)
IN_VMEM = pl.BlockSpec(memory_space=pltpu.VMEM)


def held(*dims, dtype=F32):
    return pltpu.VMEM(dims, dtype)


def loading(kernel, scalars, far, outs):
    def run(*refs):
        first, sources, rest = refs[:scalars], refs[scalars : scalars + far], refs[scalars + far :]
        *rest, sems = rest
        targets, rest = rest[len(rest) - far :], rest[: len(rest) - far]
        wait_all(start_copies(list(zip(sources, targets)), sems))
        kernel(*first, *targets, *rest)

    return run


def call(kernel, outs, scratch=(), copies=0, scalars=0, far=0, count=0, far_outs=0, flops=0, name=None):
    def run(*args):
        sems, extra, inner = copies, [], kernel
        if far and not copies:
            sources = args[scalars : scalars + far]
            extra = [pltpu.VMEM(source.shape, source.dtype) for source in sources]
            sems, inner = far, loading(kernel, scalars, far, outs)
        return pl.pallas_call(
            inner,
            out_shape=outs,
            in_specs=[pl.BlockSpec(memory_space=pltpu.SMEM)] * scalars + [IN_HBM] * far + [IN_VMEM] * count,
            out_specs=[IN_HBM] * far_outs + [IN_VMEM] * (len(outs) - far_outs),
            scratch_shapes=list(scratch) + extra + ([pltpu.SemaphoreType.DMA((sems,))] if sems else []),
            compiler_params=pltpu.CompilerParams(vmem_limit_bytes=LARGE if sems else SMALL),
            cost_estimate=pl.CostEstimate(flops=flops, bytes_accessed=2000000, transcendentals=0),
            name=name,
        )(*args)

    return run


def body(
    prompt_inputs, prompt_keys, prompt_queries, prompt_logdecay, prompt_cotangent,
    answer_inputs, answer_keys, answer_queries, answer_logdecay, answer_cotangent, answer_lengths,
):
    tokens, heads, _ = prompt_inputs.shape
    _, length, answer_heads, _ = answer_inputs.shape
    width, answer_width = heads * HEAD, answer_heads * HEAD
    chunks, answer_chunks = tokens // T, length // T
    seq, comp = lax.axis_size("seq"), lax.axis_size("comp")
    quads = heads // answer_heads
    planes = seq // quads
    chips = seq // 2
    same_core = [[2 * chip + side for chip in range(chips)] for side in range(2)]
    same_pair = [[quads * plane + q for plane in range(planes)] for q in range(quads)]
    place = lax.axis_index("seq").astype(jnp.int32)
    group = (place // quads).reshape(1)
    core, y = place % 2, place // 2 % 2
    at = jnp.stack([core, y])
    core = core.reshape(1)

    def swap_cores(value):
        return lax.ppermute(value, "seq", [(i, i ^ 1) for i in range(seq)])

    def swap_chips(value):
        return lax.ppermute(value, "seq", [(i, i ^ 2) for i in range(seq)])

    def over(value, axis, groups=None):
        return lax.all_to_all(value, axis, 0, 0, axis_index_groups=groups, tiled=True)

    x = jnp.transpose(prompt_inputs, (1, 2, 0)).reshape(width, tokens)
    cot = jnp.transpose(prompt_cotangent, (1, 2, 0)).reshape(width, tokens)
    logs = prompt_logdecay.T
    keys, queries = prompt_keys.reshape(tokens, N), prompt_queries.reshape(tokens, N)
    ax = jnp.transpose(answer_inputs[0], (1, 2, 0)).reshape(answer_width, length)
    acot = jnp.transpose(answer_cotangent[0], (1, 2, 0)).reshape(answer_width, length)
    alogs = answer_logdecay[0].T
    all_keys, all_queries = answer_keys.reshape(length * GROUPS, N), answer_queries.reshape(length * GROUPS, N)

    prompt_lanes, prompt_rows = held(width, tokens, dtype=BF16), held(tokens, N, dtype=BF16)
    prompt_states = held(chunks, width, N)
    prompt_scratch = [prompt_lanes, prompt_lanes, held(heads, tokens), prompt_rows, prompt_rows]
    carried, pulled, mine, peer, totals = call(
        summary_kernel,
        [
            shape(chunks, width, N), shape(chunks, width, N), shape(chips, 2 * PART, N),
            shape(chips + 1, 2 * PART, N), shape(heads, N),
        ],
        scratch=prompt_scratch + [prompt_states, prompt_states, held(width, N), held(width, N)],
        copies=5 + 2 * chunks, scalars=1, far=5, far_outs=2, flops=10**9, name="prompt_summary",
    )(core, x, cot, logs, keys, queries)
    theirs = swap_cores(peer)

    answer_lanes, answer_rows = held(answer_width, length, dtype=BF16), held(length, N, dtype=BF16)
    answer_logs, answer_states = held(answer_heads, length), held(answer_chunks, answer_width, N)
    raw, raw_chunk = held(answer_chunks, T * GROUPS, N, dtype=BF16), held(2, T * GROUPS, N)
    ends, akeys, aqueries, start_grad = call(
        ends_kernel,
        [
            shape(answer_chunks, answer_width, N), shape(length, N, dtype=BF16), shape(length, N, dtype=BF16),
            shape(answer_width, N),
        ],
        scratch=[answer_lanes, answer_logs, answer_states, answer_rows, answer_rows, raw, raw, raw_chunk, raw_chunk],
        copies=4 + 3 * answer_chunks, scalars=2, far=4, far_outs=3, flops=10**9, name="answer_ends",
    )(answer_lengths, group, acot, alogs, all_keys, all_queries)
    half = shape(planes, 2 * PART, N)
    half_more = shape(planes + 1, 2 * PART, N)
    keep, away, chip_totals = call(
        pack_chip_kernel, [half, half_more, shape(heads, N)], scalars=1, count=3, flops=10**7, name="pack_chip"
    )(at, mine, theirs, totals)
    chip_theirs = swap_chips(away)
    (sent,) = call(
        pack_kernel, [shape(planes, GRADS + PART, N)], scalars=1, count=4, flops=10**7, name="pack"
    )(at, keep, chip_theirs, chip_totals, start_grad)
    blocks = over(sent, "seq", same_pair)

    near_input, near_key, near_query = call(
        prompt_near_kernel, [shape(chunks, width, T), shape(tokens, N), shape(tokens, N)],
        scratch=prompt_scratch + [held(chunks, width, T), held(tokens, N), held(tokens, N)],
        copies=5 + 3 * chunks, far=5, far_outs=3, flops=3 * 10**9, name="prompt_near",
    )(x, cot, logs, keys, queries)
    ax_grad, aq_local, key_mine, key_peer = call(
        answer_kernel,
        [
            shape(answer_width, length, dtype=BF16), shape(length, N),
            shape(chips, PART, N), shape(chips, PART, N),
        ],
        scratch=[
            answer_lanes, answer_lanes, answer_logs, answer_rows, answer_rows, answer_states,
            held(answer_chunks, answer_width, T, dtype=BF16), held(length, N), held(answer_width, N),
        ],
        copies=5 + 3 * answer_chunks, scalars=2, far=6, far_outs=2, flops=3 * 10**9, name="answer_grads",
    )(answer_lengths, core, ax, acot, alogs, akeys, aqueries, ends)

    starts, sent = call(
        scan_kernel, [shape(planes, PART, N), shape(comp, 2 * PART, N)], count=1, flops=10**7, name="scan"
    )(blocks)
    sent, ax_grad, aq_local, key_mine, key_peer = lax.optimization_barrier(
        (sent, ax_grad, aq_local, key_mine, key_peer)
    )
    finals = over(sent, "comp")
    key_parts = key_mine + swap_cores(key_peer)
    finals, near_input, near_key, near_query = lax.optimization_barrier((finals, near_input, near_key, near_query))
    (sent,) = call(
        scan_back_kernel, [shape(planes, 3 * PART, N)], count=3, flops=10**7, name="scan_back"
    )(blocks, starts, finals)
    states = over(sent, "seq", same_pair)
    chip_own, chip_other = call(
        unpack_kernel, [half, half], scalars=1, count=4, flops=10**7, name="unpack"
    )(at, keep, chip_theirs, chip_totals, states)
    chip_got = swap_chips(chip_other)

    query_mine, query_peer = call(
        start_part_kernel, [shape(chips, PART, N), shape(chips, PART, N)],
        scalars=2, far=3, count=1, flops=10**9, name="answer_start_part",
    )(answer_lengths, core, acot, alogs, aq_local, states)
    (sent,) = call(tail_kernel, [shape(chips, 2 * PART, N)], count=3, flops=10**7, name="pack_tail")(
        key_parts, query_mine, swap_cores(query_peer)
    )
    parts = over(sent, "seq", same_core)
    own, other = call(
        unpack_chip_kernel, [shape(chips, 2 * PART, N), shape(chips, 2 * PART, N)],
        scalars=1, count=5, flops=10**7, name="unpack_chip",
    )(at, mine, theirs, totals, chip_own, chip_got)
    x_grad, k_grad, q_grad = call(
        prompt_far_kernel,
        [shape(width, tokens, dtype=BF16), shape(tokens, N, dtype=BF16), shape(tokens, N, dtype=BF16)],
        scratch=[
            prompt_lanes, prompt_lanes, held(heads, tokens), prompt_rows, prompt_states, prompt_states,
            held(chunks, width, T), held(tokens, N), held(tokens, N),
            held(chips, 2 * PART, N), held(chips, 2 * PART, N),
            held(chunks, width, T, dtype=BF16), prompt_rows, prompt_rows, held(width, N), held(width, N),
        ],
        copies=8 + 6 * chunks, scalars=1, far=11, far_outs=3, flops=3 * 10**9, name="prompt_far",
    )(
        core, x, cot, logs, keys, carried, pulled, near_input, near_key, near_query, own, swap_cores(other),
    )

    gathered = shape(PART * GROUPS, N, dtype=BF16)
    key_out, query_out = call(
        gather_kernel, [gathered, gathered], scratch=[held(PART * GROUPS, N)],
        count=1, flops=10**7, name="gather_groups",
    )(parts)

    return (
        jnp.transpose(x_grad.reshape(heads, HEAD, tokens), (2, 0, 1)),
        k_grad.reshape(tokens, 1, N),
        q_grad.reshape(tokens, 1, N),
        jnp.transpose(ax_grad.reshape(answer_heads, HEAD, length), (2, 0, 1))[None],
        key_out.reshape(1, PART, GROUPS, N),
        query_out.reshape(1, PART, GROUPS, N),
    )


def solution(mesh):
    in_specs = (
        P("seq", "comp", None),
        P("seq", "comp", None),
        P("seq", "comp", None),
        P("seq", "comp"),
        P("seq", "comp", None),
        P("comp", None, "seq", None),
        P("comp", None, None, None),
        P("comp", None, None, None),
        P("comp", None, "seq"),
        P("comp", None, "seq", None),
        P("comp"),
    )
    out_specs = (
        P("seq", "comp", None),
        P("seq", "comp", None),
        P("seq", "comp", None),
        P("comp", None, "seq", None),
        P("comp", "seq", None, None),
        P("comp", "seq", None, None),
    )
    return jax.shard_map(body, mesh=mesh, in_specs=in_specs, out_specs=out_specs, check_vma=False)
```

time: 182 us -> 111 us (0.61); the launches traced: 179 us -> 111 us
  waiting for transfers between devices: 83.4 us -> 28.1 us
  blocking collectives: 19.7 us -> 0 us
  Pallas kernels: 29.1 us -> 48.4 us
  local copies, waits for them, and re-layouts: 13.2 us -> 7.01 us
  other arithmetic: 5.32 us -> 0.11 us
    ppermute x2 -> x6, waiting for transfers between devices: 40.8 us -> 6.62 us  [the longest x4 3.96 us: swap_cores(): return lax.ppermute(value, 'seq', [(i, i ^ 1) for i in range(seq)])]
    all_to_all x3 -> x4, waiting for transfers between devices: 42.6 us -> 21.5 us  [over(): lax.all_to_all(value, axis, 0, 0, axis_index_groups=groups, tiled=True)]
    all_to_all x1 -> x0, blocking collectives: 19.7 us -> none  [body(): lax.all_to_all(jnp.broadcast_to(final[None], (comp, part, N)), 'comp', 0,...]
    pallas_call x6 -> x14, Pallas kernels: 29.1 us -> 48.4 us  [run(): pl.pallas_call(inner, out_shape=outs, in_specs=[pl.BlockSpec(memory_space...]
    dynamic_slice x1 -> x0, local copies, waits for them, and re-layouts: 4.1 us -> none  [body(): lax.dynamic_slice_in_dim(answer_queries[0], group, 1, 1).reshape(length, N)]
    reduce_sum x3 -> x0, other arithmetic: 2.71 us -> none  [the longest x1 1.52 us: body(): final_grad = lax.ppermute(jnp.sum(parts, axis=0), ('seq', 'comp'), swap)]
    concatenate x2 -> x0, other arithmetic: 2.61 us -> none  [the longest x1 1.32 us: body(): jnp.concatenate([by_owner(all_carried), by_owner(all_pulled), slice_total...]
    ppermute x2 -> x6, starting transfers between devices: 5.12 us -> 2.68 us  [the longest x2 2.4 us: swap_chips(): return lax.ppermute(value, 'seq', [(i, i ^ 2) for i in range(seq)])]
  transfers between devices with their start and end apart: 5 -> 10, of which waited for: 4 -> 8; matrix products, arithmetic and copies ran while one was open for 3% -> 0% of each run, Pallas kernels for 6% -> 34%
where the time goes in v2:
time: 111 us
  Pallas kernels  48.4 us (44%)
  waiting for transfers between devices  28.1 us (25%)
  starting transfers between devices  25.4 us (23%)
  local copies, waits for them, and re-layouts  7.01 us (6%)
  between operations  1.51 us (1%)
    pallas_call x14, Pallas kernels, run(): pl.pallas_call(inner, out_shape=outs, in_specs=[pl.BlockSpec(memory_space...  48.4 us
    all_to_all x4, starting transfers between devices, over(): lax.all_to_all(value, axis, 0, 0, axis_index_groups=groups, tiled=True)  22.8 us
    all_to_all x4, waiting for transfers between devices, over(): lax.all_to_all(value, axis, 0, 0, axis_index_groups=groups, tiled=True)  21.5 us
    unnamed x24, local copies, waits for them, and re-layouts  7.01 us
    ppermute x4, waiting for transfers between devices, swap_cores(): return lax.ppermute(value, 'seq', [(i, i ^ 1) for i in range(seq)])  3.96 us
    ppermute x2, waiting for transfers between devices, swap_chips(): return lax.ppermute(value, 'seq', [(i, i ^ 2) for i in range(seq)])  2.66 us
    ppermute x2, starting transfers between devices, swap_chips(): return lax.ppermute(value, 'seq', [(i, i ^ 2) for i in range(seq)])  2.4 us
  transfers between devices with their start and end apart: 10, of which 8 were waited for; matrix products, arithmetic and copies ran while one was open for 0% of the time, Pallas kernels for 34%

profile of v2, /device:TPU:16, one launch (start us, length us, event | category | flops | bytes accessed | tf_op | source)
XLA Modules:
  0.0 110.6 jit_solution(566743251445016368)
XLA Ops:
  0.6 6.1 %prompt_summary.1 = (f32[4,1024,128]{2,1,0:T(8,128)}, f32[4,1024,128]{2,1,0:T(8,128)}, f32[16,64,128]{2,1,0:T(8,128)}, f32[17,64,128]{2,1,0:T(8,128)}, f32[16,128]{1,0:T(8,128)}) custom-call(s32[1]{0:T(128)} %bitcast.core_ref.refs_1_, bf16[1024,512]{1,0:T(8,128)(2,1)} %bitcast.47, bf16[1024,512]{1,0:T(8,128)(2,1)} %bitcast.50, f32[16,512]{1,0:T(8,128)} %bitcast.61, ...), custom_call_target="tpu_custom_call" | custom-call | flops 1000000000 | bytes 2000000 | tf_op jit(solution)/shard_map/prompt_summary/pallas_call | solution.py:538
  6.8 0.1 collective-permute-start
  6.9 0.1 pad_add_fusion.at_ref
  7.0 2.0 %collective-permute-done.got_ref = f32[17,64,128]{2,1,0:T(8,128)S(1)} collective-permute-done((f32[17,64,128]{2,1,0:T(8,128)}, f32[17,64,128]{2,1,0:T(8,128)S(1)}, u32[]{:S(2)}, u32[]{:S(2)}) %collective-permute-start) | collective-permute-done | bytes 557088 | tf_op jit(solution)/shard_map/ppermute | solution.py:573
  9.1 1.0 copy-done
  10.1 0.7 copy-done.6
  10.8 0.6 pack_chip.1
  11.4 1.4 %collective-permute-start.1 = (f32[9,64,128]{2,1,0:T(8,128)S(1)}, f32[9,64,128]{2,1,0:T(8,128)S(1)}, u32[]{:S(2)}, u32[]{:S(2)}) collective-permute-start(f32[9,64,128]{2,1,0:T(8,128)S(1)} %get-tuple-element.53), channel_id=1, source_target_pairs={{0,16},{8,24},{16,0},{24,8},{32,48},{40,56},{48,32},{56,40},{64,80... | collective-permute-start | bytes 884744 | tf_op jit(solution)/shard_map/ppermute | solution.py:576
  13.5 6.8 %answer_ends.1 = (f32[8,256,128]{2,1,0:T(8,128)}, bf16[1024,128]{1,0:T(8,128)(2,1)}, bf16[1024,128]{1,0:T(8,128)(2,1)}, f32[256,128]{1,0:T(8,128)}) custom-call(s32[1]{0:T(128)S(6)} %copy.17.length_ref.refs_0_, s32[1]{0:T(128)} %bitcast.11.group_ref, bf16[256,1024]{1,0:T(8,128)(2,1)} %bitcast.41, f32[4,1024]{1,0:T(4,128)} %bitcast.44, ...), custom_call_target="tpu_custom_call" | custom-call | flops 1000000000 | bytes 2000000 | tf_op jit(solution)/shard_map/answer_ends/pallas_call | solution.py:538
  20.2 0.4 collective-permute-done.1.got_ref
  20.6 0.9 copy-done.5
  21.5 1.4 %pack.1 = f32[8,104,128]{2,1,0:T(8,128)} custom-call(s32[2]{0:T(128)S(1)} %pad_add_fusion.at_ref, f32[8,64,128]{2,1,0:T(8,128)S(1)} %get-tuple-element.52.keep_ref, f32[9,64,128]{2,1,0:T(8,128)S(1)} %collective-permute-done.1.got_ref, f32[16,128]{1,0:T(8,128)S(1)} %get-tuple-element.54.total_ref, f32[256,128]{1,0:T(8,128)S(1)} %copy-done.5), custom_call_target="tpu_custom_call" | custom-call | flops 10000000 | bytes 2000000 | tf_op jit(solution)/shard_map/pack/pallas_call | solution.py:538
  22.9 8.5 %all-to-all-start = ((f32[8,104,128]{2,1,0:T(8,128)}), f32[8,104,128]{2,1,0:T(8,128)S(1)}, u32[]{:S(2)}, u32[]{:S(2)}) async-start(f32[8,104,128]{2,1,0:T(8,128)} %pack.1), calls=%async_computation | async-start | bytes 851968 | tf_op jit(solution)/shard_map/all_to_all | solution.py:579
  31.4 9.7 %answer_grads.1 = (bf16[256,1024]{1,0:T(8,128)(2,1)}, f32[1024,128]{1,0:T(8,128)}, f32[16,32,128]{2,1,0:T(8,128)}, f32[16,32,128]{2,1,0:T(8,128)}) custom-call(s32[1]{0:T(128)S(6)} %copy.17.length_ref.refs_0_, s32[1]{0:T(128)} %bitcast.core_ref.refs_1_, bf16[256,1024]{1,0:T(8,128)(2,1)} %bitcast.53, bf16[256,1024]{1,0:T(8,128)(2,1)} %bitcast.42, ...), custom_call_target="tpu_custom_call" | custom-call | flops 3000000000 | bytes 2000000 | tf_op jit(solution)/shard_map/answer_grads/pallas_call | solution.py:538
  41.1 5.3 %all-to-all-done.blocks_ref = f32[8,104,128]{2,1,0:T(8,128)S(1)} async-done(((f32[8,104,128]{2,1,0:T(8,128)}), f32[8,104,128]{2,1,0:T(8,128)S(1)}, u32[]{:S(2)}, u32[]{:S(2)}) %all-to-all-start) | async-done | bytes 426016 | tf_op jit(solution)/shard_map/all_to_all | solution.py:579
  46.4 0.7 scan.1
  47.2 7.3 %all-to-all-start.1 = ((f32[8,64,128]{2,1,0:T(8,128)}), f32[8,64,128]{2,1,0:T(8,128)S(1)}, u32[]{:S(2)}, u32[]{:S(2)}) async-start(f32[8,64,128]{2,1,0:T(8,128)} %get-tuple-element.64), calls=%async_computation.1 | async-start | bytes 524288 | tf_op jit(solution)/shard_map/all_to_all | solution.py:579
  54.4 5.7 %prompt_near.1 = (f32[4,1024,128]{2,1,0:T(8,128)}, f32[512,128]{1,0:T(8,128)}, f32[512,128]{1,0:T(8,128)}) custom-call(bf16[1024,512]{1,0:T(8,128)(2,1)} %bitcast.48, bf16[1024,512]{1,0:T(8,128)(2,1)} %bitcast.51, f32[16,512]{1,0:T(8,128)} %bitcast.62, bf16[512,128]{1,0:T(8,128)(2,1)} %bitcast.57, bf16[512,128]{1,0:T(8,128)(2,1)} %bitcast.55), custom_call_target="tpu_custom_call" | custom-call | flops 3000000000 | bytes 2000000 | tf_op jit(solution)/shard_map/prompt_near/pallas_call | solution.py:538
  60.1 0.4 all-to-all-done.1.got_ref
  60.5 0.8 scan_back.1
  61.3 3.5 %all-to-all-start.2 = ((f32[8,96,128]{2,1,0:T(8,128)}), f32[8,96,128]{2,1,0:T(8,128)S(1)}, u32[]{:S(2)}, u32[]{:S(2)}) async-start(f32[8,96,128]{2,1,0:T(8,128)} %scan_back.1), calls=%async_computation.2 | async-start | bytes 786432 | tf_op jit(solution)/shard_map/all_to_all | solution.py:579
  64.8 0.0 copy-done.11
  64.8 0.0 copy-start.9
  64.8 0.1 collective-permute-start.4
  64.9 12.3 %all-to-all-done.2.states_ref.refs_5_ = f32[8,96,128]{2,1,0:T(8,128)S(1)} async-done(((f32[8,96,128]{2,1,0:T(8,128)}), f32[8,96,128]{2,1,0:T(8,128)S(1)}, u32[]{:S(2)}, u32[]{:S(2)}) %all-to-all-start.2) | async-done | bytes 393248 | tf_op jit(solution)/shard_map/all_to_all | solution.py:579
  77.2 0.7 copy-done.2
  77.9 5.3 %answer_start_part.1 = (f32[16,32,128]{2,1,0:T(8,128)}, f32[16,32,128]{2,1,0:T(8,128)}) custom-call(s32[1]{0:T(128)S(6)} %copy.17.length_ref.refs_0_, s32[1]{0:T(128)} %bitcast.core_ref.refs_1_, bf16[256,1024]{1,0:T(8,128)(2,1)} %bitcast.43, f32[4,1024]{1,0:T(4,128)} %bitcast.46, f32[1024,128]{1,0:T(8,128)} %get-tuple-element.83.refs_4_, f32[8,96,128]{2,1,0:T(8,128)} %copy-done.2), custom_call_target="tpu_custom_call" | custom-call | flops 1000000000 | bytes 2000000 | tf_op jit(solution)/shard_map/answer_start_part/pallas_call | solution.py:538
  83.2 0.0 copy-start.1
  83.2 0.1 collective-permute-start.5
  83.3 0.0 copy-start.3
  83.3 1.0 copy-done.3
  84.4 0.6 unpack.1
  85.0 1.0 collective-permute-start.2
  86.0 0.0 collective-permute-done.4
  86.1 0.0 collective-permute-done.5.query_got_ref
  86.1 0.9 copy-done.4
  87.0 0.8 pack_tail.1
  87.9 3.6 %all-to-all-start.3 = ((f32[16,64,128]{2,1,0:T(8,128)}), f32[16,64,128]{2,1,0:T(8,128)S(1)}, u32[]{:S(2)}, u32[]{:S(2)}) async-start(f32[16,64,128]{2,1,0:T(8,128)} %pack_tail.1), calls=%async_computation.3 | async-start | bytes 1048576 | tf_op jit(solution)/shard_map/all_to_all | solution.py:579
  91.4 2.3 %collective-permute-done.2.away_ref = f32[8,64,128]{2,1,0:T(8,128)S(1)} collective-permute-done((f32[8,64,128]{2,1,0:T(8,128)S(1)}, f32[8,64,128]{2,1,0:T(8,128)S(1)}, u32[]{:S(2)}, u32[]{:S(2)}) %collective-permute-start.2) | collective-permute-done | bytes 262176 | tf_op jit(solution)/shard_map/ppermute | solution.py:576
  93.8 0.7 unpack_chip.1
  94.5 0.0 copy-start.8
  94.5 0.8 copy-done.8
  95.3 0.0 collective-permute-start.3
  95.3 1.9 %collective-permute-done.3.got_hbm = f32[16,64,128]{2,1,0:T(8,128)S(1)} collective-permute-done((f32[16,64,128]{2,1,0:T(8,128)S(1)}, f32[16,64,128]{2,1,0:T(8,128)S(1)}, u32[]{:S(2)}, u32[]{:S(2)}) %collective-permute-start.3) | collective-permute-done | bytes 524320 | tf_op jit(solution)/shard_map/ppermute | solution.py:573
  97.2 0.8 copy-done.10
  98.0 8.4 %prompt_far.1 = (bf16[1024,512]{1,0:T(8,128)(2,1)}, bf16[512,128]{1,0:T(8,128)(2,1)}, bf16[512,128]{1,0:T(8,128)(2,1)}) custom-call(s32[1]{0:T(128)} %bitcast.core_ref.refs_1_, bf16[1024,512]{1,0:T(8,128)(2,1)} %bitcast.49, bf16[1024,512]{1,0:T(8,128)(2,1)} %bitcast.52, f32[16,512]{1,0:T(8,128)} %bitcast.63, bf16[512,128]{1,0:T(8,128)(2,1)} %bitcast.58, ...), custom_call_target="tpu_custom_call" | custom-call | flops 3000000000 | bytes 2000000 | tf_op jit(solution)/shard_map/prompt_far/pallas_call | solution.py:538
  106.4 3.5 %all-to-all-done.3.parts_ref = f32[16,64,128]{2,1,0:T(8,128)S(1)} async-done(((f32[16,64,128]{2,1,0:T(8,128)}), f32[16,64,128]{2,1,0:T(8,128)S(1)}, u32[]{:S(2)}, u32[]{:S(2)}) %all-to-all-start.3) | async-done | bytes 524320 | tf_op jit(solution)/shard_map/all_to_all | solution.py:579
  109.9 0.7 gather_groups.1
  (12 shorter events, 0.1 us)
Async XLA Ops:
  6.8 2.3 %collective-permute-start = (f32[17,64,128]{2,1,0:T(8,128)}, f32[17,64,128]{2,1,0:T(8,128)S(1)}, u32[]{:S(2)}, u32[]{:S(2)}) collective-permute-start(f32[17,64,128]{2,1,0:T(8,128)} %get-tuple-element.50), channel_id=1, source_target_pairs={{0,8},{8,0},{16,24},{24,16},{32,40},{40,32},{48,56},{56,48},{64,72... | collective-permute-start | bytes 1671176 | tf_op jit(solution)/shard_map/ppermute | solution.py:573
  9.1 1.0 copy-start
  10.1 0.7 copy-start.6
  11.4 9.1 %collective-permute-start.1 = (f32[9,64,128]{2,1,0:T(8,128)S(1)}, f32[9,64,128]{2,1,0:T(8,128)S(1)}, u32[]{:S(2)}, u32[]{:S(2)}) collective-permute-start(f32[9,64,128]{2,1,0:T(8,128)S(1)} %get-tuple-element.53), channel_id=1, source_target_pairs={{0,16},{8,24},{16,0},{24,8},{32,48},{40,56},{48,32},{56,40},{64,80... | collective-permute-start | bytes 884744 | tf_op jit(solution)/shard_map/ppermute | solution.py:576
  20.6 0.9 copy-start.5
  22.9 23.5 %all-to-all-start = ((f32[8,104,128]{2,1,0:T(8,128)}), f32[8,104,128]{2,1,0:T(8,128)S(1)}, u32[]{:S(2)}, u32[]{:S(2)}) async-start(f32[8,104,128]{2,1,0:T(8,128)} %pack.1), calls=%async_computation | async-start | bytes 851968 | tf_op jit(solution)/shard_map/all_to_all | solution.py:579
  47.2 13.4 %all-to-all-start.1 = ((f32[8,64,128]{2,1,0:T(8,128)}), f32[8,64,128]{2,1,0:T(8,128)S(1)}, u32[]{:S(2)}, u32[]{:S(2)}) async-start(f32[8,64,128]{2,1,0:T(8,128)} %get-tuple-element.64), calls=%async_computation.1 | async-start | bytes 524288 | tf_op jit(solution)/shard_map/all_to_all | solution.py:579
  54.4 10.4 %copy-start.11 = (f32[16,32,128]{2,1,0:T(8,128)S(1)}, f32[16,32,128]{2,1,0:T(8,128)}, u32[]{:S(2)}) copy-start(f32[16,32,128]{2,1,0:T(8,128)} %get-tuple-element.82) | copy-start | bytes 786436
  61.3 15.8 %all-to-all-start.2 = ((f32[8,96,128]{2,1,0:T(8,128)}), f32[8,96,128]{2,1,0:T(8,128)S(1)}, u32[]{:S(2)}, u32[]{:S(2)}) async-start(f32[8,96,128]{2,1,0:T(8,128)} %scan_back.1), calls=%async_computation.2 | async-start | bytes 786432 | tf_op jit(solution)/shard_map/all_to_all | solution.py:579
  64.8 21.2 %copy-start.9 = (f32[16,32,128]{2,1,0:T(8,128)S(1)}, f32[16,32,128]{2,1,0:T(8,128)}, u32[]{:S(2)}) copy-start(f32[16,32,128]{2,1,0:T(8,128)} %get-tuple-element.81) | copy-start | bytes 786436
  64.8 21.2 %collective-permute-start.4 = (f32[16,32,128]{2,1,0:T(8,128)S(1)}, f32[16,32,128]{2,1,0:T(8,128)S(1)}, u32[]{:S(2)}, u32[]{:S(2)}) collective-permute-start(f32[16,32,128]{2,1,0:T(8,128)S(1)} %copy-done.11), channel_id=1, source_target_pairs={{0,8},{8,0},{16,24},{24,16},{32,40},{40,32},{48,56},{56,48},{64,72... | collective-permute-start | bytes 786440 | tf_op jit(solution)/shard_map/ppermute | solution.py:573
  77.2 0.7 copy-start.2
  77.9 15.8 %copy-start.7 = (f32[16,128]{1,0:T(8,128)S(1)}, f32[16,128]{1,0:T(8,128)}, u32[]{:S(2)}) copy-start(f32[16,128]{1,0:T(8,128)} %get-tuple-element.51.total_ref) | copy-start | bytes 24580
  83.2 10.5 %copy-start.1 = (f32[16,64,128]{2,1,0:T(8,128)S(1)}, f32[16,64,128]{2,1,0:T(8,128)}, u32[]{:S(2)}) copy-start(f32[16,64,128]{2,1,0:T(8,128)} %get-tuple-element.49.mine_ref) | copy-start | bytes 1572868
  83.2 2.8 %collective-permute-start.5 = (f32[16,32,128]{2,1,0:T(8,128)}, f32[16,32,128]{2,1,0:T(8,128)S(1)}, u32[]{:S(2)}, u32[]{:S(2)}) collective-permute-start(f32[16,32,128]{2,1,0:T(8,128)} %get-tuple-element.85), channel_id=1, source_target_pairs={{0,8},{8,0},{16,24},{24,16},{32,40},{40,32},{48,56},{56,48},{64,72... | collective-permute-start | bytes 786440 | tf_op jit(solution)/shard_map/ppermute | solution.py:573
  83.3 1.0 copy-start.3
  85.0 8.7 %collective-permute-start.2 = (f32[8,64,128]{2,1,0:T(8,128)S(1)}, f32[8,64,128]{2,1,0:T(8,128)S(1)}, u32[]{:S(2)}, u32[]{:S(2)}) collective-permute-start(f32[8,64,128]{2,1,0:T(8,128)S(1)} %get-tuple-element.74), channel_id=1, source_target_pairs={{0,16},{8,24},{16,0},{24,8},{32,48},{40,56},{48,32},{56,40},{64,80... | collective-permute-start | bytes 786440 | tf_op jit(solution)/shard_map/ppermute | solution.py:576
  86.1 1.0 copy-start.4
  87.9 22.1 %all-to-all-start.3 = ((f32[16,64,128]{2,1,0:T(8,128)}), f32[16,64,128]{2,1,0:T(8,128)S(1)}, u32[]{:S(2)}, u32[]{:S(2)}) async-start(f32[16,64,128]{2,1,0:T(8,128)} %pack_tail.1), calls=%async_computation.3 | async-start | bytes 1048576 | tf_op jit(solution)/shard_map/all_to_all | solution.py:579
  94.5 0.8 copy-start.8
  95.3 1.9 %collective-permute-start.3 = (f32[16,64,128]{2,1,0:T(8,128)S(1)}, f32[16,64,128]{2,1,0:T(8,128)S(1)}, u32[]{:S(2)}, u32[]{:S(2)}) collective-permute-start(f32[16,64,128]{2,1,0:T(8,128)S(1)} %get-tuple-element.76), channel_id=1, source_target_pairs={{0,8},{8,0},{16,24},{24,16},{32,40},{40,32},{48,56},{56,48},{64,72... | collective-permute-start | bytes 1572872 | tf_op jit(solution)/shard_map/ppermute | solution.py:573
  97.2 0.8 copy-start.10

commit v3 on v2

--- a/solution.py
+++ b/solution.py
@@ -201,6 +201,7 @@
 
 STATES = 2 * PART
 GRADS = STATES + 8
+KEYS = STATES + PART
 
 
 def head_of(place, side_y, core):
@@ -257,18 +258,28 @@
         out_ref[group, PART:] = current
 
 
-def scan_back_kernel(blocks_ref, starts_ref, got_ref, out_ref):
+def key_chip_kernel(at_ref, mine_ref, got_ref, keep_ref, away_ref):
+    y = at_ref[1]
+    keep_ref[...] = mine_ref[pl.ds(y * PLANES, PLANES)] + got_ref[pl.ds(y * PLANES, PLANES)]
+    away_ref[...] = mine_ref[pl.ds((1 - y) * PLANES, PLANES)] + got_ref[pl.ds((1 - y) * PLANES, PLANES)]
+
+
+def scan_back_kernel(blocks_ref, starts_ref, got_ref, key_keep_ref, key_got_ref, out_ref):
     current = got_ref[0, :PART]
     for answer in range(1, got_ref.shape[0]):
         current = current + got_ref[answer, :PART]
     for place in range(PLANES - 1, -1, -1):
         out_ref[place, :PART] = starts_ref[place]
         out_ref[place, PART:STATES] = current
-        out_ref[place, STATES:] = got_ref[place, PART:]
+        out_ref[place, STATES:KEYS] = got_ref[place, PART:]
+        out_ref[place, KEYS:] = key_keep_ref[place] + key_got_ref[place]
         current = jnp.exp(blocks_ref[place, STATES : STATES + 1]) * current + blocks_ref[place, PART:STATES]
 
 
-def unpack_kernel(at_ref, keep_ref, got_ref, total_ref, states_ref, own_ref, other_ref):
+def unpack_kernel(at_ref, keep_ref, got_ref, total_ref, states_ref, own_ref, other_ref, key_ref, sums_ref):
+    for group in range(GROUPS):
+        sums_ref[pl.ds(group, PART, stride=GROUPS), :] = states_ref[group, KEYS:]
+    key_ref[...] = sums_ref[...].astype(BF16)
     core, y = at_ref[0], at_ref[1]
     for place in range(PLANES):
         total0, total1 = both_totals(y == 0, head_of(place, y, core), total_ref, got_ref)
@@ -296,12 +307,10 @@
                 ref[here, PART:] = end
 
 
-def gather_kernel(parts_ref, key_ref, query_ref, sums_ref):
-    for ref, first in ((key_ref, 0), (query_ref, PART)):
-        for group in range(GROUPS):
-            chip0, chip1 = parts_ref[2 * group], parts_ref[2 * group + 1]
-            sums_ref[pl.ds(group, PART, stride=GROUPS), :] = (chip0 + chip1)[first : first + PART]
-        ref[...] = sums_ref[...].astype(BF16)
+def gather_kernel(parts_ref, query_ref, sums_ref):
+    for group in range(GROUPS):
+        sums_ref[pl.ds(group, PART, stride=GROUPS), :] = parts_ref[2 * group] + parts_ref[2 * group + 1]
+    query_ref[...] = sums_ref[...].astype(BF16)
 
 
 def chunk_grads(inputs, cot, logs3, keys, queries, start, end):
@@ -364,7 +373,10 @@
             lanes_of(input_ref, n).astype(F32), cot, logs3, keys, queries, start, ends_ref[n]
         )
         input_grad_ref[n] = input_grad.astype(BF16)
-        by_core(n, core_ref[0], key_grad, key_mine_ref, key_peer_ref)
+        for side_y in range(2):
+            first, second = (key_grad[PART * row : PART * (row + 1)] for row in (2 * side_y, 2 * side_y + 1))
+            key_mine_ref[side_y * PLANES + n] = jnp.where(core_ref[0] == 0, first, second)
+            key_peer_ref[side_y * PLANES + n] = jnp.where(core_ref[0] == 0, second, first)
         query_grad_ref[n * T : (n + 1) * T, :] = query_grad
         pairs = [
             (input_grad_ref.at[n], lanes_at(input_grad_hbm, n)),
@@ -485,7 +497,7 @@
 
 def start_part_kernel(length_ref, core_ref, cot_ref, logs_ref, local_ref, state_ref, mine_ref, peer_ref):
     width = cot_ref.shape[0]
-    state = jnp.concatenate([state_ref[place, STATES:] for place in range(state_ref.shape[0])], axis=0)
+    state = jnp.concatenate([state_ref[place, STATES:KEYS] for place in range(state_ref.shape[0])], axis=0)
     state_high, state_low = split(state)
     total = jnp.zeros((logs_ref.shape[0], T), F32)
     for n in range(cot_ref.shape[1] // T):
@@ -498,11 +510,6 @@
         part = both[:, :N] + (both[:, N:] + dot(low, state_high))
         by_core(n, core_ref[0], tokens_of(local_ref, n) + part, mine_ref, peer_ref)
         total = total + last
-
-
-def tail_kernel(key_ref, query_mine_ref, query_got_ref, out_ref):
-    out_ref[:, :PART] = key_ref[...]
-    out_ref[:, PART:] = query_mine_ref[...] + query_got_ref[...]
 
 
 def shape(*dims, dtype=F32):
@@ -649,29 +656,34 @@
         (sent, ax_grad, aq_local, key_mine, key_peer)
     )
     finals = over(sent, "comp")
-    key_parts = key_mine + swap_cores(key_peer)
+    key_part = shape(planes, PART, N)
+    key_keep, key_away = call(key_chip_kernel, [key_part, key_part], scalars=1, count=2, flops=10**7, name="key_chip")(
+        at, key_mine, swap_cores(key_peer)
+    )
+    key_got = swap_chips(key_away)
     finals, near_input, near_key, near_query = lax.optimization_barrier((finals, near_input, near_key, near_query))
     (sent,) = call(
-        scan_back_kernel, [shape(planes, 3 * PART, N)], count=3, flops=10**7, name="scan_back"
-    )(blocks, starts, finals)
+        scan_back_kernel, [shape(planes, KEYS + PART, N)], count=5, flops=10**7, name="scan_back"
+    )(blocks, starts, finals, key_keep, key_got)
     states = over(sent, "seq", same_pair)
-    chip_own, chip_other = call(
-        unpack_kernel, [half, half], scalars=1, count=4, flops=10**7, name="unpack"
+    gathered = shape(PART * GROUPS, N, dtype=BF16)
+    chip_own, chip_other, key_out = call(
+        unpack_kernel, [half, half, gathered], scratch=[held(PART * GROUPS, N)],
+        scalars=1, count=4, flops=10**7, name="unpack",
     )(at, keep, chip_theirs, chip_totals, states)
+    states, chip_own, chip_other = lax.optimization_barrier((states, chip_own, chip_other))
     chip_got = swap_chips(chip_other)
 
     query_mine, query_peer = call(
         start_part_kernel, [shape(chips, PART, N), shape(chips, PART, N)],
         scalars=2, far=3, count=1, flops=10**9, name="answer_start_part",
     )(answer_lengths, core, acot, alogs, aq_local, states)
-    (sent,) = call(tail_kernel, [shape(chips, 2 * PART, N)], count=3, flops=10**7, name="pack_tail")(
-        key_parts, query_mine, swap_cores(query_peer)
-    )
-    parts = over(sent, "seq", same_core)
     own, other = call(
         unpack_chip_kernel, [shape(chips, 2 * PART, N), shape(chips, 2 * PART, N)],
         scalars=1, count=5, flops=10**7, name="unpack_chip",
     )(at, mine, theirs, totals, chip_own, chip_got)
+    sent, own, other = lax.optimization_barrier((query_mine + swap_cores(query_peer), own, other))
+    parts = over(sent, "seq", same_core)
     x_grad, k_grad, q_grad = call(
         prompt_far_kernel,
         [shape(width, tokens, dtype=BF16), shape(tokens, N, dtype=BF16), shape(tokens, N, dtype=BF16)],
@@ -686,10 +698,8 @@
         core, x, cot, logs, keys, carried, pulled, near_input, near_key, near_query, own, swap_cores(other),
     )
 
-    gathered = shape(PART * GROUPS, N, dtype=BF16)
-    key_out, query_out = call(
-        gather_kernel, [gathered, gathered], scratch=[held(PART * GROUPS, N)],
-        count=1, flops=10**7, name="gather_groups",
+    (query_out,) = call(
+        gather_kernel, [gathered], scratch=[held(PART * GROUPS, N)], count=1, flops=10**7, name="gather_groups"
     )(parts)
 
     return (

time: 111 us -> 121 us (1.090)
  blocking collectives: 0 us -> 36 us
  waiting for transfers between devices: 28.1 us -> 9.11 us
  starting transfers between devices: 25.4 us -> 20.1 us
  local copies, waits for them, and re-layouts: 7.01 us -> 4.4 us
    all_to_all x0 -> x2, blocking collectives: none -> 36 us  [over(): lax.all_to_all(value, axis, 0, 0, axis_index_groups=groups, tiled=True)]
    all_to_all x4 -> x2, waiting for transfers between devices: 21.5 us -> 5.34 us  [over(): lax.all_to_all(value, axis, 0, 0, axis_index_groups=groups, tiled=True)]
    all_to_all x4 -> x2, starting transfers between devices: 22.8 us -> 15.7 us  [over(): lax.all_to_all(value, axis, 0, 0, axis_index_groups=groups, tiled=True)]
    unnamed x24 -> x18, local copies, waits for them, and re-layouts: 7.01 us -> 4.4 us
    ppermute x2 -> x3, starting transfers between devices: 2.4 us -> 3.92 us  [swap_chips(): return lax.ppermute(value, 'seq', [(i, i ^ 2) for i in range(seq)])]
    ppermute x2 -> x3, waiting for transfers between devices: 2.66 us -> 1.18 us  [swap_chips(): return lax.ppermute(value, 'seq', [(i, i ^ 2) for i in range(seq)])]
    ppermute x4, waiting for transfers between devices: 3.96 us -> 2.59 us  [swap_cores(): return lax.ppermute(value, 'seq', [(i, i ^ 1) for i in range(seq)])]
  transfers between devices with their start and end apart: 10 -> 9, of which waited for: 8 -> 6; matrix products, arithmetic and copies ran while one was open for 0% -> 0% of each run, Pallas kernels for 34% -> 24%
where the time goes in v3:
time: 121 us; the launch traced here: 120 us
  Pallas kernels  48 us (40%)
  blocking collectives  36 us (30%)
  starting transfers between devices  20.1 us (17%)
  waiting for transfers between devices  9.11 us (8%)
  local copies, waits for them, and re-layouts  4.4 us (4%)
  between operations  1.61 us (1%)
    pallas_call x14, Pallas kernels, run(): pl.pallas_call(inner, out_shape=outs, in_specs=[pl.BlockSpec(memory_space...  48 us
    all_to_all x2, blocking collectives, over(): lax.all_to_all(value, axis, 0, 0, axis_index_groups=groups, tiled=True)  36 us
    all_to_all x2, starting transfers between devices, over(): lax.all_to_all(value, axis, 0, 0, axis_index_groups=groups, tiled=True)  15.7 us
    all_to_all x2, waiting for transfers between devices, over(): lax.all_to_all(value, axis, 0, 0, axis_index_groups=groups, tiled=True)  5.34 us
    unnamed x18, local copies, waits for them, and re-layouts  4.4 us
    ppermute x3, starting transfers between devices, swap_chips(): return lax.ppermute(value, 'seq', [(i, i ^ 2) for i in range(seq)])  3.92 us
    ppermute x4, waiting for transfers between devices, swap_cores(): return lax.ppermute(value, 'seq', [(i, i ^ 1) for i in range(seq)])  2.59 us
  transfers between devices with their start and end apart: 9, of which 6 were waited for; matrix products, arithmetic and copies ran while one was open for 0% of the time, Pallas kernels for 24%

profile of v3, /device:TPU:16, one launch (start us, length us, event | category | flops | bytes accessed | tf_op | source)
XLA Modules:
  0.0 120.2 jit_solution(15279778814908362132)
XLA Ops:
  0.6 6.1 %prompt_summary.1 = (f32[4,1024,128]{2,1,0:T(8,128)}, f32[4,1024,128]{2,1,0:T(8,128)}, f32[16,64,128]{2,1,0:T(8,128)}, f32[17,64,128]{2,1,0:T(8,128)}, f32[16,128]{1,0:T(8,128)}) custom-call(s32[1]{0:T(128)} %bitcast.core_ref.refs_1_, bf16[1024,512]{1,0:T(8,128)(2,1)} %bitcast.48, bf16[1024,512]{1,0:T(8,128)(2,1)} %bitcast.51, f32[16,512]{1,0:T(8,128)} %bitcast.61, ...), custom_call_target="tpu_custom_call" | custom-call | flops 1000000000 | bytes 2000000 | tf_op jit(solution)/shard_map/prompt_summary/pallas_call | solution.py:545
  6.8 0.1 collective-permute-start
  6.9 0.1 pad_add_fusion.at_ref
  7.0 2.0 %collective-permute-done.got_ref = f32[17,64,128]{2,1,0:T(8,128)S(1)} collective-permute-done((f32[17,64,128]{2,1,0:T(8,128)}, f32[17,64,128]{2,1,0:T(8,128)S(1)}, u32[]{:S(2)}, u32[]{:S(2)}) %collective-permute-start) | collective-permute-done | bytes 557088 | tf_op jit(solution)/shard_map/ppermute | solution.py:580
  9.1 0.0 copy-start
  9.1 1.0 copy-done
  10.1 0.0 copy-start.5
  10.1 0.7 copy-done.5
  10.8 0.6 pack_chip.1
  11.4 1.4 %collective-permute-start.1 = (f32[9,64,128]{2,1,0:T(8,128)S(1)}, f32[9,64,128]{2,1,0:T(8,128)S(1)}, u32[]{:S(2)}, u32[]{:S(2)}) collective-permute-start(f32[9,64,128]{2,1,0:T(8,128)S(1)} %get-tuple-element.60), channel_id=1, source_target_pairs={{0,16},{8,24},{16,0},{24,8},{32,48},{40,56},{48,32},{56,40},{64,80... | collective-permute-start | bytes 884744 | tf_op jit(solution)/shard_map/ppermute | solution.py:583
  13.5 6.7 %answer_ends.1 = (f32[8,256,128]{2,1,0:T(8,128)}, bf16[1024,128]{1,0:T(8,128)(2,1)}, bf16[1024,128]{1,0:T(8,128)(2,1)}, f32[256,128]{1,0:T(8,128)}) custom-call(s32[1]{0:T(128)S(6)} %copy.17.length_ref.refs_0_, s32[1]{0:T(128)} %bitcast.11.group_ref, bf16[256,1024]{1,0:T(8,128)(2,1)} %bitcast.41, f32[4,1024]{1,0:T(4,128)} %bitcast.45, ...), custom_call_target="tpu_custom_call" | custom-call | flops 1000000000 | bytes 2000000 | tf_op jit(solution)/shard_map/answer_ends/pallas_call | solution.py:545
  20.2 0.4 collective-permute-done.1.got_ref
  20.6 0.0 copy-start.4
  20.6 0.9 copy-done.4
  21.5 1.4 %pack.1 = f32[8,104,128]{2,1,0:T(8,128)} custom-call(s32[2]{0:T(128)S(1)} %pad_add_fusion.at_ref, f32[8,64,128]{2,1,0:T(8,128)S(1)} %get-tuple-element.59.keep_ref, f32[9,64,128]{2,1,0:T(8,128)S(1)} %collective-permute-done.1.got_ref, f32[16,128]{1,0:T(8,128)S(1)} %get-tuple-element.61.total_ref, f32[256,128]{1,0:T(8,128)S(1)} %copy-done.4), custom_call_target="tpu_custom_call" | custom-call | flops 10000000 | bytes 2000000 | tf_op jit(solution)/shard_map/pack/pallas_call | solution.py:545
  22.9 8.5 %all-to-all-start = ((f32[8,104,128]{2,1,0:T(8,128)}), f32[8,104,128]{2,1,0:T(8,128)S(1)}, u32[]{:S(2)}, u32[]{:S(2)}) async-start(f32[8,104,128]{2,1,0:T(8,128)} %pack.1), calls=%async_computation | async-start | bytes 851968 | tf_op jit(solution)/shard_map/all_to_all | solution.py:586
  31.3 9.7 %answer_grads.1 = (bf16[256,1024]{1,0:T(8,128)(2,1)}, f32[1024,128]{1,0:T(8,128)}, f32[16,32,128]{2,1,0:T(8,128)}, f32[16,32,128]{2,1,0:T(8,128)}) custom-call(s32[1]{0:T(128)S(6)} %copy.17.length_ref.refs_0_, s32[1]{0:T(128)} %bitcast.core_ref.refs_1_, bf16[256,1024]{1,0:T(8,128)(2,1)} %bitcast.54, bf16[256,1024]{1,0:T(8,128)(2,1)} %bitcast.42, ...), custom_call_target="tpu_custom_call" | custom-call | flops 3000000000 | bytes 2000000 | tf_op jit(solution)/shard_map/answer_grads/pallas_call | solution.py:545
  41.1 5.3 %all-to-all-done.blocks_ref = f32[8,104,128]{2,1,0:T(8,128)S(1)} async-done(((f32[8,104,128]{2,1,0:T(8,128)}), f32[8,104,128]{2,1,0:T(8,128)S(1)}, u32[]{:S(2)}, u32[]{:S(2)}) %all-to-all-start) | async-done | bytes 426016 | tf_op jit(solution)/shard_map/all_to_all | solution.py:586
  46.4 0.7 scan.1
  47.1 0.0 collective-permute-start.2
  47.1 7.3 %all-to-all-start.1 = ((f32[8,64,128]{2,1,0:T(8,128)}), f32[8,64,128]{2,1,0:T(8,128)S(1)}, u32[]{:S(2)}, u32[]{:S(2)}) async-start(f32[8,64,128]{2,1,0:T(8,128)} %get-tuple-element.71), calls=%async_computation.1 | async-start | bytes 524288 | tf_op jit(solution)/shard_map/all_to_all | solution.py:586
  54.4 0.0 collective-permute-done.2.got_ref
  54.4 0.9 copy-done.3
  55.3 0.6 key_chip.1
  55.9 1.4 %collective-permute-start.3 = (f32[8,32,128]{2,1,0:T(8,128)S(1)}, f32[8,32,128]{2,1,0:T(8,128)S(1)}, u32[]{:S(2)}, u32[]{:S(2)}) collective-permute-start(f32[8,32,128]{2,1,0:T(8,128)S(1)} %get-tuple-element.84), channel_id=1, source_target_pairs={{0,16},{8,24},{16,0},{24,8},{32,48},{40,56},{48,32},{56,40},{64,80... | collective-permute-start | bytes 393224 | tf_op jit(solution)/shard_map/ppermute | solution.py:583
  57.3 5.7 %prompt_near.1 = (f32[4,1024,128]{2,1,0:T(8,128)}, f32[512,128]{1,0:T(8,128)}, f32[512,128]{1,0:T(8,128)}) custom-call(bf16[1024,512]{1,0:T(8,128)(2,1)} %bitcast.49, bf16[1024,512]{1,0:T(8,128)(2,1)} %bitcast.52, f32[16,512]{1,0:T(8,128)} %bitcast.62, bf16[512,128]{1,0:T(8,128)(2,1)} %bitcast.58, bf16[512,128]{1,0:T(8,128)(2,1)} %bitcast.56), custom_call_target="tpu_custom_call" | custom-call | flops 3000000000 | bytes 2000000 | tf_op jit(solution)/shard_map/prompt_near/pallas_call | solution.py:545
  63.0 0.0 all-to-all-done.1.got_ref
  63.0 0.4 collective-permute-done.3.key_got_ref
  63.4 20.2 %all_to_all.20.states_ref.refs_5_ = f32[8,128,128]{2,1,0:T(8,128)S(1)} all-to-all(f32[8,128,128]{2,1,0:T(8,128)S(1)} %scan_back.1), channel_id=1, replica_groups={{0,32,64,96,128,160,192,224},{8,40,72,104,136,168,200,232},{16,48,80,11..., dimensions={0} | all-to-all | bytes 1048576 | tf_op jit(solution)/shard_map/all_to_all | solution.py:586
  83.5 1.2 %unpack.1 = (f32[8,64,128]{2,1,0:T(8,128)S(1)}, f32[8,64,128]{2,1,0:T(8,128)S(1)}, bf16[256,128]{1,0:T(8,128)(2,1)}) custom-call(s32[2]{0:T(128)S(1)} %pad_add_fusion.at_ref, f32[8,64,128]{2,1,0:T(8,128)S(1)} %get-tuple-element.59.keep_ref, f32[9,64,128]{2,1,0:T(8,128)S(1)} %collective-permute-done.1.got_ref, f32[16,128]{1,0:T(8,128)S(1)} %get-tuple-element.61.total_ref, ...), custom_call_target="tpu_custom_call" | custom-call | flops 10000000 | bytes 2000000 | tf_op jit(solution)/shard_map/unpack/pallas_call | solution.py:545
  84.8 1.2 collective-permute-start.5
  86.0 0.0 copy-done.2
  86.0 5.3 %answer_start_part.1 = (f32[16,32,128]{2,1,0:T(8,128)}, f32[16,32,128]{2,1,0:T(8,128)}) custom-call(s32[1]{0:T(128)S(6)} %copy.17.length_ref.refs_0_, s32[1]{0:T(128)} %bitcast.core_ref.refs_1_, bf16[256,1024]{1,0:T(8,128)(2,1)} %bitcast.43, f32[4,1024]{1,0:T(4,128)} %bitcast.47, f32[1024,128]{1,0:T(8,128)} %get-tuple-element.78.refs_4_, ...), custom_call_target="tpu_custom_call" | custom-call | flops 1000000000 | bytes 2000000 | tf_op jit(solution)/shard_map/answer_start_part/pallas_call | solution.py:545
  91.3 0.1 collective-permute-start.4
  91.4 0.5 collective-permute-done.5.away_ref
  91.9 0.0 copy-done.1
  91.9 0.0 copy-done.6
  91.9 0.7 unpack_chip.1
  92.6 0.0 copy-start.7
  92.6 0.5 collective-permute-done.4
  93.1 1.0 add.14
  94.1 0.2 collective-permute-start.6
  94.4 15.9 %all_to_all.21.parts_ref = f32[16,32,128]{2,1,0:T(8,128)S(1)} all-to-all(f32[16,32,128]{2,1,0:T(8,128)S(1)} %add.14), channel_id=1, replica_groups={{0,16,32,48,64,80,96,112,128,144,160,176,192,208,224,240},{8,24,40,56,7..., dimensions={0} | all-to-all | bytes 524288 | tf_op jit(solution)/shard_map/all_to_all | solution.py:586
  110.2 0.7 gather_groups.1
  110.9 0.0 collective-permute-done.6.got_hbm
  110.9 0.0 copy-done.7
  110.9 0.8 copy-done.8
  111.7 8.4 %prompt_far.1 = (bf16[1024,512]{1,0:T(8,128)(2,1)}, bf16[512,128]{1,0:T(8,128)(2,1)}, bf16[512,128]{1,0:T(8,128)(2,1)}) custom-call(s32[1]{0:T(128)} %bitcast.core_ref.refs_1_, bf16[1024,512]{1,0:T(8,128)(2,1)} %bitcast.50, bf16[1024,512]{1,0:T(8,128)(2,1)} %bitcast.53, f32[16,512]{1,0:T(8,128)} %bitcast.63, bf16[512,128]{1,0:T(8,128)(2,1)} %bitcast.59, ...), custom_call_target="tpu_custom_call" | custom-call | flops 3000000000 | bytes 2000000 | tf_op jit(solution)/shard_map/prompt_far/pallas_call | solution.py:545
  (6 shorter events, 0.1 us)
Async XLA Ops:
  6.8 2.3 %collective-permute-start = (f32[17,64,128]{2,1,0:T(8,128)}, f32[17,64,128]{2,1,0:T(8,128)S(1)}, u32[]{:S(2)}, u32[]{:S(2)}) collective-permute-start(f32[17,64,128]{2,1,0:T(8,128)} %get-tuple-element.57), channel_id=1, source_target_pairs={{0,8},{8,0},{16,24},{24,16},{32,40},{40,32},{48,56},{56,48},{64,72... | collective-permute-start | bytes 1671176 | tf_op jit(solution)/shard_map/ppermute | solution.py:580
  9.1 1.0 copy-start
  10.1 0.7 copy-start.5
  11.4 9.1 %collective-permute-start.1 = (f32[9,64,128]{2,1,0:T(8,128)S(1)}, f32[9,64,128]{2,1,0:T(8,128)S(1)}, u32[]{:S(2)}, u32[]{:S(2)}) collective-permute-start(f32[9,64,128]{2,1,0:T(8,128)S(1)} %get-tuple-element.60), channel_id=1, source_target_pairs={{0,16},{8,24},{16,0},{24,8},{32,48},{40,56},{48,32},{56,40},{64,80... | collective-permute-start | bytes 884744 | tf_op jit(solution)/shard_map/ppermute | solution.py:583
  20.6 0.9 copy-start.4
  22.9 23.5 %all-to-all-start = ((f32[8,104,128]{2,1,0:T(8,128)}), f32[8,104,128]{2,1,0:T(8,128)S(1)}, u32[]{:S(2)}, u32[]{:S(2)}) async-start(f32[8,104,128]{2,1,0:T(8,128)} %pack.1), calls=%async_computation | async-start | bytes 851968 | tf_op jit(solution)/shard_map/all_to_all | solution.py:586
  47.1 7.3 %collective-permute-start.2 = (f32[16,32,128]{2,1,0:T(8,128)}, f32[16,32,128]{2,1,0:T(8,128)S(1)}, u32[]{:S(2)}, u32[]{:S(2)}) collective-permute-start(f32[16,32,128]{2,1,0:T(8,128)} %get-tuple-element.82), channel_id=1, source_target_pairs={{0,8},{8,0},{16,24},{24,16},{32,40},{40,32},{48,56},{56,48},{64,72... | collective-permute-start | bytes 786440 | tf_op jit(solution)/shard_map/ppermute | solution.py:580
  47.1 15.8 %all-to-all-start.1 = ((f32[8,64,128]{2,1,0:T(8,128)}), f32[8,64,128]{2,1,0:T(8,128)S(1)}, u32[]{:S(2)}, u32[]{:S(2)}) async-start(f32[8,64,128]{2,1,0:T(8,128)} %get-tuple-element.71), calls=%async_computation.1 | async-start | bytes 524288 | tf_op jit(solution)/shard_map/all_to_all | solution.py:586
  54.4 1.0 copy-start.3
  55.9 7.4 %collective-permute-start.3 = (f32[8,32,128]{2,1,0:T(8,128)S(1)}, f32[8,32,128]{2,1,0:T(8,128)S(1)}, u32[]{:S(2)}, u32[]{:S(2)}) collective-permute-start(f32[8,32,128]{2,1,0:T(8,128)S(1)} %get-tuple-element.84), channel_id=1, source_target_pairs={{0,16},{8,24},{16,0},{24,8},{32,48},{40,56},{48,32},{56,40},{64,80... | collective-permute-start | bytes 393224 | tf_op jit(solution)/shard_map/ppermute | solution.py:583
  83.5 2.4 %copy-start.2 = (f32[8,128,128]{2,1,0:T(8,128)}, f32[8,128,128]{2,1,0:T(8,128)S(1)}, u32[]{:S(2)}) copy-start(f32[8,128,128]{2,1,0:T(8,128)S(1)} %all_to_all.20.states_ref.refs_5_) | copy-start | bytes 1572868
  84.8 7.1 %copy-start.1 = (f32[16,64,128]{2,1,0:T(8,128)S(1)}, f32[16,64,128]{2,1,0:T(8,128)}, u32[]{:S(2)}) copy-start(f32[16,64,128]{2,1,0:T(8,128)} %get-tuple-element.56.mine_ref) | copy-start | bytes 1572868
  84.8 7.1 %copy-start.6 = (f32[16,128]{1,0:T(8,128)S(1)}, f32[16,128]{1,0:T(8,128)}, u32[]{:S(2)}) copy-start(f32[16,128]{1,0:T(8,128)} %get-tuple-element.58.total_ref) | copy-start | bytes 24580
  84.8 7.1 %collective-permute-start.5 = (f32[8,64,128]{2,1,0:T(8,128)S(1)}, f32[8,64,128]{2,1,0:T(8,128)S(1)}, u32[]{:S(2)}, u32[]{:S(2)}) collective-permute-start(f32[8,64,128]{2,1,0:T(8,128)S(1)} %get-tuple-element.91), channel_id=1, source_target_pairs={{0,16},{8,24},{16,0},{24,8},{32,48},{40,56},{48,32},{56,40},{64,80... | collective-permute-start | bytes 786440 | tf_op jit(solution)/shard_map/ppermute | solution.py:583
  91.3 1.8 %collective-permute-start.4 = (f32[16,32,128]{2,1,0:T(8,128)}, f32[16,32,128]{2,1,0:T(8,128)S(1)}, u32[]{:S(2)}, u32[]{:S(2)}) collective-permute-start(f32[16,32,128]{2,1,0:T(8,128)} %get-tuple-element.89), channel_id=1, source_target_pairs={{0,8},{8,0},{16,24},{24,16},{32,40},{40,32},{48,56},{56,48},{64,72... | collective-permute-start | bytes 786440 | tf_op jit(solution)/shard_map/ppermute | solution.py:580
  92.6 18.3 %copy-start.7 = (f32[16,64,128]{2,1,0:T(8,128)}, f32[16,64,128]{2,1,0:T(8,128)S(1)}, u32[]{:S(2)}) copy-start(f32[16,64,128]{2,1,0:T(8,128)S(1)} %get-tuple-element.94.own_hbm) | copy-start | bytes 1572868
  94.1 16.8 %collective-permute-start.6 = (f32[16,64,128]{2,1,0:T(8,128)S(1)}, f32[16,64,128]{2,1,0:T(8,128)S(1)}, u32[]{:S(2)}, u32[]{:S(2)}) collective-permute-start(f32[16,64,128]{2,1,0:T(8,128)S(1)} %get-tuple-element.95), channel_id=1, source_target_pairs={{0,8},{8,0},{16,24},{24,16},{32,40},{40,32},{48,56},{56,48},{64,72... | collective-permute-start | bytes 1572872 | tf_op jit(solution)/shard_map/ppermute | solution.py:580
  110.9 0.8 copy-start.8

commit v4 on v2

--- a/solution.py
+++ b/solution.py
@@ -483,21 +483,27 @@
     wait_all(sent)
 
 
-def start_part_kernel(length_ref, core_ref, cot_ref, logs_ref, local_ref, state_ref, mine_ref, peer_ref):
-    width = cot_ref.shape[0]
-    state = jnp.concatenate([state_ref[place, STATES:] for place in range(state_ref.shape[0])], axis=0)
-    state_high, state_low = split(state)
+def prepare_kernel(length_ref, cot_ref, logs_ref, local_ref, high_ref, low_ref, local_out_ref):
+    local_out_ref[...] = local_ref[...]
     total = jnp.zeros((logs_ref.shape[0], T), F32)
     for n in range(cot_ref.shape[1] // T):
         sums, _, last = chunk_logs(logs_ref, n)
         scaled = lanes_of(cot_ref, n).astype(F32) * rows(jnp.exp(total + sums))
-        scaled = jnp.where(live_mask(n, length_ref[0], width), scaled, 0.0)
+        scaled = jnp.where(live_mask(n, length_ref[0], cot_ref.shape[0]), scaled, 0.0)
         high, low = split(scaled)
-        high, low = high.T, low.T
-        both = dot(high, side(state_high, state_low))
-        part = both[:, :N] + (both[:, N:] + dot(low, state_high))
+        high_ref[n * T : (n + 1) * T, :] = high.T
+        low_ref[n * T : (n + 1) * T, :] = low.T
+        total = total + last
+
+
+def start_part_kernel(core_ref, high_ref, low_ref, local_ref, state_ref, mine_ref, peer_ref):
+    state = jnp.concatenate([state_ref[place, STATES:] for place in range(state_ref.shape[0])], axis=0)
+    state_high, state_low = split(state)
+    both = side(state_high, state_low)
+    for n in range(high_ref.shape[0] // T):
+        part = dot(tokens_of(high_ref, n), both)
+        part = part[:, :N] + (part[:, N:] + dot(tokens_of(low_ref, n), state_high))
         by_core(n, core_ref[0], tokens_of(local_ref, n) + part, mine_ref, peer_ref)
-        total = total + last
 
 
 def tail_kernel(key_ref, query_mine_ref, query_got_ref, out_ref):
@@ -654,16 +660,23 @@
     (sent,) = call(
         scan_back_kernel, [shape(planes, 3 * PART, N)], count=3, flops=10**7, name="scan_back"
     )(blocks, starts, finals)
+    sent, late_cot, late_logs, aq_local = lax.optimization_barrier((sent, acot, alogs, aq_local))
     states = over(sent, "seq", same_pair)
+    late_high, late_low, aq_local = call(
+        prepare_kernel,
+        [shape(length, answer_width, dtype=BF16), shape(length, answer_width, dtype=BF16), shape(length, N)],
+        scalars=1, count=3, flops=10**9, name="answer_prepare",
+    )(answer_lengths, late_cot, late_logs, aq_local)
     chip_own, chip_other = call(
         unpack_kernel, [half, half], scalars=1, count=4, flops=10**7, name="unpack"
     )(at, keep, chip_theirs, chip_totals, states)
+    states, chip_own, chip_other = lax.optimization_barrier((states, chip_own, chip_other))
     chip_got = swap_chips(chip_other)
 
     query_mine, query_peer = call(
         start_part_kernel, [shape(chips, PART, N), shape(chips, PART, N)],
-        scalars=2, far=3, count=1, flops=10**9, name="answer_start_part",
-    )(answer_lengths, core, acot, alogs, aq_local, states)
+        scalars=1, count=4, flops=10**9, name="answer_start_part",
+    )(core, late_high, late_low, aq_local, states)
     (sent,) = call(tail_kernel, [shape(chips, 2 * PART, N)], count=3, flops=10**7, name="pack_tail")(
         key_parts, query_mine, swap_cores(query_peer)
     )
@@ -686,6 +699,7 @@
         core, x, cot, logs, keys, carried, pulled, near_input, near_key, near_query, own, swap_cores(other),
     )
 
+    parts, x_grad, k_grad, q_grad = lax.optimization_barrier((parts, x_grad, k_grad, q_grad))
     gathered = shape(PART * GROUPS, N, dtype=BF16)
     key_out, query_out = call(
         gather_kernel, [gathered, gathered], scratch=[held(PART * GROUPS, N)],

time: 111 us -> 107 us (0.964)
  Pallas kernels: 48.4 us -> 44.3 us
  waiting for transfers between devices: 28.1 us -> 24.8 us
  local copies, waits for them, and re-layouts: 7.01 us -> 9.01 us
    pallas_call x14 -> x15, Pallas kernels: 48.4 us -> 44.3 us  [run(): pl.pallas_call(inner, out_shape=outs, in_specs=[pl.BlockSpec(memory_space...]
    all_to_all x4, waiting for transfers between devices: 21.5 us -> 18.3 us  [over(): lax.all_to_all(value, axis, 0, 0, axis_index_groups=groups, tiled=True)]
    unnamed x24 -> x30, local copies, waits for them, and re-layouts: 7.01 us -> 9.01 us
  transfers between devices with their start and end apart: 10 -> 10, of which waited for: 8 -> 8; matrix products, arithmetic and copies ran while one was open for 0% -> 1% of each run, Pallas kernels for 34% -> 32%
where the time goes in v4:
time: 107 us; the launch traced here: 106 us
  Pallas kernels  44.3 us (41%)
  starting transfers between devices  25.5 us (24%)
  waiting for transfers between devices  24.8 us (23%)
  local copies, waits for them, and re-layouts  9.01 us (8%)
  between operations  1.53 us (1%)
  other arithmetic  1.07 us (1%)
    pallas_call x15, Pallas kernels, run(): pl.pallas_call(inner, out_shape=outs, in_specs=[pl.BlockSpec(memory_space...  44.3 us
    all_to_all x4, starting transfers between devices, over(): lax.all_to_all(value, axis, 0, 0, axis_index_groups=groups, tiled=True)  22.8 us
    all_to_all x4, waiting for transfers between devices, over(): lax.all_to_all(value, axis, 0, 0, axis_index_groups=groups, tiled=True)  18.3 us
    unnamed x30, local copies, waits for them, and re-layouts  9.01 us
    ppermute x4, waiting for transfers between devices, swap_cores(): return lax.ppermute(value, 'seq', [(i, i ^ 1) for i in range(seq)])  3.96 us
    ppermute x2, waiting for transfers between devices, swap_chips(): return lax.ppermute(value, 'seq', [(i, i ^ 2) for i in range(seq)])  2.54 us
    ppermute x2, starting transfers between devices, swap_chips(): return lax.ppermute(value, 'seq', [(i, i ^ 2) for i in range(seq)])  2.44 us
  transfers between devices with their start and end apart: 10, of which 8 were waited for; matrix products, arithmetic and copies ran while one was open for 1% of the time, Pallas kernels for 32%

profile of v4, /device:TPU:16, one launch (start us, length us, event | category | flops | bytes accessed | tf_op | source)
XLA Modules:
  0.0 106.2 jit_solution(11743511824959810581)
XLA Ops:
  0.6 6.2 %prompt_summary.1 = (f32[4,1024,128]{2,1,0:T(8,128)}, f32[4,1024,128]{2,1,0:T(8,128)}, f32[16,64,128]{2,1,0:T(8,128)}, f32[17,64,128]{2,1,0:T(8,128)}, f32[16,128]{1,0:T(8,128)}) custom-call(s32[1]{0:T(128)} %bitcast.core_ref, bf16[1024,512]{1,0:T(8,128)(2,1)} %bitcast.47, bf16[1024,512]{1,0:T(8,128)(2,1)} %bitcast.50, f32[16,512]{1,0:T(8,128)} %bitcast.61, ...), custom_call_target="tpu_custom_call" | custom-call | flops 1000000000 | bytes 2000000 | tf_op jit(solution)/shard_map/prompt_summary/pallas_call | solution.py:544
  6.8 0.1 collective-permute-start
  7.0 0.1 pad_add_fusion.at_ref
  7.0 2.0 %collective-permute-done.got_ref = f32[17,64,128]{2,1,0:T(8,128)S(1)} collective-permute-done((f32[17,64,128]{2,1,0:T(8,128)}, f32[17,64,128]{2,1,0:T(8,128)S(1)}, u32[]{:S(2)}, u32[]{:S(2)}) %collective-permute-start) | collective-permute-done | bytes 557088 | tf_op jit(solution)/shard_map/ppermute | solution.py:579
  9.1 1.0 copy-done
  10.1 0.7 copy-done.4
  10.8 0.6 pack_chip.1
  11.5 1.4 %collective-permute-start.1 = (f32[9,64,128]{2,1,0:T(8,128)S(1)}, f32[9,64,128]{2,1,0:T(8,128)S(1)}, u32[]{:S(2)}, u32[]{:S(2)}) collective-permute-start(f32[9,64,128]{2,1,0:T(8,128)S(1)} %get-tuple-element.65), channel_id=1, source_target_pairs={{0,16},{8,24},{16,0},{24,8},{32,48},{40,56},{48,32},{56,40},{64,80... | collective-permute-start | bytes 884744 | tf_op jit(solution)/shard_map/ppermute | solution.py:582
  13.5 6.7 %answer_ends.1 = (f32[8,256,128]{2,1,0:T(8,128)}, bf16[1024,128]{1,0:T(8,128)(2,1)}, bf16[1024,128]{1,0:T(8,128)(2,1)}, f32[256,128]{1,0:T(8,128)}) custom-call(s32[1]{0:T(128)S(6)} %copy.17.length_ref, s32[1]{0:T(128)} %bitcast.9.group_ref, bf16[256,1024]{1,0:T(8,128)(2,1)} %bitcast.39, f32[4,1024]{1,0:T(4,128)} %bitcast.42, bf16[8192,128]{1,0:T(8,128)(2,1)} %bitcast.45, ...), custom_call_target="tpu_custom_call" | custom-call | flops 1000000000 | bytes 2000000 | tf_op jit(solution)/shard_map/answer_ends/pallas_call | solution.py:544
  20.2 0.4 collective-permute-done.1.got_ref
  20.6 0.9 copy-done.3
  21.5 1.4 %pack.1 = f32[8,104,128]{2,1,0:T(8,128)} custom-call(s32[2]{0:T(128)S(1)} %pad_add_fusion.at_ref, f32[8,64,128]{2,1,0:T(8,128)S(1)} %get-tuple-element.64.keep_ref, f32[9,64,128]{2,1,0:T(8,128)S(1)} %collective-permute-done.1.got_ref, f32[16,128]{1,0:T(8,128)S(1)} %get-tuple-element.66.total_ref, f32[256,128]{1,0:T(8,128)S(1)} %copy-done.3), custom_call_target="tpu_custom_call" | custom-call | flops 10000000 | bytes 2000000 | tf_op jit(solution)/shard_map/pack/pallas_call | solution.py:544
  22.9 8.5 %all-to-all-start = ((f32[8,104,128]{2,1,0:T(8,128)}), f32[8,104,128]{2,1,0:T(8,128)S(1)}, u32[]{:S(2)}, u32[]{:S(2)}) async-start(f32[8,104,128]{2,1,0:T(8,128)} %pack.1), calls=%async_computation | async-start | bytes 851968 | tf_op jit(solution)/shard_map/all_to_all | solution.py:585
  31.4 9.8 %answer_grads.1 = (bf16[256,1024]{1,0:T(8,128)(2,1)}, f32[1024,128]{1,0:T(8,128)}, f32[16,32,128]{2,1,0:T(8,128)}, f32[16,32,128]{2,1,0:T(8,128)}) custom-call(s32[1]{0:T(128)S(6)} %copy.17.length_ref, s32[1]{0:T(128)} %bitcast.core_ref, bf16[256,1024]{1,0:T(8,128)(2,1)} %bitcast.53, bf16[256,1024]{1,0:T(8,128)(2,1)} %bitcast.40, f32[4,1024]{1,0:T(4,128)} %bitcast.43, ...), custom_call_target="tpu_custom_call" | custom-call | flops 3000000000 | bytes 2000000 | tf_op jit(solution)/shard_map/answer_grads/pallas_call | solution.py:544
  41.2 5.3 %all-to-all-done.blocks_ref = f32[8,104,128]{2,1,0:T(8,128)S(1)} async-done(((f32[8,104,128]{2,1,0:T(8,128)}), f32[8,104,128]{2,1,0:T(8,128)S(1)}, u32[]{:S(2)}, u32[]{:S(2)}) %all-to-all-start) | async-done | bytes 426016 | tf_op jit(solution)/shard_map/all_to_all | solution.py:585
  46.4 0.7 scan.1
  47.2 7.3 %all-to-all-start.1 = ((f32[8,64,128]{2,1,0:T(8,128)}), f32[8,64,128]{2,1,0:T(8,128)S(1)}, u32[]{:S(2)}, u32[]{:S(2)}) async-start(f32[8,64,128]{2,1,0:T(8,128)} %get-tuple-element.79), calls=%async_computation.1 | async-start | bytes 524288 | tf_op jit(solution)/shard_map/all_to_all | solution.py:585
  54.4 5.7 %prompt_near.1 = (f32[4,1024,128]{2,1,0:T(8,128)}, f32[512,128]{1,0:T(8,128)}, f32[512,128]{1,0:T(8,128)}) custom-call(bf16[1024,512]{1,0:T(8,128)(2,1)} %bitcast.48, bf16[1024,512]{1,0:T(8,128)(2,1)} %bitcast.51, f32[16,512]{1,0:T(8,128)} %bitcast.62, bf16[512,128]{1,0:T(8,128)(2,1)} %bitcast.57, bf16[512,128]{1,0:T(8,128)(2,1)} %bitcast.55), custom_call_target="tpu_custom_call" | custom-call | flops 3000000000 | bytes 2000000 | tf_op jit(solution)/shard_map/prompt_near/pallas_call | solution.py:544
  60.1 0.4 all-to-all-done.1.got_ref
  60.5 0.8 scan_back.1
  61.4 3.5 %all-to-all-start.2 = ((f32[8,96,128]{2,1,0:T(8,128)}), f32[8,96,128]{2,1,0:T(8,128)S(1)}, u32[]{:S(2)}, u32[]{:S(2)}) async-start(f32[8,96,128]{2,1,0:T(8,128)} %scan_back.1), calls=%async_computation.2 | async-start | bytes 786432 | tf_op jit(solution)/shard_map/all_to_all | solution.py:585
  64.8 0.1 collective-permute-start.2
  65.0 1.0 copy-done.12
  66.0 0.6 answer_prepare.1
  66.6 0.0 copy-start.8
  66.6 0.8 copy-done.8
  67.4 0.8 copy-done.10
  68.2 9.0 %all-to-all-done.2.states_ref.state_ref = f32[8,96,128]{2,1,0:T(8,128)S(1)} async-done(((f32[8,96,128]{2,1,0:T(8,128)}), f32[8,96,128]{2,1,0:T(8,128)S(1)}, u32[]{:S(2)}, u32[]{:S(2)}) %all-to-all-start.2) | async-done | bytes 393248 | tf_op jit(solution)/shard_map/all_to_all | solution.py:585
  77.2 0.6 unpack.1
  77.8 0.0 copy-start.9
  77.8 1.0 copy-done.9
  78.9 1.0 copy-done.11
  79.9 0.4 answer_start_part.1
  80.4 0.0 copy-start.5
  80.4 0.1 collective-permute-start.3
  80.5 1.1 %collective-permute-start.4 = (f32[8,64,128]{2,1,0:T(8,128)S(1)}, f32[8,64,128]{2,1,0:T(8,128)S(1)}, u32[]{:S(2)}, u32[]{:S(2)}) collective-permute-start(f32[8,64,128]{2,1,0:T(8,128)S(1)} %get-tuple-element.103), channel_id=1, source_target_pairs={{0,16},{8,24},{16,0},{24,8},{32,48},{40,56},{48,32},{56,40},{64,80... | collective-permute-start | bytes 786440 | tf_op jit(solution)/shard_map/ppermute | solution.py:582
  81.5 0.0 collective-permute-done.2
  81.6 1.0 add.14.key_ref
  82.6 0.9 pack_tail.1
  83.5 3.6 %all-to-all-start.3 = ((f32[16,64,128]{2,1,0:T(8,128)}), f32[16,64,128]{2,1,0:T(8,128)S(1)}, u32[]{:S(2)}, u32[]{:S(2)}) async-start(f32[16,64,128]{2,1,0:T(8,128)} %pack_tail.1), calls=%async_computation.3 | async-start | bytes 1048576 | tf_op jit(solution)/shard_map/all_to_all | solution.py:585
  87.0 2.2 %collective-permute-done.4.away_ref = f32[8,64,128]{2,1,0:T(8,128)S(1)} collective-permute-done((f32[8,64,128]{2,1,0:T(8,128)S(1)}, f32[8,64,128]{2,1,0:T(8,128)S(1)}, u32[]{:S(2)}, u32[]{:S(2)}) %collective-permute-start.4) | collective-permute-done | bytes 262176 | tf_op jit(solution)/shard_map/ppermute | solution.py:582
  89.2 0.7 unpack_chip.1
  89.9 0.8 copy-done.7
  90.7 1.9 %collective-permute-done.5.got_hbm = f32[16,64,128]{2,1,0:T(8,128)S(1)} collective-permute-done((f32[16,64,128]{2,1,0:T(8,128)S(1)}, f32[16,64,128]{2,1,0:T(8,128)S(1)}, u32[]{:S(2)}, u32[]{:S(2)}) %collective-permute-start.5) | collective-permute-done | bytes 524320 | tf_op jit(solution)/shard_map/ppermute | solution.py:579
  92.6 0.8 copy-done.14
  93.5 8.4 %prompt_far.1 = (bf16[1024,512]{1,0:T(8,128)(2,1)}, bf16[512,128]{1,0:T(8,128)(2,1)}, bf16[512,128]{1,0:T(8,128)(2,1)}) custom-call(s32[1]{0:T(128)} %bitcast.core_ref, bf16[1024,512]{1,0:T(8,128)(2,1)} %bitcast.49, bf16[1024,512]{1,0:T(8,128)(2,1)} %bitcast.52, f32[16,512]{1,0:T(8,128)} %bitcast.63, bf16[512,128]{1,0:T(8,128)(2,1)} %bitcast.58, ...), custom_call_target="tpu_custom_call" | custom-call | flops 3000000000 | bytes 2000000 | tf_op jit(solution)/shard_map/prompt_far/pallas_call | solution.py:544
  101.8 3.7 %all-to-all-done.3.parts_ref = f32[16,64,128]{2,1,0:T(8,128)S(1)} async-done(((f32[16,64,128]{2,1,0:T(8,128)}), f32[16,64,128]{2,1,0:T(8,128)S(1)}, u32[]{:S(2)}, u32[]{:S(2)}) %all-to-all-start.3) | async-done | bytes 524320 | tf_op jit(solution)/shard_map/all_to_all | solution.py:585
  105.5 0.7 gather_groups.1
  (19 shorter events, 0.0 us)
Async XLA Ops:
  6.8 2.3 %collective-permute-start = (f32[17,64,128]{2,1,0:T(8,128)}, f32[17,64,128]{2,1,0:T(8,128)S(1)}, u32[]{:S(2)}, u32[]{:S(2)}) collective-permute-start(f32[17,64,128]{2,1,0:T(8,128)} %get-tuple-element.62), channel_id=1, source_target_pairs={{0,8},{8,0},{16,24},{24,16},{32,40},{40,32},{48,56},{56,48},{64,72... | collective-permute-start | bytes 1671176 | tf_op jit(solution)/shard_map/ppermute | solution.py:579
  9.1 1.0 copy-start
  10.1 0.7 copy-start.4
  11.5 9.1 %collective-permute-start.1 = (f32[9,64,128]{2,1,0:T(8,128)S(1)}, f32[9,64,128]{2,1,0:T(8,128)S(1)}, u32[]{:S(2)}, u32[]{:S(2)}) collective-permute-start(f32[9,64,128]{2,1,0:T(8,128)S(1)} %get-tuple-element.65), channel_id=1, source_target_pairs={{0,16},{8,24},{16,0},{24,8},{32,48},{40,56},{48,32},{56,40},{64,80... | collective-permute-start | bytes 884744 | tf_op jit(solution)/shard_map/ppermute | solution.py:582
  20.6 0.9 copy-start.3
  22.9 23.5 %all-to-all-start = ((f32[8,104,128]{2,1,0:T(8,128)}), f32[8,104,128]{2,1,0:T(8,128)S(1)}, u32[]{:S(2)}, u32[]{:S(2)}) async-start(f32[8,104,128]{2,1,0:T(8,128)} %pack.1), calls=%async_computation | async-start | bytes 851968 | tf_op jit(solution)/shard_map/all_to_all | solution.py:585
  47.2 13.4 %all-to-all-start.1 = ((f32[8,64,128]{2,1,0:T(8,128)}), f32[8,64,128]{2,1,0:T(8,128)S(1)}, u32[]{:S(2)}, u32[]{:S(2)}) async-start(f32[8,64,128]{2,1,0:T(8,128)} %get-tuple-element.79), calls=%async_computation.1 | async-start | bytes 524288 | tf_op jit(solution)/shard_map/all_to_all | solution.py:585
  54.4 10.5 %copy-start.2 = (bf16[1,1024,4,64]{1,3,2,0:T(8,128)(2,1)S(1)}, bf16[1,1024,4,64]{1,3,2,0:T(8,128)(2,1)}, u32[]{:S(2)}) copy-start(bf16[1,1024,4,64]{1,3,2,0:T(8,128)(2,1)} %param.20) | copy-start | bytes 1572868
  54.4 10.5 %copy-start.6 = (f32[1,1024,4]{1,2,0:T(4,128)S(1)}, f32[1,1024,4]{1,2,0:T(4,128)}, u32[]{:S(2)}) copy-start(f32[1,1024,4]{1,2,0:T(4,128)} %param.19) | copy-start | bytes 49156
  61.4 15.8 %all-to-all-start.2 = ((f32[8,96,128]{2,1,0:T(8,128)}), f32[8,96,128]{2,1,0:T(8,128)S(1)}, u32[]{:S(2)}, u32[]{:S(2)}) async-start(f32[8,96,128]{2,1,0:T(8,128)} %scan_back.1), calls=%async_computation.2 | async-start | bytes 786432 | tf_op jit(solution)/shard_map/all_to_all | solution.py:585
  64.8 16.7 %collective-permute-start.2 = (f32[16,32,128]{2,1,0:T(8,128)}, f32[16,32,128]{2,1,0:T(8,128)}, u32[]{:S(2)}, u32[]{:S(2)}) collective-permute-start(f32[16,32,128]{2,1,0:T(8,128)} %get-tuple-element.77), channel_id=1, source_target_pairs={{0,8},{8,0},{16,24},{24,16},{32,40},{40,32},{48,56},{56,48},{64,72... | collective-permute-start | bytes 786440 | tf_op jit(solution)/shard_map/ppermute | solution.py:579
  64.9 1.0 copy-start.12
  66.6 0.8 copy-start.8
  67.4 0.8 copy-start.10
  68.2 13.3 %copy-start.13 = (f32[16,32,128]{2,1,0:T(8,128)S(1)}, f32[16,32,128]{2,1,0:T(8,128)}, u32[]{:S(2)}) copy-start(f32[16,32,128]{2,1,0:T(8,128)} %get-tuple-element.76) | copy-start | bytes 786436
  77.8 1.0 copy-start.9
  78.9 1.0 copy-start.11
  80.3 8.9 %copy-start.1 = (f32[16,64,128]{2,1,0:T(8,128)S(1)}, f32[16,64,128]{2,1,0:T(8,128)}, u32[]{:S(2)}) copy-start(f32[16,64,128]{2,1,0:T(8,128)} %get-tuple-element.61.mine_ref) | copy-start | bytes 1572868
  80.4 8.8 %copy-start.5 = (f32[16,128]{1,0:T(8,128)S(1)}, f32[16,128]{1,0:T(8,128)}, u32[]{:S(2)}) copy-start(f32[16,128]{1,0:T(8,128)} %get-tuple-element.63.total_ref) | copy-start | bytes 24580
  80.4 2.2 %collective-permute-start.3 = (f32[16,32,128]{2,1,0:T(8,128)S(1)}, f32[16,32,128]{2,1,0:T(8,128)S(1)}, u32[]{:S(2)}, u32[]{:S(2)}) collective-permute-start(f32[16,32,128]{2,1,0:T(8,128)S(1)} %get-tuple-element.96), channel_id=1, source_target_pairs={{0,8},{8,0},{16,24},{24,16},{32,40},{40,32},{48,56},{56,48},{64,72... | collective-permute-start | bytes 786440 | tf_op jit(solution)/shard_map/ppermute | solution.py:579
  80.5 8.7 %collective-permute-start.4 = (f32[8,64,128]{2,1,0:T(8,128)S(1)}, f32[8,64,128]{2,1,0:T(8,128)S(1)}, u32[]{:S(2)}, u32[]{:S(2)}) collective-permute-start(f32[8,64,128]{2,1,0:T(8,128)S(1)} %get-tuple-element.103), channel_id=1, source_target_pairs={{0,16},{8,24},{16,0},{24,8},{32,48},{40,56},{48,32},{56,40},{64,80... | collective-permute-start | bytes 786440 | tf_op jit(solution)/shard_map/ppermute | solution.py:582
  83.5 22.1 %all-to-all-start.3 = ((f32[16,64,128]{2,1,0:T(8,128)}), f32[16,64,128]{2,1,0:T(8,128)S(1)}, u32[]{:S(2)}, u32[]{:S(2)}) async-start(f32[16,64,128]{2,1,0:T(8,128)} %pack_tail.1), calls=%async_computation.3 | async-start | bytes 1048576 | tf_op jit(solution)/shard_map/all_to_all | solution.py:585
  89.9 0.8 copy-start.7
  90.7 1.9 %collective-permute-start.5 = (f32[16,64,128]{2,1,0:T(8,128)S(1)}, f32[16,64,128]{2,1,0:T(8,128)S(1)}, u32[]{:S(2)}, u32[]{:S(2)}) collective-permute-start(f32[16,64,128]{2,1,0:T(8,128)S(1)} %get-tuple-element.105), channel_id=1, source_target_pairs={{0,8},{8,0},{16,24},{24,16},{32,40},{40,32},{48,56},{56,48},{64,72... | collective-permute-start | bytes 1572872 | tf_op jit(solution)/shard_map/ppermute | solution.py:579
  92.6 0.8 copy-start.14

commit v5 on v4

--- a/solution.py
+++ b/solution.py
@@ -191,6 +191,11 @@
     peer_ref[places, :heads] = total_ref[...]
     peer_ref[places, heads:] = jnp.zeros_like(peer_ref[places, heads:])
     wait_all(sent)
+
+
+def hold_kernel(mine_ref, total_ref, mine_out_ref, total_out_ref):
+    mine_out_ref[...] = mine_ref[...]
+    total_out_ref[...] = total_ref[...]
 
 
 def both_totals(first, head, mine_ref, got_ref):
@@ -606,6 +611,9 @@
         copies=5 + 2 * chunks, scalars=1, far=5, far_outs=2, flops=10**9, name="prompt_summary",
     )(core, x, cot, logs, keys, queries)
     theirs = swap_cores(peer)
+    held_mine, held_totals = call(
+        hold_kernel, [shape(chips, 2 * PART, N), shape(heads, N)], count=2, flops=10**7, name="hold"
+    )(mine, totals)
 
     answer_lanes, answer_rows = held(answer_width, length, dtype=BF16), held(length, N, dtype=BF16)
     answer_logs, answer_states = held(answer_heads, length), held(answer_chunks, answer_width, N)
@@ -623,7 +631,7 @@
     half_more = shape(planes + 1, 2 * PART, N)
     keep, away, chip_totals = call(
         pack_chip_kernel, [half, half_more, shape(heads, N)], scalars=1, count=3, flops=10**7, name="pack_chip"
-    )(at, mine, theirs, totals)
+    )(at, held_mine, theirs, held_totals)
     chip_theirs = swap_chips(away)
     (sent,) = call(
         pack_kernel, [shape(planes, GRADS + PART, N)], scalars=1, count=4, flops=10**7, name="pack"
@@ -656,7 +664,9 @@
     )
     finals = over(sent, "comp")
     key_parts = key_mine + swap_cores(key_peer)
-    finals, near_input, near_key, near_query = lax.optimization_barrier((finals, near_input, near_key, near_query))
+    finals, near_input, near_key, near_query, key_parts = lax.optimization_barrier(
+        (finals, near_input, near_key, near_query, key_parts)
+    )
     (sent,) = call(
         scan_back_kernel, [shape(planes, 3 * PART, N)], count=3, flops=10**7, name="scan_back"
     )(blocks, starts, finals)
@@ -667,16 +677,16 @@
         [shape(length, answer_width, dtype=BF16), shape(length, answer_width, dtype=BF16), shape(length, N)],
         scalars=1, count=3, flops=10**9, name="answer_prepare",
     )(answer_lengths, late_cot, late_logs, aq_local)
-    chip_own, chip_other = call(
-        unpack_kernel, [half, half], scalars=1, count=4, flops=10**7, name="unpack"
-    )(at, keep, chip_theirs, chip_totals, states)
-    states, chip_own, chip_other = lax.optimization_barrier((states, chip_own, chip_other))
-    chip_got = swap_chips(chip_other)
-
     query_mine, query_peer = call(
         start_part_kernel, [shape(chips, PART, N), shape(chips, PART, N)],
         scalars=1, count=4, flops=10**9, name="answer_start_part",
     )(core, late_high, late_low, aq_local, states)
+    states, query_mine, query_peer = lax.optimization_barrier((states, query_mine, query_peer))
+    chip_own, chip_other = call(
+        unpack_kernel, [half, half], scalars=1, count=4, flops=10**7, name="unpack"
+    )(at, keep, chip_theirs, chip_totals, states)
+    chip_got = swap_chips(chip_other)
+
     (sent,) = call(tail_kernel, [shape(chips, 2 * PART, N)], count=3, flops=10**7, name="pack_tail")(
         key_parts, query_mine, swap_cores(query_peer)
     )

time: 107 us -> 107 us (level)
  waiting for transfers between devices: 24.8 us -> 26 us
    ppermute x4, waiting for transfers between devices: 3.96 us -> 2.18 us  [swap_cores(): return lax.ppermute(value, 'seq', [(i, i ^ 1) for i in range(seq)])]
    all_to_all x4, waiting for transfers between devices: 18.3 us -> 20 us  [over(): lax.all_to_all(value, axis, 0, 0, axis_index_groups=groups, tiled=True)]
    ppermute x2, waiting for transfers between devices: 2.54 us -> 3.8 us  [swap_chips(): return lax.ppermute(value, 'seq', [(i, i ^ 2) for i in range(seq)])]
    pallas_call x15 -> x16, Pallas kernels: 44.3 us -> 44.3 us  [run(): pl.pallas_call(inner, out_shape=outs, in_specs=[pl.BlockSpec(memory_space...]
  transfers between devices with their start and end apart: 10 -> 10, of which waited for: 8 -> 8; matrix products, arithmetic and copies ran while one was open for 1% -> 0% of each run, Pallas kernels for 32% -> 31%
where the time goes in v5:
time: 107 us
  Pallas kernels  44.3 us (41%)
  waiting for transfers between devices  26 us (24%)
  starting transfers between devices  25.6 us (24%)
  local copies, waits for them, and re-layouts  8.99 us (8%)
  between operations  1.55 us (1%)
    pallas_call x16, Pallas kernels, run(): pl.pallas_call(inner, out_shape=outs, in_specs=[pl.BlockSpec(memory_space...  44.3 us
    all_to_all x4, starting transfers between devices, over(): lax.all_to_all(value, axis, 0, 0, axis_index_groups=groups, tiled=True)  22.7 us
    all_to_all x4, waiting for transfers between devices, over(): lax.all_to_all(value, axis, 0, 0, axis_index_groups=groups, tiled=True)  20 us
    unnamed x30, local copies, waits for them, and re-layouts  8.99 us
    ppermute x2, waiting for transfers between devices, swap_chips(): return lax.ppermute(value, 'seq', [(i, i ^ 2) for i in range(seq)])  3.8 us
    ppermute x2, starting transfers between devices, swap_chips(): return lax.ppermute(value, 'seq', [(i, i ^ 2) for i in range(seq)])  2.6 us
    ppermute x4, waiting for transfers between devices, swap_cores(): return lax.ppermute(value, 'seq', [(i, i ^ 1) for i in range(seq)])  2.18 us
  transfers between devices with their start and end apart: 10, of which 8 were waited for; matrix products, arithmetic and copies ran while one was open for 0% of the time, Pallas kernels for 31%

profile of v5, /device:TPU:16, one launch (start us, length us, event | category | flops | bytes accessed | tf_op | source)
XLA Modules:
  0.0 106.5 jit_solution(5382751492888181317)
XLA Ops:
  0.6 6.2 %prompt_summary.1 = (f32[4,1024,128]{2,1,0:T(8,128)}, f32[4,1024,128]{2,1,0:T(8,128)}, f32[16,64,128]{2,1,0:T(8,128)}, f32[17,64,128]{2,1,0:T(8,128)}, f32[16,128]{1,0:T(8,128)}) custom-call(s32[1]{0:T(128)} %bitcast.core_ref, bf16[1024,512]{1,0:T(8,128)(2,1)} %bitcast.47, bf16[1024,512]{1,0:T(8,128)(2,1)} %bitcast.50, f32[16,512]{1,0:T(8,128)} %bitcast.61, ...), custom_call_target="tpu_custom_call" | custom-call | flops 1000000000 | bytes 2000000 | tf_op jit(solution)/shard_map/prompt_summary/pallas_call | solution.py:549
  6.8 0.1 collective-permute-start
  7.0 1.0 copy-done
  8.0 0.7 copy-done.4
  8.7 0.1 pad_add_fusion.at_ref
  8.8 0.3 collective-permute-done.got_ref
  9.1 0.6 pack_chip.1
  9.7 1.4 %collective-permute-start.1 = (f32[9,64,128]{2,1,0:T(8,128)S(1)}, f32[9,64,128]{2,1,0:T(8,128)S(1)}, u32[]{:S(2)}, u32[]{:S(2)}) collective-permute-start(f32[9,64,128]{2,1,0:T(8,128)S(1)} %get-tuple-element.70), channel_id=1, source_target_pairs={{0,16},{8,24},{16,0},{24,8},{32,48},{40,56},{48,32},{56,40},{64,80... | collective-permute-start | bytes 884744 | tf_op jit(solution)/shard_map/ppermute | solution.py:587
  11.8 6.8 %answer_ends.1 = (f32[8,256,128]{2,1,0:T(8,128)}, bf16[1024,128]{1,0:T(8,128)(2,1)}, bf16[1024,128]{1,0:T(8,128)(2,1)}, f32[256,128]{1,0:T(8,128)}) custom-call(s32[1]{0:T(128)S(6)} %copy.17.length_ref, s32[1]{0:T(128)} %bitcast.9.group_ref, bf16[256,1024]{1,0:T(8,128)(2,1)} %bitcast.39, f32[4,1024]{1,0:T(4,128)} %bitcast.42, bf16[8192,128]{1,0:T(8,128)(2,1)} %bitcast.45, ...), custom_call_target="tpu_custom_call" | custom-call | flops 1000000000 | bytes 2000000 | tf_op jit(solution)/shard_map/answer_ends/pallas_call | solution.py:549
  18.5 0.4 collective-permute-done.1.got_ref
  18.9 0.9 copy-done.3
  19.8 1.4 %pack.1 = f32[8,104,128]{2,1,0:T(8,128)} custom-call(s32[2]{0:T(128)S(1)} %pad_add_fusion.at_ref, f32[8,64,128]{2,1,0:T(8,128)S(1)} %get-tuple-element.69.keep_ref, f32[9,64,128]{2,1,0:T(8,128)S(1)} %collective-permute-done.1.got_ref, f32[16,128]{1,0:T(8,128)S(1)} %get-tuple-element.71.total_ref, f32[256,128]{1,0:T(8,128)S(1)} %copy-done.3), custom_call_target="tpu_custom_call" | custom-call | flops 10000000 | bytes 2000000 | tf_op jit(solution)/shard_map/pack/pallas_call | solution.py:549
  21.2 8.5 %all-to-all-start = ((f32[8,104,128]{2,1,0:T(8,128)}), f32[8,104,128]{2,1,0:T(8,128)S(1)}, u32[]{:S(2)}, u32[]{:S(2)}) async-start(f32[8,104,128]{2,1,0:T(8,128)} %pack.1), calls=%async_computation | async-start | bytes 851968 | tf_op jit(solution)/shard_map/all_to_all | solution.py:590
  29.7 9.8 %answer_grads.1 = (bf16[256,1024]{1,0:T(8,128)(2,1)}, f32[1024,128]{1,0:T(8,128)}, f32[16,32,128]{2,1,0:T(8,128)}, f32[16,32,128]{2,1,0:T(8,128)}) custom-call(s32[1]{0:T(128)S(6)} %copy.17.length_ref, s32[1]{0:T(128)} %bitcast.core_ref, bf16[256,1024]{1,0:T(8,128)(2,1)} %bitcast.53, bf16[256,1024]{1,0:T(8,128)(2,1)} %bitcast.40, f32[4,1024]{1,0:T(4,128)} %bitcast.43, ...), custom_call_target="tpu_custom_call" | custom-call | flops 3000000000 | bytes 2000000 | tf_op jit(solution)/shard_map/answer_grads/pallas_call | solution.py:549
  39.5 5.3 %all-to-all-done.blocks_ref = f32[8,104,128]{2,1,0:T(8,128)S(1)} async-done(((f32[8,104,128]{2,1,0:T(8,128)}), f32[8,104,128]{2,1,0:T(8,128)S(1)}, u32[]{:S(2)}, u32[]{:S(2)}) %all-to-all-start) | async-done | bytes 426016 | tf_op jit(solution)/shard_map/all_to_all | solution.py:590
  44.8 0.7 scan.1
  45.5 7.3 %all-to-all-start.1 = ((f32[8,64,128]{2,1,0:T(8,128)}), f32[8,64,128]{2,1,0:T(8,128)S(1)}, u32[]{:S(2)}, u32[]{:S(2)}) async-start(f32[8,64,128]{2,1,0:T(8,128)} %get-tuple-element.81), calls=%async_computation.1 | async-start | bytes 524288 | tf_op jit(solution)/shard_map/all_to_all | solution.py:590
  52.8 0.0 collective-permute-start.2
  52.8 5.7 %prompt_near.1 = (f32[4,1024,128]{2,1,0:T(8,128)}, f32[512,128]{1,0:T(8,128)}, f32[512,128]{1,0:T(8,128)}) custom-call(bf16[1024,512]{1,0:T(8,128)(2,1)} %bitcast.48, bf16[1024,512]{1,0:T(8,128)(2,1)} %bitcast.51, f32[16,512]{1,0:T(8,128)} %bitcast.62, bf16[512,128]{1,0:T(8,128)(2,1)} %bitcast.57, bf16[512,128]{1,0:T(8,128)(2,1)} %bitcast.55), custom_call_target="tpu_custom_call" | custom-call | flops 3000000000 | bytes 2000000 | tf_op jit(solution)/shard_map/prompt_near/pallas_call | solution.py:549
  58.5 0.0 copy-start.2
  58.5 0.0 copy-start.6
  58.5 0.0 collective-permute-done.2
  58.6 0.3 all-to-all-done.1.got_ref
  58.9 0.8 scan_back.1
  59.7 3.5 %all-to-all-start.2 = ((f32[8,96,128]{2,1,0:T(8,128)}), f32[8,96,128]{2,1,0:T(8,128)S(1)}, u32[]{:S(2)}, u32[]{:S(2)}) async-start(f32[8,96,128]{2,1,0:T(8,128)} %scan_back.1), calls=%async_computation.2 | async-start | bytes 786432 | tf_op jit(solution)/shard_map/all_to_all | solution.py:590
  63.2 1.0 copy-done.12
  64.2 0.6 answer_prepare.1
  64.8 0.0 copy-start.8
  64.8 0.8 copy-done.8
  65.6 0.8 copy-done.10
  66.4 11.9 %all-to-all-done.2.state_ref.states_ref = f32[8,96,128]{2,1,0:T(8,128)S(1)} async-done(((f32[8,96,128]{2,1,0:T(8,128)}), f32[8,96,128]{2,1,0:T(8,128)S(1)}, u32[]{:S(2)}, u32[]{:S(2)}) %all-to-all-start.2) | async-done | bytes 393248 | tf_op jit(solution)/shard_map/all_to_all | solution.py:590
  78.3 1.0 copy-done.9
  79.4 1.0 copy-done.11
  80.4 0.4 answer_start_part.1
  80.9 0.0 copy-start.5
  80.9 0.1 collective-permute-start.3
  81.0 0.6 unpack.1
  81.6 1.2 %collective-permute-start.4 = (f32[8,64,128]{2,1,0:T(8,128)S(1)}, f32[8,64,128]{2,1,0:T(8,128)S(1)}, u32[]{:S(2)}, u32[]{:S(2)}) collective-permute-start(f32[8,64,128]{2,1,0:T(8,128)S(1)} %get-tuple-element.109), channel_id=1, source_target_pairs={{0,16},{8,24},{16,0},{24,8},{32,48},{40,56},{48,32},{56,40},{64,80... | collective-permute-start | bytes 786440 | tf_op jit(solution)/shard_map/ppermute | solution.py:587
  82.9 0.8 pack_tail.1
  83.7 3.6 %all-to-all-start.3 = ((f32[16,64,128]{2,1,0:T(8,128)}), f32[16,64,128]{2,1,0:T(8,128)S(1)}, u32[]{:S(2)}, u32[]{:S(2)}) async-start(f32[16,64,128]{2,1,0:T(8,128)} %pack_tail.1), calls=%async_computation.3 | async-start | bytes 1048576 | tf_op jit(solution)/shard_map/all_to_all | solution.py:590
  87.3 3.4 %collective-permute-done.4.away_ref = f32[8,64,128]{2,1,0:T(8,128)S(1)} collective-permute-done((f32[8,64,128]{2,1,0:T(8,128)S(1)}, f32[8,64,128]{2,1,0:T(8,128)S(1)}, u32[]{:S(2)}, u32[]{:S(2)}) %collective-permute-start.4) | collective-permute-done | bytes 262176 | tf_op jit(solution)/shard_map/ppermute | solution.py:587
  90.7 0.7 unpack_chip.1
  91.4 0.8 copy-done.7
  92.2 1.9 %collective-permute-done.5.got_hbm = f32[16,64,128]{2,1,0:T(8,128)S(1)} collective-permute-done((f32[16,64,128]{2,1,0:T(8,128)S(1)}, f32[16,64,128]{2,1,0:T(8,128)S(1)}, u32[]{:S(2)}, u32[]{:S(2)}) %collective-permute-start.5) | collective-permute-done | bytes 524320 | tf_op jit(solution)/shard_map/ppermute | solution.py:584
  94.1 0.8 copy-done.14
  94.9 8.4 %prompt_far.1 = (bf16[1024,512]{1,0:T(8,128)(2,1)}, bf16[512,128]{1,0:T(8,128)(2,1)}, bf16[512,128]{1,0:T(8,128)(2,1)}) custom-call(s32[1]{0:T(128)} %bitcast.core_ref, bf16[1024,512]{1,0:T(8,128)(2,1)} %bitcast.49, bf16[1024,512]{1,0:T(8,128)(2,1)} %bitcast.52, f32[16,512]{1,0:T(8,128)} %bitcast.63, bf16[512,128]{1,0:T(8,128)(2,1)} %bitcast.58, ...), custom_call_target="tpu_custom_call" | custom-call | flops 3000000000 | bytes 2000000 | tf_op jit(solution)/shard_map/prompt_far/pallas_call | solution.py:549
  103.3 2.5 %all-to-all-done.3.parts_ref = f32[16,64,128]{2,1,0:T(8,128)S(1)} async-done(((f32[16,64,128]{2,1,0:T(8,128)}), f32[16,64,128]{2,1,0:T(8,128)S(1)}, u32[]{:S(2)}, u32[]{:S(2)}) %all-to-all-start.3) | async-done | bytes 524320 | tf_op jit(solution)/shard_map/all_to_all | solution.py:590
  105.8 0.7 gather_groups.1
  (20 shorter events, 0.1 us)
Async XLA Ops:
  6.8 2.3 %collective-permute-start = (f32[17,64,128]{2,1,0:T(8,128)}, f32[17,64,128]{2,1,0:T(8,128)S(1)}, u32[]{:S(2)}, u32[]{:S(2)}) collective-permute-start(f32[17,64,128]{2,1,0:T(8,128)} %get-tuple-element.67), channel_id=1, source_target_pairs={{0,8},{8,0},{16,24},{24,16},{32,40},{40,32},{48,56},{56,48},{64,72... | collective-permute-start | bytes 1671176 | tf_op jit(solution)/shard_map/ppermute | solution.py:584
  7.0 1.0 copy-start
  8.0 0.7 copy-start.4
  9.7 9.2 %collective-permute-start.1 = (f32[9,64,128]{2,1,0:T(8,128)S(1)}, f32[9,64,128]{2,1,0:T(8,128)S(1)}, u32[]{:S(2)}, u32[]{:S(2)}) collective-permute-start(f32[9,64,128]{2,1,0:T(8,128)S(1)} %get-tuple-element.70), channel_id=1, source_target_pairs={{0,16},{8,24},{16,0},{24,8},{32,48},{40,56},{48,32},{56,40},{64,80... | collective-permute-start | bytes 884744 | tf_op jit(solution)/shard_map/ppermute | solution.py:587
  18.9 0.9 copy-start.3
  21.2 23.5 %all-to-all-start = ((f32[8,104,128]{2,1,0:T(8,128)}), f32[8,104,128]{2,1,0:T(8,128)S(1)}, u32[]{:S(2)}, u32[]{:S(2)}) async-start(f32[8,104,128]{2,1,0:T(8,128)} %pack.1), calls=%async_computation | async-start | bytes 851968 | tf_op jit(solution)/shard_map/all_to_all | solution.py:590
  45.5 13.4 %all-to-all-start.1 = ((f32[8,64,128]{2,1,0:T(8,128)}), f32[8,64,128]{2,1,0:T(8,128)S(1)}, u32[]{:S(2)}, u32[]{:S(2)}) async-start(f32[8,64,128]{2,1,0:T(8,128)} %get-tuple-element.81), calls=%async_computation.1 | async-start | bytes 524288 | tf_op jit(solution)/shard_map/all_to_all | solution.py:590
  52.8 5.7 %copy-start.13 = (f32[16,32,128]{2,1,0:T(8,128)S(1)}, f32[16,32,128]{2,1,0:T(8,128)}, u32[]{:S(2)}) copy-start(f32[16,32,128]{2,1,0:T(8,128)} %get-tuple-element.85) | copy-start | bytes 786436
  52.8 5.7 %collective-permute-start.2 = (f32[16,32,128]{2,1,0:T(8,128)}, f32[16,32,128]{2,1,0:T(8,128)S(1)}, u32[]{:S(2)}, u32[]{:S(2)}) collective-permute-start(f32[16,32,128]{2,1,0:T(8,128)} %get-tuple-element.86), channel_id=1, source_target_pairs={{0,8},{8,0},{16,24},{24,16},{32,40},{40,32},{48,56},{56,48},{64,72... | collective-permute-start | bytes 786440 | tf_op jit(solution)/shard_map/ppermute | solution.py:584
  58.5 4.7 %copy-start.2 = (bf16[1,1024,4,64]{1,3,2,0:T(8,128)(2,1)S(1)}, bf16[1,1024,4,64]{1,3,2,0:T(8,128)(2,1)}, u32[]{:S(2)}) copy-start(bf16[1,1024,4,64]{1,3,2,0:T(8,128)(2,1)} %param.20) | copy-start | bytes 1572868
  58.5 4.7 %copy-start.6 = (f32[1,1024,4]{1,2,0:T(4,128)S(1)}, f32[1,1024,4]{1,2,0:T(4,128)}, u32[]{:S(2)}) copy-start(f32[1,1024,4]{1,2,0:T(4,128)} %param.19) | copy-start | bytes 49156
  59.7 18.7 %all-to-all-start.2 = ((f32[8,96,128]{2,1,0:T(8,128)}), f32[8,96,128]{2,1,0:T(8,128)S(1)}, u32[]{:S(2)}, u32[]{:S(2)}) async-start(f32[8,96,128]{2,1,0:T(8,128)} %scan_back.1), calls=%async_computation.2 | async-start | bytes 786432 | tf_op jit(solution)/shard_map/all_to_all | solution.py:590
  63.2 1.0 copy-start.12
  64.8 0.8 copy-start.8
  65.6 0.8 copy-start.10
  78.3 1.0 copy-start.9
  79.4 1.0 copy-start.11
  80.9 9.8 %copy-start.1 = (f32[16,64,128]{2,1,0:T(8,128)S(1)}, f32[16,64,128]{2,1,0:T(8,128)}, u32[]{:S(2)}) copy-start(f32[16,64,128]{2,1,0:T(8,128)} %get-tuple-element.64.mine_ref) | copy-start | bytes 1572868
  80.9 9.8 %copy-start.5 = (f32[16,128]{1,0:T(8,128)S(1)}, f32[16,128]{1,0:T(8,128)}, u32[]{:S(2)}) copy-start(f32[16,128]{1,0:T(8,128)} %get-tuple-element.65.total_ref) | copy-start | bytes 24580
  80.9 2.0 %collective-permute-start.3 = (f32[16,32,128]{2,1,0:T(8,128)S(1)}, f32[16,32,128]{2,1,0:T(8,128)S(1)}, u32[]{:S(2)}, u32[]{:S(2)}) collective-permute-start(f32[16,32,128]{2,1,0:T(8,128)S(1)} %get-tuple-element.101), channel_id=1, source_target_pairs={{0,8},{8,0},{16,24},{24,16},{32,40},{40,32},{48,56},{56,48},{64,72... | collective-permute-start | bytes 786440 | tf_op jit(solution)/shard_map/ppermute | solution.py:584
  81.6 9.0 %collective-permute-start.4 = (f32[8,64,128]{2,1,0:T(8,128)S(1)}, f32[8,64,128]{2,1,0:T(8,128)S(1)}, u32[]{:S(2)}, u32[]{:S(2)}) collective-permute-start(f32[8,64,128]{2,1,0:T(8,128)S(1)} %get-tuple-element.109), channel_id=1, source_target_pairs={{0,16},{8,24},{16,0},{24,8},{32,48},{40,56},{48,32},{56,40},{64,80... | collective-permute-start | bytes 786440 | tf_op jit(solution)/shard_map/ppermute | solution.py:587
  83.7 22.1 %all-to-all-start.3 = ((f32[16,64,128]{2,1,0:T(8,128)}), f32[16,64,128]{2,1,0:T(8,128)S(1)}, u32[]{:S(2)}, u32[]{:S(2)}) async-start(f32[16,64,128]{2,1,0:T(8,128)} %pack_tail.1), calls=%async_computation.3 | async-start | bytes 1048576 | tf_op jit(solution)/shard_map/all_to_all | solution.py:590
  91.4 0.8 copy-start.7
  92.2 1.9 %collective-permute-start.5 = (f32[16,64,128]{2,1,0:T(8,128)S(1)}, f32[16,64,128]{2,1,0:T(8,128)S(1)}, u32[]{:S(2)}, u32[]{:S(2)}) collective-permute-start(f32[16,64,128]{2,1,0:T(8,128)S(1)} %get-tuple-element.111), channel_id=1, source_target_pairs={{0,8},{8,0},{16,24},{24,16},{32,40},{40,32},{48,56},{56,48},{64,72... | collective-permute-start | bytes 1572872 | tf_op jit(solution)/shard_map/ppermute | solution.py:584
  94.1 0.8 copy-start.14
